TPU v7x, 128 devices: a whole 4x4x4 slice. The times are simulated.
128 devices in a mesh: dp: 16 (over z_hi, x, core), tensor: 8 (over z_lo, y).
Axes of the slice: x: 4, y: 4, z: 4 (z_hi: 2, z_lo: 2; z = z_hi * 2 + z_lo), core: 2. Of those that a mesh axis runs over, the one named last changes fastest.
Arguments:
- tokens: bfloat16 [16384, 2048], P('dp'), may hold values from -6 to 6
- cotangent: bfloat16 [16384, 2048], P('dp'), may hold values from -6 to 6
- seq_lengths: int32 [16, 8], P('dp'), may hold values from 0 to 1024, as said below
- ln_gain: bfloat16 [2048], replicated, may hold values from 0.5 to 1.5
- ln_bias: bfloat16 [2048], replicated, may hold values from -1.75 to 1.75
- w_qkv: bfloat16 [2048, 6144], P(None, 'tensor'), may hold values from -0.125 to 0.125
- b_qkv: bfloat16 [6144], P('tensor'), may hold values from -3 to 3
- w_dense: bfloat16 [2048, 2048], P('tensor'), may hold values from -0.5 to 0.5
- b_dense: bfloat16 [2048], replicated, may hold values from -1.75 to 1.75
- w_fc1: bfloat16 [2048, 8192], P(None, 'tensor'), may hold values from -0.125 to 0.125
- b_fc1: bfloat16 [8192], P('tensor'), may hold values from -3 to 3
- w_fc2: bfloat16 [8192, 2048], P('tensor'), may hold values from -0.0625 to 0.0625
- b_fc2: bfloat16 [2048], replicated, may hold values from -1.75 to 1.75
Outputs:
- output: bfloat16 [16384, 2048], P('dp')
- grad_tokens: bfloat16 [16384, 2048], P('dp')
- grad_ln_gain: float32 [2048], P('dp')
- grad_ln_bias: float32 [2048], P('dp')
- grad_w_qkv: float32 [2048, 6144], P('dp', 'tensor')
- grad_b_qkv: float32 [6144], P(('tensor', 'dp'))
- grad_w_dense: float32 [2048, 2048], P('tensor', 'dp')
- grad_b_dense: float32 [2048], P('dp')
- grad_w_fc1: float32 [2048, 8192], P('dp', 'tensor')
- grad_b_fc1: float32 [8192], P(('tensor', 'dp'))
- grad_w_fc2: float32 [8192, 2048], P('tensor', 'dp')
- grad_b_fc2: float32 [2048], P('dp')
Inputs may be any that keep to these rules, and one draw needn't show every extreme that they name: `seq_lengths`: row r lists the lengths of the sequences packed in order from the start of slot r of 1024 positions; the rest of the slot is padding and zero entries are unused places. In every draw one row is a single sequence of exactly 1024.
All inputs are finite; a program needn't handle non-finite values.
Results may differ from a plain program's by a relative error of at most 0.014.
Values may be sent and summed in bfloat16 or wider, within the bound.
No kernel may reach another device: no remote copies, remote signals or barrier semaphores. Data moves between devices by JAX's collectives and lax.ppermute only.
A program may use at most 192 MiB of HBM per device.

v0:
```python
import functools

import jax
import jax.numpy as jnp
from jax import lax
from jax.experimental import pallas as pl
from jax.experimental.pallas import tpu as pltpu
from jax.sharding import Mesh
from jax.sharding import PartitionSpec as P

HEAD_DIM = 64
ROTARY = 32
DP = ("zh", "x", "core")
TENSOR = ("zl", "y")
BF16 = jnp.bfloat16
F32 = jnp.float32
ROWS = 256
QUERIES = 512
BLOCK = 128
AT_ONCE = 4
VMEM_BYTES = 56 * 2**20
GELU = 0.7978845608


def dot(left, right, left_dim, right_dim):
    return lax.dot_general(
        left, right, (((left_dim,), (right_dim,)), ((), ())), preferred_element_type=F32
    )


def kernel_call(kernel, name, out_shape, prefetch=0, vmem=VMEM_BYTES, flops=1, **spec):
    if prefetch:
        spec = {
            "grid_spec": pltpu.PrefetchScalarGridSpec(
                num_scalar_prefetch=prefetch,
                grid=spec.pop("grid"),
                in_specs=spec.pop("in_specs"),
                out_specs=spec.pop("out_specs"),
                scratch_shapes=spec.pop("scratch_shapes", ()),
            ),
            **spec,
        }
    return pl.pallas_call(
        kernel,
        out_shape=out_shape,
        compiler_params=pltpu.CompilerParams(vmem_limit_bytes=vmem),
        cost_estimate=pl.CostEstimate(flops=flops, bytes_accessed=1, transcendentals=0),
        name=name,
        **spec,
    )


def made(rows, columns, kind=BF16):
    return jax.ShapeDtypeStruct((rows, columns), kind)


def kept(array):
    return pl.BlockSpec(array.shape, lambda *_: (0,) * array.ndim)


AWAY = pl.BlockSpec(memory_space=pltpu.HBM)
NEAR = pl.BlockSpec(memory_space=pltpu.VMEM)
SCALARS = pl.BlockSpec(memory_space=pltpu.SMEM)


def ends_of(lengths_ref):
    ends = [lengths_ref[0, 0]]
    for place in range(1, lengths_ref.shape[1]):
        ends.append(ends[-1] + lengths_ref[0, place])
    return ends


def starts_at(ends, places):
    start = jnp.zeros_like(places)
    for end in ends:
        start = jnp.maximum(start, jnp.where(places >= end, end, 0))
    return start


def turned_halves(columns):
    lane = lax.broadcasted_iota(jnp.int32, columns.shape, 1)
    return jnp.where(
        lane % ROTARY < ROTARY // 2, pltpu.roll(columns, 112, 1), pltpu.roll(columns, 16, 1)
    )


def span(part, size, first=0):
    at = part * size + first
    return pl.ds(at if isinstance(at, int) else pl.multiple_of(at, BLOCK if size % BLOCK == 0 else size), size)


class Copies:
    def __init__(self, sems):
        self.sems, self.made = sems, {}

    def start(self, name, source, target):
        copy = pltpu.make_async_copy(source, target, self.sems.at[len(self.made)])
        self.made[name] = copy
        copy.start()

    def numbered(self, names, count):
        first = len(self.made)
        for at in range(len(names) * count):
            self.made[("kept", first + at)] = None
        return {name: first + at * count for at, name in enumerate(names)}

    def at(self, source, target, number):
        return pltpu.make_async_copy(source, target, self.sems.at[number])

    def wait(self, *names):
        for name in names:
            self.made[name].wait()


OFFSETS = tuple((planes, places) for planes in range(2) for places in range(4))
FAR = (1, 2)
CUTS = (0, 48, 96, 128)
PARTS = tuple(zip(CUTS, CUTS[1:]))
BLOCK_NAMES = tuple(o for o in OFFSETS if o != FAR) + (0, 1, 2)


def block_shapes(width):
    return [made(BLOCK, width)] * 7 + [made(high - low, width) for low, high in PARTS]


def block_copy(copies, place_ref_of, which, total, ref, columns, number):
    name = BLOCK_NAMES[which]
    low, high = PARTS[name] if isinstance(name, int) else (0, BLOCK)
    place = place_ref_of[OFFSETS.index(FAR if isinstance(name, int) else name)]
    first = pl.multiple_of(place * BLOCK, BLOCK) + low
    return copies.at(
        total.at[pl.ds(first, high - low), columns], ref.at[:, columns], number
    )


def each_block_copy(copies, places_ref, total, refs, parts, size, first, do):
    for part in parts:
        columns = span(part, size)
        for which, ref in enumerate(refs):
            number = first + part * len(refs) + which
            do(block_copy(copies, places_ref, which, total, ref, columns, number))


def start(copy):
    copy.start()


def wait(copy):
    copy.wait()


def forward_kernel(
    lengths_ref,
    freq_ref,
    gain_ref,
    bias_ref,
    b_qkv_ref,
    b_fc1_ref,
    tokens_hbm,
    cot_hbm,
    w_qkv_hbm,
    w_fc1_hbm,
    w_dense_hbm,
    w_fc2_hbm,
    hidden_hbm,
    grad_hbm,
    act_hbm,
    slope_hbm,
    ctx_hbm,
    qkv_grad_hbm,
    stats_hbm,
    branch_hbm,
    tokens,
    grad,
    hidden,
    w_qkv,
    w_fc1,
    w_dense,
    w_fc2,
    qkv,
    act,
    slope,
    ctx_grad,
    ctx,
    qkv_grad,
    cosines,
    sines,
    stats,
    turn_sum,
    value_sum,
    both_ctx,
    both_grad,
    sems,
):
    slot_len, width = tokens.shape
    blocks = slot_len // ROWS
    copies = Copies(sems)
    ends = ends_of(lengths_ref)
    row_copies = {
        "tokens": (tokens_hbm, tokens),
        "cot": (cot_hbm, grad),
        "hidden": (hidden, hidden_hbm),
        "grad": (grad, grad_hbm),
        "act": (act, act_hbm),
        "slope": (slope, slope_hbm),
    }
    numbers = copies.numbered(tuple(row_copies), blocks)
    parts, size = 4, width // 4
    first_branch = copies.numbered(("branch",), parts)["branch"]
    w_fc2_number = copies.numbered(("w_fc2",), 1)["w_fc2"]

    def rows_at(block, part=0, height=ROWS):
        return span(part, height, block * ROWS)

    def row_copy(name, block):
        source, target = row_copies[name]
        at = rows_at(block)
        return copies.at(source.at[at, :], target.at[at, :], numbers[name] + block)

    def normalise(block, part, height):
        at = rows_at(block, part, height)
        places = block * ROWS + part * height
        places = places + lax.broadcasted_iota(jnp.int32, (height, 128), 0)
        lane = lax.broadcasted_iota(jnp.int32, (height, 128), 1)
        position = (places - starts_at(ends, places)).astype(F32)
        angle = position * freq_ref[...]
        cosines[at, :] = jnp.where(lane % HEAD_DIM < ROTARY, jnp.cos(angle), 1.0)
        sine = jnp.sin(angle)
        sines[at, :] = jnp.where(
            lane % HEAD_DIM < ROTARY // 2, -sine, jnp.where(lane % HEAD_DIM < ROTARY, sine, 0.0)
        )
        valid = (places < ends[-1])[:, :1]
        inputs = tokens[at, :].astype(F32)
        mean = jnp.mean(inputs, axis=1, keepdims=True)
        center = inputs - mean
        inv_sigma = lax.rsqrt(jnp.mean(center * center, axis=1, keepdims=True) + 1e-05)
        stats[at, :] = jnp.where(lane == 0, mean, inv_sigma)
        hidden[at, :] = (
            center * inv_sigma * gain_ref[...].astype(F32)[None]
            + bias_ref[...].astype(F32)[None]
        ).astype(BF16)
        grad[at, :] = jnp.where(valid, grad[at, :], jnp.zeros((height, width), BF16))

    def turn(at, projected):
        lane = lax.broadcasted_iota(jnp.int32, (ROWS, 128), 1)
        cosine, sine = cosines[at, :], sines[at, :]
        for block in range(qkv.shape[1] // 128):
            columns = slice(block * 128, block * 128 + 128)
            plain = projected[:, columns]
            turned = plain * cosine + turned_halves(plain) * sine
            if block % 3 == 1:
                turned = jnp.where(lane < HEAD_DIM, plain, turned)
            if block % 3 == 2:
                turned = jnp.where(lane < HEAD_DIM, turned, plain)
            qkv[at, columns] = turned.astype(BF16)

    def activate(at, up, columns):
        square = up * up
        share = 0.5 * jnp.tanh(up * (GELU + (GELU * 0.044715) * square)) + 0.5
        active = up * share
        act[at, columns] = active.astype(BF16)
        slope[at, columns] = (
            share + active * (1.0 - share) * (2 * GELU + (6 * GELU * 0.044715) * square)
        ).astype(BF16)

    def attend(pair, head):
        heads = pl.ds(pl.multiple_of(pair * 6 * HEAD_DIM, 6 * HEAD_DIM), 6 * HEAD_DIM)
        wide = pl.ds(pl.multiple_of(pair * 2 * HEAD_DIM, 2 * HEAD_DIM), 2 * HEAD_DIM)
        at = 3 * HEAD_DIM * head
        mine = slice(HEAD_DIM * head, HEAD_DIM * head + HEAD_DIM)
        all_heads = qkv[:, heads]
        for block in reversed(range(slot_len // QUERIES)):
            rows = slice(block * QUERIES, block * QUERIES + QUERIES)
            reach = (block + 1) * QUERIES
            query = all_heads[rows, at : at + 64] * BF16(HEAD_DIM**-0.5)
            key = all_heads[0:reach, at + 64 : at + 128]
            value = all_heads[0:reach, at + 128 : at + 192]
            upstream = ctx_grad[rows, wide][:, mine]
            scores = dot(key, query, 1, 1)
            place = block * QUERIES + lax.broadcasted_iota(jnp.int32, (1, QUERIES), 1)
            begin = starts_at(ends, place)
            key_place = lax.broadcasted_iota(jnp.int32, (reach, QUERIES), 0)
            scores = jnp.where((key_place >= begin) & (key_place <= place), scores, -1e30)
            raised = jnp.exp(scores - jnp.max(scores, axis=0, keepdims=True))
            prob = raised * (1.0 / jnp.sum(raised, axis=0, keepdims=True))
            prob_low = prob.astype(BF16)
            context = dot(value, prob_low, 0, 0)
            prob_grad = dot(value, upstream, 1, 1)
            row_dot = jnp.sum(prob_grad * prob, axis=0, keepdims=True)
            score_grad = (prob * (prob_grad - row_dot)).astype(BF16)
            query_grad = dot(key, score_grad, 0, 0)
            value_part = dot(prob_low, upstream, 1, 0)
            key_part = dot(score_grad, query, 1, 0)
            if reach == slot_len:
                value_sum[...] = value_part
                turn_sum[:, 64:128] = key_part
            else:
                value_sum[0:reach] += value_part
                turn_sum[0:reach, 64:128] += key_part
            turn_sum[rows, 0:64] = query_grad.T * HEAD_DIM**-0.5
            both_ctx[rows, mine] = context.T.astype(BF16)
        both = turn_sum[...]
        both = both * cosines[...] - turned_halves(both) * sines[...]
        both_grad[:, at : at + 128] = both.astype(BF16)
        both_grad[:, at + 128 : at + 192] = value_sum[...].astype(BF16)
        if head:
            ctx[:, wide] = both_ctx[...]
            qkv_grad[:, heads] = both_grad[...]

    def last_weights():
        return copies.at(w_fc2_hbm, w_fc2, w_fc2_number)

    def branch_copy(part):
        columns = span(part, size)
        return copies.at(
            tokens.at[:, columns], branch_hbm.at[:, columns], first_branch + part
        )

    for name in ("tokens", "cot"):
        row_copy(name, 0).start()
    copies.start("w_qkv", w_qkv_hbm, w_qkv)
    for name in ("tokens", "cot"):
        row_copy(name, 1).start()
    copies.start("w_fc1", w_fc1_hbm, w_fc1)
    copies.start("w_dense", w_dense_hbm, w_dense)

    def one_block(block, ready):
        for name in ("tokens", "cot"):
            row_copy(name, block).wait()
        for part in range(4):
            normalise(block, part, ROWS // 4)
        for name in ("hidden", "grad"):
            row_copy(name, block).start()
        ready("w_qkv")
        at = rows_at(block)
        turn(at, dot(hidden[at, :], w_qkv[...], 1, 0) + b_qkv_ref[...].astype(F32)[None])
        ready("w_fc1", "w_dense")
        half = w_fc1.shape[1] // 2
        for part in range(2):
            columns = slice(part * half, part * half + half)
            up = dot(hidden[at, :], w_fc1[:, columns], 1, 0)
            activate(at, up + b_fc1_ref[columns].astype(F32)[None], columns)
        ctx_grad[at, :] = dot(grad[at, :], w_dense[...], 1, 1).astype(BF16)
        for name in ("act", "slope"):
            row_copy(name, block).start()

    for later in range(2, blocks):
        for name in ("tokens", "cot"):
            row_copy(name, later).start()
    last_weights().start()
    one_block(0, copies.wait)

    @pl.loop(1, blocks)
    def _(block):
        one_block(block, lambda *names: None)

    copies.start("stats", stats, stats_hbm)

    @pl.loop(0, ctx.shape[1] // (2 * HEAD_DIM))
    def _(pair):
        for head in range(2):
            attend(pair, head)

    copies.start("ctx", ctx, ctx_hbm)
    copies.start("qkv_grad", qkv_grad, qkv_grad_hbm)
    last_weights().wait()

    @pl.loop(0, parts)
    def _(part):
        columns = span(part, size)
        tokens[:, columns] = (
            dot(ctx[...], w_dense[:, columns], 1, 0) + dot(act[...], w_fc2[:, columns], 1, 0)
        ).astype(BF16)
        branch_copy(part).start()

    for name in ("hidden", "grad", "act", "slope"):
        for block in range(blocks):
            row_copy(name, block).wait()
    copies.wait("stats", "ctx", "qkv_grad")
    for part in range(parts):
        branch_copy(part).wait()


def forward(lengths, freq, tokens, cot, gain, bias, b_qkv, b_fc1, w_qkv, w_fc1, w_dense, w_fc2):
    slot_len, width = tokens.shape
    units, heads, ctx_width = w_fc2.shape[0], w_qkv.shape[1], w_dense.shape[0]
    row_kinds = (width, width, units, units, ctx_width, heads)

    def room(rows, columns, kind=BF16):
        return pltpu.VMEM((rows, columns), kind)

    return kernel_call(
        forward_kernel,
        "forward",
        [made(slot_len, columns) for columns in row_kinds]
        + [made(slot_len, 128, F32), made(slot_len, width)],
        grid=(1,),
        in_specs=[SCALARS] + [kept(a) for a in (freq, gain, bias, b_qkv, b_fc1)] + [AWAY] * 6,
        out_specs=[AWAY] * 8,
        scratch_shapes=[room(slot_len, width)] * 3
        + [pltpu.VMEM(w.shape, BF16) for w in (w_qkv, w_fc1, w_dense, w_fc2)]
        + [
            room(slot_len, heads),
            room(slot_len, units),
            room(slot_len, units),
            room(slot_len, ctx_width),
            room(slot_len, ctx_width),
            room(slot_len, heads),
        ]
        + [room(slot_len, 128, F32)] * 4
        + [
            room(slot_len, HEAD_DIM, F32),
            room(slot_len, 2 * HEAD_DIM),
            room(slot_len, 6 * HEAD_DIM),
            pltpu.SemaphoreType.DMA((80,)),
        ],
    )(lengths, freq, gain, bias, b_qkv, b_fc1, tokens, cot, w_qkv, w_fc1, w_dense, w_fc2)


def backward_kernel(
    places_ref,
    grad_hbm,
    slope_hbm,
    qkv_grad_hbm,
    tokens_hbm,
    stats_hbm,
    w_fc2_hbm,
    w_fc1_hbm,
    w_qkv_hbm,
    norm_sum_ref,
    grad_sum_ref,
    head_sum_ref,
    unit_sum_ref,
    up_grad_hbm,
    *rest,
):
    blocks, scratch = rest[: len(BLOCK_NAMES)], rest[len(BLOCK_NAMES) :]
    grad, slope, qkv_grad, tokens, stats, w_fc2, w_fc1, w_qkv, *scratch = scratch
    up_grad, hidden, gain_sum, shift_sum, grad_sum, head_sum, unit_sum, sems = scratch
    copies = Copies(sems)
    slot_len, width = grad.shape
    units, size = w_fc2.shape[0], 512

    def part_of(part):
        return span(part, size)

    def bring_rows(name, part, source, target):
        at = part_of(part)
        copies.start((name, part), source.at[at, :], target.at[at, :])

    def add_to(ref, columns, array):
        ref[:, columns] += jnp.sum(array, axis=0, keepdims=True)

    def to_units(rows, part):
        at, columns = part_of(rows), part_of(part)
        up = dot(grad[at, :], w_fc2[columns, :], 1, 1) * slope[at, columns].astype(F32)
        up = up.astype(BF16)
        up_grad[at, columns] = up
        add_to(unit_sum, columns, up.astype(F32))

    def to_hidden(rows, part):
        at, columns = part_of(rows), part_of(part)
        result = dot(up_grad[at, :], w_fc1[columns, :], 1, 1) + dot(
            qkv_grad[at, :], w_qkv[columns, :], 1, 1
        )
        hidden[at, columns] = result.astype(BF16)
        normed = (tokens[at, columns].astype(F32) - stats[at, 0:1]) * stats[at, 1:2]
        add_to(gain_sum, columns, result * normed)
        add_to(shift_sum, columns, result)

    parts = width // size
    first_block = copies.numbered(("blocks",), parts * len(blocks))["blocks"]

    def blocks_of(which, do):
        each_block_copy(copies, places_ref, hidden, blocks, which, size, first_block, do)

    for part in range(2):
        bring_rows("grad", part, grad_hbm, grad)
        bring_rows("slope", part, slope_hbm, slope)
        bring_rows("w_fc2", part, w_fc2_hbm, w_fc2)
    for total in (gain_sum, shift_sum, grad_sum, head_sum, unit_sum):
        total[...] = jnp.zeros_like(total)
    copies.wait(("w_fc2", 0), ("grad", 0), ("slope", 0))
    copies.start("w_fc1", w_fc1_hbm, w_fc1)
    copies.start("w_qkv", w_qkv_hbm, w_qkv)
    copies.start("qkv_grad", qkv_grad_hbm, qkv_grad)
    copies.start("tokens", tokens_hbm, tokens)
    copies.start("stats", stats_hbm, stats)

    @pl.loop(0, 4)
    def _(turn):
        rows, part = turn // 2, turn % 2

        @pl.when(turn == 1)
        def _():
            copies.wait(("w_fc2", 1))

        @pl.when(turn == 2)
        def _():
            copies.wait(("grad", 1), ("slope", 1))

        to_units(rows, part)

        @pl.when(part == 0)
        def _():
            add_to(grad_sum, slice(0, width), grad[part_of(rows), :].astype(F32))

    copies.start("up_grad", up_grad, up_grad_hbm)
    copies.wait("w_fc1", "w_qkv", "qkv_grad", "tokens", "stats")
    add_to(head_sum, slice(0, qkv_grad.shape[1]), qkv_grad[...].astype(F32))

    @pl.loop(0, parts)
    def _(part):
        for rows in range(slot_len // size):
            to_hidden(rows, part)
        blocks_of((part,), start)

    for ref, first, total in (
        (norm_sum_ref, 0, gain_sum),
        (norm_sum_ref, 16, shift_sum),
        (grad_sum_ref, 0, grad_sum),
        (head_sum_ref, 0, head_sum),
        (unit_sum_ref, 0, unit_sum),
    ):
        share = total.shape[1] // 16
        if share < BLOCK:
            ref[...] = jnp.zeros_like(ref)
        for row in range(16):
            ref[first + row : first + row + 1, 0:share] = total[:, row * share : row * share + share]
    copies.wait("up_grad")
    blocks_of(range(parts), wait)


def backward(places, grad, slope, qkv_grad, tokens, stats, w_fc2, w_fc1, w_qkv):
    slot_len, width = tokens.shape
    units, heads = w_fc2.shape[0], w_qkv.shape[1]
    sizes = (width, width, width, heads, units)
    sums = [made(rows, BLOCK, F32) for rows in (32, 16, 16, 16)]
    arrays = (grad, slope, qkv_grad, tokens, stats, w_fc2, w_fc1, w_qkv)
    norm_sum, grad_sum, head_sum, unit_sum, up_grad, *blocks = kernel_call(
        backward_kernel,
        "backward",
        sums + [made(slot_len, units)] + block_shapes(width),
        grid=(1,),
        in_specs=[SCALARS] + [AWAY] * len(arrays),
        out_specs=[kept(array) for array in sums] + [AWAY] * (1 + len(BLOCK_NAMES)),
        scratch_shapes=[pltpu.VMEM(array.shape, array.dtype) for array in arrays]
        + [pltpu.VMEM((slot_len, units), BF16), pltpu.VMEM((slot_len, width), BF16)]
        + [pltpu.VMEM((1, size), F32) for size in sizes]
        + [pltpu.SemaphoreType.DMA((64,))],
    )(places, *arrays)
    sums = (norm_sum, grad_sum, head_sum, unit_sum)
    return up_grad, sums, dict(zip(BLOCK_NAMES, blocks))


def weight_kernel(order_ref, *refs):
    lefts, (first_ref, second_ref, *sums, out_ref) = refs[:AT_ONCE], refs[AT_ONCE:]
    cut, end = first_ref.shape[1], first_ref.shape[1] + second_ref.shape[1]
    left = jnp.concatenate([ref[...] for ref in lefts], axis=1)
    out_ref[:, 0:cut] = dot(left, first_ref[...], 0, 0).astype(BF16)
    out_ref[:, cut:end] = dot(left, second_ref[...], 0, 0).astype(BF16)
    if sums:
        for half in range(AT_ONCE):
            block = order_ref[AT_ONCE * pl.program_id(0) + half]
            lines = [
                ref[pl.ds(first + block, 1), :]
                for ref in sums
                for first in range(0, ref.shape[0], 16)
            ]
            lines.append(jnp.zeros((BLOCK - len(lines), BLOCK), F32))
            columns = jnp.concatenate(lines, axis=0).T
            out_ref[half * BLOCK : half * BLOCK + BLOCK, end:] = columns.astype(BF16)


def weight_blocks(order, left, first, second, *sums):
    slot_len = left.shape[0]
    width = first.shape[1] + second.shape[1] + (BLOCK if sums else 0)
    return kernel_call(
        weight_kernel,
        "weights",
        made(left.shape[1], width),
        prefetch=1,
        grid=(left.shape[1] // (AT_ONCE * BLOCK),),
        in_specs=[
            *[
                pl.BlockSpec(
                    (slot_len, BLOCK),
                    functools.partial(lambda at, i, order: (0, order[AT_ONCE * i + at]), at),
                )
                for at in range(AT_ONCE)
            ],
            kept(first),
            kept(second),
            *[kept(array) for array in sums],
        ],
        out_specs=pl.BlockSpec((AT_ONCE * BLOCK, width), lambda i, order: (i, 0)),
    )(order, *[left] * AT_ONCE, first, second, *sums)


def combine(name, *sums):
    arrays = [term[0] for terms in sums for term in terms]
    specs = [
        pl.BlockSpec((term[1], term[0].shape[1]), functools.partial(lambda at, _: (at, 0), term[2]))
        for terms in sums
        for term in terms
    ]
    heights = [max(term[4] for term in terms) for terms in sums]

    def kernel(*refs):
        ins, outs = list(refs[: len(arrays)]), refs[len(arrays) :]
        for terms, height, out in zip(sums, heights, outs):
            mine = [(ins.pop(0), term[3], term[4]) for term in terms]
            cuts = sorted({cut for _, low, high in mine for cut in (low, high)})
            for low, high in zip(cuts, cuts[1:]):
                parts = [
                    ref[low - first : high - first, :].astype(F32)
                    for ref, first, last in mine
                    if first <= low and high <= last
                ]
                out[low:high, :] = functools.reduce(lambda a, b: a + b, parts).astype(BF16)

    shapes = [made(height, terms[0][0].shape[1]) for height, terms in zip(heights, sums)]
    return kernel_call(
        kernel,
        name,
        shapes,
        grid=(1,),
        in_specs=specs,
        out_specs=[pl.BlockSpec(shape.shape, lambda _: (0, 0)) for shape in shapes],
    )(*arrays)


def whole_term(array, low=0):
    return (array, array.shape[0], 0, low, low + array.shape[0])


def output_kernel(lengths_ref, tokens_ref, branch_ref, b_dense_ref, b_fc2_ref, out_ref):
    bias = b_dense_ref[...].astype(F32) + b_fc2_ref[...].astype(F32)
    rows = tokens_ref.shape[0]
    place = pl.program_id(0) * rows + lax.broadcasted_iota(jnp.int32, (rows, 1), 0)
    total = jnp.where(
        place < ends_of(lengths_ref)[-1], branch_ref[...].astype(F32) + bias[None], 0.0
    )
    out_ref[...] = (tokens_ref[...].astype(F32) + total).astype(BF16)


def finish_output(lengths, tokens, branch_sum, b_dense, b_fc2):
    slot_len, width = tokens.shape
    row = pl.BlockSpec((ROWS, width), lambda i: (i, 0))
    return kernel_call(
        output_kernel,
        "output",
        made(slot_len, width),
        grid=(slot_len // ROWS,),
        in_specs=[SCALARS, row, row, kept(b_dense), kept(b_fc2)],
        out_specs=row,
    )(lengths, tokens, branch_sum, b_dense, b_fc2)


def input_kernel(places_ref, *refs):
    *terms, tokens_ref, cot_ref, stats_ref, gain_ref, out_ref = refs
    total = functools.reduce(lambda a, b: a + b, [t[...].astype(F32) for t in terms])
    inv_sigma = stats_ref[:, 1:2]
    normed = (tokens_ref[...].astype(F32) - stats_ref[:, 0:1]) * inv_sigma
    scaled = total * gain_ref[...].astype(F32)[None]
    out_ref[...] = (
        cot_ref[...].astype(F32)
        + inv_sigma
        * (
            scaled
            - jnp.mean(scaled, axis=1, keepdims=True)
            - normed * jnp.mean(scaled * normed, axis=1, keepdims=True)
        )
    ).astype(BF16)


def input_rows(places, terms, tokens, cot, stats, gain):
    width = tokens.shape[1]

    def mine(columns):
        return pl.BlockSpec((BLOCK, columns), lambda i, places: (places[0], 0))

    return kernel_call(
        input_kernel,
        "input",
        made(BLOCK, width),
        prefetch=1,
        grid=(1,),
        in_specs=[kept(t) for t in terms] + [mine(width), mine(width), mine(128), kept(gain)],
        out_specs=pl.BlockSpec((BLOCK, width), lambda *_: (0, 0)),
    )(places, *terms, tokens, cot, stats, gain)


def place_kernel(blocks, places_ref, *refs):
    pieces, out_ref, sems = refs[: len(blocks)], refs[-2], refs[-1]
    copies = []
    for i, ((offset, low, high), piece) in enumerate(zip(blocks, pieces)):
        first = pl.multiple_of(places_ref[OFFSETS.index(offset)] * BLOCK, BLOCK)
        copies.append(
            pltpu.make_async_copy(
                piece, out_ref.at[pl.ds(first + low, high - low), :], sems.at[i]
            )
        )
    for copy in copies:
        copy.start()
    for copy in copies:
        copy.wait()


def place_rows(places, blocks, pieces, whole=None):
    rest = {} if whole is None else {"input_output_aliases": {len(pieces) + 1: 0}}
    given = [] if whole is None else [whole]
    return kernel_call(
        functools.partial(place_kernel, blocks),
        "place",
        made(8 * BLOCK, pieces[0].shape[1]),
        in_specs=[SCALARS] + [NEAR] * len(pieces) + [AWAY] * len(given),
        out_specs=AWAY,
        scratch_shapes=[pltpu.SemaphoreType.DMA((len(pieces),))],
        **rest,
    )(places, *pieces, *given)


def up_kernel(near_ref, far_ref, first_ref, second_ref):
    total = near_ref[...].astype(F32) + far_ref[...].astype(F32)
    cut = first_ref.shape[1]
    first_ref[...] = total[:, :cut]
    second_ref[...] = total[:, cut:]


def down_kernel(near_ref, far_ref, first_ref, second_ref, sums_ref):
    total = near_ref[...].astype(F32) + far_ref[...].astype(F32)
    cut, end = first_ref.shape[0], first_ref.shape[0] + second_ref.shape[0]
    first_ref[...] = total[:, :cut].T
    second_ref[...] = total[:, cut:end].T
    sums_ref[...] = total[:, end:].T[: sums_ref.shape[0]]


def last_sum(kernel, name, shapes, near, far):
    return kernel_call(
        kernel,
        name,
        [made(*shape, F32) for shape in shapes],
        grid=(1,),
        in_specs=[pl.BlockSpec(far.shape, lambda _: (0, 0))] * 2,
        out_specs=[pl.BlockSpec(shape, lambda _: (0, 0)) for shape in shapes],
    )(near, far)


def shift(array, axis, size, by):
    return lax.ppermute(array, axis, [(i, (i + by) % size) for i in range(size)])


def y_up(array):
    return shift(array, "y", 4, 1)


def y_down(array):
    return shift(array, "y", 4, 3)


def across(array):
    return shift(array, "zl", 2, 1)


def after(arrays, *earlier):
    return lax.optimization_barrier((arrays, earlier))[0]


class TensorSum:
    def __init__(self, blocks):
        self.blocks = blocks

    def send_far(self):
        b = self.blocks
        self.far = across(b[0]), y_up(b[1]), y_down(b[2])

    def send_middle(self, earlier):
        b = self.blocks
        far = *self.far[:2], after(self.far[2], earlier)
        sent = combine(
            "middle",
            *[
                [whole_term(b[offset]), whole_term(part, low)]
                for offset, part, (low, _) in zip(((0, 2), (1, 1), (1, 3)), far, PARTS)
            ],
        )
        self.middle = y_up(sent[0]), across(sent[1]), y_down(sent[2])
        return sent

    def send_near(self, earlier):
        b = self.blocks
        two_on, diagonal, other = self.middle
        other = after(other, earlier)
        sent = combine(
            "near",
            [whole_term(b[(0, 1)]), whole_term(two_on), whole_term(diagonal)],
            [whole_term(b[(1, 0)]), whole_term(other)],
        )
        self.near = [y_up(sent[0]), across(sent[1]), y_down(after(b[(0, 3)], sent))]
        return sent

    def terms(self):
        return [self.blocks[(0, 0)], *self.near]


class TensorGather:
    def __init__(self, places, rows):
        self.places, self.rows = places, rows
        self.one = y_up(rows), y_down(rows), across(rows)

    def second(self, earlier):
        before, ahead, partner = self.one = after(self.one, earlier)
        self.two = y_down(ahead), across(ahead), y_up(partner)
        return self.one

    def third(self, earlier):
        two_on, diagonal, other = self.two = after(self.two, earlier)
        (a, b), (c, d), (e, f) = PARTS
        self.three = across(two_on[a:b]), y_down(diagonal[c:d]), y_up(other[e:f])
        blocks = [(0, 0), (0, 3), (0, 1), (1, 0), (0, 2), (1, 1), (1, 3)]
        self.whole = place_rows(
            self.places,
            [(offset, 0, BLOCK) for offset in blocks],
            [self.rows, *self.one, *self.two],
        )
        return self.whole

    def finish(self, earlier):
        parts = after(self.three, earlier)
        return place_rows(
            self.places, [(FAR, low, high) for low, high in PARTS], list(parts), self.whole
        )


class DataSum:
    def __init__(self, partial_sums, earlier):
        self.near = lax.psum_scatter(
            after(partial_sums, earlier), ("x", "core"), scatter_dimension=0, tiled=True
        )

    def send(self, earlier):
        self.near = after(self.near, earlier)
        self.far = shift(self.near[BLOCK:], "zh", 2, 1)

    def finish(self, kernel, name, shapes, earlier):
        return last_sum(kernel, name, shapes, self.near, after(self.far, earlier))


def dp_order():
    half = lax.axis_index("zh")
    return jnp.stack(
        [(half + part) % 2 * 8 + block for block in range(8) for part in range(2)]
    ).astype(jnp.int32)


def per_device(
    tokens,
    cotangent,
    seq_lengths,
    ln_gain,
    ln_bias,
    w_qkv,
    b_qkv,
    w_dense,
    b_dense,
    w_fc1,
    b_fc1,
    w_fc2,
    b_fc2,
):
    units = w_fc2.shape[0]
    plane, place = lax.axis_index("zl"), lax.axis_index("y")
    places = jnp.stack(
        [(plane + planes) % 2 * 4 + (place + steps) % 4 for planes, steps in OFFSETS]
    ).astype(jnp.int32)
    order = dp_order()
    frequency = 10000.0 ** (-jnp.arange(ROTARY // 2, dtype=F32) * 2.0 / ROTARY)
    frequency = jnp.tile(frequency, 8)[None]
    hidden, grad, activated, slope, context, qkv_grad, stats, branch_part = forward(
        seq_lengths,
        frequency,
        tokens,
        cotangent,
        ln_gain,
        ln_bias,
        b_qkv,
        b_fc1,
        w_qkv,
        w_fc1,
        w_dense,
        w_fc2,
    )
    branch_sum = lax.psum(branch_part, TENSOR)
    up_grad, sums, blocks = backward(
        after(places, branch_part), grad, slope, qkv_grad, tokens, stats, w_fc2, w_fc1, w_qkv
    )
    hidden_sum = TensorSum(blocks)
    hidden_sum.send_far()
    norm_sum, *sums = sums
    norm_across = across(norm_sum)
    up_part = weight_blocks(after(order, up_grad), hidden, up_grad, qkv_grad)
    done = hidden_sum.send_middle((up_part, norm_across))
    up = DataSum(up_part, done)
    norm_sum = norm_sum + norm_across
    around = [y_up(norm_sum), y_down(norm_sum), shift(norm_sum, "y", 4, 2)]
    done = hidden_sum.send_near((done, around))
    norm_sum = norm_sum + around[0] + around[1] + around[2]
    down_part = weight_blocks(after(order, done), grad, activated, context, norm_sum, *sums)
    rows = input_rows(
        after(places, down_part), hidden_sum.terms(), tokens, cotangent, stats, ln_gain
    )
    down = DataSum(down_part, rows)
    input_grad = TensorGather(places, rows)
    done = input_grad.second((rows, branch_sum))
    up.send(done)
    down.send(up.near)
    output = finish_output(after(seq_lengths, down.near), tokens, branch_sum, b_dense, b_fc2)
    done = input_grad.third(output)
    input_grad.three = after(input_grad.three, done)
    grad_fc1, grad_qkv = up.finish(
        up_kernel, "up", ((BLOCK, units), (BLOCK, w_qkv.shape[1])), input_grad.three[0]
    )
    grad_fc2, grad_dense, small = down.finish(
        down_kernel,
        "down",
        ((units, BLOCK), (w_dense.shape[0], BLOCK), (8, BLOCK)),
        grad_qkv,
    )
    input_grad = input_grad.finish(small)
    out_bias = small[2]
    return (
        output,
        input_grad,
        small[0],
        small[1],
        grad_qkv,
        small[3, :48],
        grad_dense,
        out_bias,
        grad_fc1,
        small[4, :64],
        grad_fc2,
        out_bias,
    )


def solution(mesh):
    parts = Mesh(mesh.devices.reshape(2, 4, 2, 2, 4), DP + TENSOR)
    rows = P(DP, None)
    placed = (
        rows,
        rows,
        rows,
        P(),
        P(),
        P(None, TENSOR),
        P(TENSOR),
        P(TENSOR, None),
        P(),
        P(None, TENSOR),
        P(TENSOR),
        P(TENSOR, None),
        P(),
    )
    return jax.shard_map(
        per_device,
        mesh=parts,
        in_specs=placed,
        out_specs=(
            rows,
            rows,
            P(DP),
            P(DP),
            P(DP, TENSOR),
            P(TENSOR + DP),
            P(TENSOR, DP),
            P(DP),
            P(DP, TENSOR),
            P(TENSOR + DP),
            P(TENSOR, DP),
            P(DP),
        ),
        check_vma=False,
    )
```

profile of v0, /device:TPU:0, one launch (start us, length us, event | category | flops | bytes accessed | tf_op | source)
XLA Modules:
  0.0 264.1 jit_solution(3872464347700279457)
XLA Ops:
  8.1 0.6 broadcast_in_dim_tile.3.freq_ref
  8.7 0.6 stack.103.places_ref
  9.3 44.3 %forward.1 = (bf16[1024,2048]{1,0:T(8,128)(2,1)}, bf16[1024,2048]{1,0:T(8,128)(2,1)}, bf16[1024,1024]{1,0:T(8,128)(2,1)}, bf16[1024,1024]{1,0:T(8,128)(2,1)}, bf...) custom-call(s32[1,8]{1,0:T(1,128)} %lengths_ref.2, ...), custom_call_target="tpu_custom_call" | custom-call | flops 1 | bytes 1 | tf_op jit(solution)/shard_map/forward/pallas_call | solution.py:392
  53.6 0.0 reduce-scatter.5.cloned.1.call-start
  53.7 20.4 %backward.1 = (f32[32,128]{1,0:T(8,128)}, f32[16,128]{1,0:T(8,128)}, f32[16,128]{1,0:T(8,128)}, f32[16,128]{1,0:T(8,128)}, bf16[1024,1024]{1,0:T(8,128)(2,1)}, /...) custom-call(s32[8]{0:T(128)} %stack.103.places_ref, ...), custom_call_target="tpu_custom_call" | custom-call | flops 1 | bytes 1 | tf_op jit(solution)/shard_map/backward/pallas_call | solution.py:540
  74.1 2.1 collective-permute-start
  76.2 1.6 collective-permute-start.1
  77.8 1.7 collective-permute-start.2
  79.4 0.1 collective-permute-start.3
  79.5 0.6 stack.94.order_ref
  80.1 13.2 %weights.2 = bf16[2048,1792]{1,0:T(8,128)(2,1)} custom-call(s32[16]{0:T(128)} %stack.94.order_ref, bf16[1024,2048]{1,0:T(8,128)(2,1)} %get-tuple-element.86.refs_0_.refs_1_.refs_2_.refs_3_, bf16[1024,2048]{1,0:T(8,128)(2,1)} %get-tuple-element.86.refs_0_.refs_1_.refs_2_.refs_3_, bf16[1024,2048]{1,0:T(8,128)(2,1)} %get-tuple-element.86.refs_0_.refs_1_.refs_2_.refs_3_, ...), custom_call_target="tpu_custom_call" | custom-call | flops 1 | bytes 1 | tf_op jit(solution)/shard_map/weights/pallas_call | solution.py:578
  93.3 19.5 %collective-permute-done.3 = f32[32,128]{1,0:T(8,128)S(1)} collective-permute-done((f32[32,128]{1,0:T(8,128)}, f32[32,128]{1,0:T(8,128)S(1)}, u32[]{:S(2)}, u32[]{:S(2)}) %collective-permute-start.3) | collective-permute-done | bytes 16416 | tf_op jit(solution)/shard_map/ppermute | solution.py:751
  112.9 0.6 copy-done.19
  113.5 0.1 copy-done.14
  113.6 0.1 copy-done.15
  113.7 2.8 %middle.1 = (bf16[128,2048]{1,0:T(8,128)(2,1)}, bf16[128,2048]{1,0:T(8,128)(2,1)}, bf16[128,2048]{1,0:T(8,128)(2,1)}) custom-call(bf16[128,2048]{1,0:T(8,128)(2,1)} %get-tuple-element.78.refs_0_, bf16[48,2048]{1,0:T(8,128)(2,1)} %copy-done.14, bf16[128,2048]{1,0:T(8,128)(2,1)} %get-tuple-element.80.refs_2_, bf16[48,2048]{1,0:T(8,128)(2,1)} %copy-done.15, ...), custom_call_target="tpu_custom_call" | custom-call | flops 1 | bytes 1 | tf_op jit(solution)/shard_map/middle/pallas_call | solution.py:623
  116.6 0.0 reduce-scatter.3.cloned.1.call-start
  116.6 0.9 copy-done.25
  117.6 0.5 collective-permute-start.6
  118.1 1.5 collective-permute-start.4
  119.6 0.5 collective-permute-start.5
  120.1 1.0 collective-permute-start.9
  121.1 1.8 collective-permute-start.8
  122.8 12.6 %collective-permute-done.9 = f32[32,128]{1,0:T(8,128)S(1)} collective-permute-done((f32[32,128]{1,0:T(8,128)S(1)}, f32[32,128]{1,0:T(8,128)S(1)}, u32[]{:S(2)}, u32[]{:S(2)}) %collective-permute-start.9) | collective-permute-done | bytes 16416 | tf_op jit(solution)/shard_map/ppermute | solution.py:751
  135.5 5.3 %collective-permute-done.7 = f32[32,128]{1,0:T(8,128)S(1)} collective-permute-done((f32[32,128]{1,0:T(8,128)S(1)}, f32[32,128]{1,0:T(8,128)S(1)}, u32[]{:S(2)}, u32[]{:S(2)}) %collective-permute-start.7) | collective-permute-done | bytes 16416 | tf_op jit(solution)/shard_map/ppermute | solution.py:751
  140.8 0.8 copy-done.7
  141.6 0.1 copy-done.8
  141.7 0.2 copy-done.9
  141.9 2.9 %near.1 = (bf16[128,2048]{1,0:T(8,128)(2,1)}, bf16[128,2048]{1,0:T(8,128)(2,1)}) custom-call(bf16[128,2048]{1,0:T(8,128)(2,1)} %get-tuple-element.77.refs_0_, bf16[128,2048]{1,0:T(8,128)(2,1)} %copy-done.8, bf16[128,2048]{1,0:T(8,128)(2,1)} %copy-done.9, bf16[128,2048]{1,0:T(8,128)(2,1)} %get-tuple-element.91.refs_3_, bf16[128,2048]{1,0:T(8,128)(2,1)} %copy-done.7), custom_call_target="tpu_custom_call" | custom-call | flops 1 | bytes 1 | tf_op jit(solution)/shard_map/near/pallas_call | solution.py:623
  144.9 1.3 collective-permute-start.12
  146.2 0.7 collective-permute-start.10
  146.9 0.6 add_add_fusion.refs_6_
  147.5 11.0 %weights.3 = bf16[2048,1408]{1,0:T(8,128)(2,1)} custom-call(s32[16]{0:T(128)} %stack.94.order_ref, bf16[1024,2048]{1,0:T(8,128)(2,1)} %get-tuple-element.73.grad_hbm.refs_0_.refs_1_.refs_2_.refs_3_, bf16[1024,2048]{1,0:T(8,128)(2,1)} %get-tuple-element.73.grad_hbm.refs_0_.refs_1_.refs_2_.refs_3_, ...), custom_call_target="tpu_custom_call" | custom-call | flops 1 | bytes 1 | tf_op jit(solution)/shard_map/weights/pallas_call | solution.py:578
  158.5 10.6 %collective-permute-done.12.refs_3_ = bf16[128,2048]{1,0:T(8,128)(2,1)S(1)} collective-permute-done((bf16[128,2048]{1,0:T(8,128)(2,1)S(1)}, bf16[128,2048]{1,0:T(8,128)(2,1)S(1)}, u32[]{:S(2)}, u32[]{:S(2)}) %collective-permute-start.12) | collective-permute-done | bytes 524320 | tf_op jit(solution)/shard_map/ppermute | solution.py:751
  169.1 2.7 %collective-permute-done.10.refs_1_ = bf16[128,2048]{1,0:T(8,128)(2,1)S(1)} collective-permute-done((bf16[128,2048]{1,0:T(8,128)(2,1)}, bf16[128,2048]{1,0:T(8,128)(2,1)S(1)}, u32[]{:S(2)}, u32[]{:S(2)}) %collective-permute-start.10) | collective-permute-done | bytes 524320 | tf_op jit(solution)/shard_map/ppermute | solution.py:751
  171.8 0.8 copy-done.11
  172.6 0.2 copy-done.12
  172.7 4.1 %input.1.refs_0_ = bf16[128,2048]{1,0:T(8,128)(2,1)} custom-call(s32[8]{0:T(128)} %stack.103.places_ref, bf16[128,2048]{1,0:T(8,128)(2,1)} %get-tuple-element.103.refs_0_, bf16[128,2048]{1,0:T(8,128)(2,1)} %copy-done.11, bf16[128,2048]{1,0:T(8,128)(2,1)} %copy-done.12, bf16[128,2048]{1,0:T(8,128)(2,1)} %copy-done.10, bf16[1024,2048]{1,0:T(8,128)(2,1)} %tokens_ref.1, ...), custom_call_target="tpu_custom_call" | custom-call | flops 1 | bytes 1 | tf_op jit(solution)/shard_map/input/pallas_call | solution.py:683
  176.9 1.0 copy-done
  177.9 1.3 collective-permute-start.15
  179.2 10.4 %collective-permute-start.14 = (bf16[128,2048]{1,0:T(8,128)(2,1)S(1)}, bf16[128,2048]{1,0:T(8,128)(2,1)S(1)}, u32[]{:S(2)}, u32[]{:S(2)}) collective-permute-start(bf16[128,2048]{1,0:T(8,128)(2,1)S(1)} %copy-done), channel_id=1, source_target_pairs={{0,3},{1,0},{2,1},{3,2},{4,7},{5,4},{6,5},{7,6},{8,11},{9,8},{10,9... | collective-permute-start | bytes 1572872 | tf_op jit(solution)/shard_map/ppermute | solution.py:751
  189.6 6.6 %collective-permute-done.15.refs_3_ = bf16[128,2048]{1,0:T(8,128)(2,1)S(1)} collective-permute-done((bf16[128,2048]{1,0:T(8,128)(2,1)S(1)}, bf16[128,2048]{1,0:T(8,128)(2,1)S(1)}, u32[]{:S(2)}, u32[]{:S(2)}) %collective-permute-start.15) | collective-permute-done | bytes 524320 | tf_op jit(solution)/shard_map/ppermute | solution.py:751
  196.2 0.1 collective-permute-done.14.refs_2_
  196.3 4.2 %collective-permute-done.13.refs_1_ = bf16[128,2048]{1,0:T(8,128)(2,1)S(1)} collective-permute-done((bf16[128,2048]{1,0:T(8,128)(2,1)S(1)}, bf16[128,2048]{1,0:T(8,128)(2,1)S(1)}, u32[]{:S(2)}, u32[]{:S(2)}) %collective-permute-start.13) | collective-permute-done | bytes 524320 | tf_op jit(solution)/shard_map/ppermute | solution.py:751
  200.5 3.4 %collective-permute-start.17 = (bf16[128,2048]{1,0:T(8,128)(2,1)S(1)}, bf16[128,2048]{1,0:T(8,128)(2,1)S(1)}, u32[]{:S(2)}, u32[]{:S(2)}) collective-permute-start(bf16[128,2048]{1,0:T(8,128)(2,1)S(1)} %collective-permute-done.14.refs_2_), channel_id=1, source_target_pairs={{0,4},{4,0},{1,5},{5,1},{2,6},{6,2},{3,7},{7,3},{8,12},{12,8},{9,1... | collective-permute-start | bytes 1572872 | tf_op jit(solution)/shard_map/ppermute | solution.py:751
  203.9 3.2 %collective-permute-start.16 = (bf16[128,2048]{1,0:T(8,128)(2,1)S(1)}, bf16[128,2048]{1,0:T(8,128)(2,1)S(1)}, u32[]{:S(2)}, u32[]{:S(2)}) collective-permute-start(bf16[128,2048]{1,0:T(8,128)(2,1)S(1)} %collective-permute-done.14.refs_2_), channel_id=1, source_target_pairs={{0,3},{1,0},{2,1},{3,2},{4,7},{5,4},{6,5},{7,6},{8,11},{9,8},{10,9... | collective-permute-start | bytes 1572872 | tf_op jit(solution)/shard_map/ppermute | solution.py:751
  207.1 1.8 slice.34
  208.9 16.0 %reduce-scatter.3.cloned.1.call-done.near_ref = bf16[256,1408]{1,0:T(8,128)(2,1)} async-done(((bf16[2048,1408]{1,0:T(8,128)(2,1)}), bf16[256,1408]{1,0:T(8,128)(2,1)}) %reduce-scatter.3.cloned.1.call-update) | async-done | bytes 720912 | tf_op jit(solution)/shard_map/reduce_scatter | solution.py:838
  224.9 1.0 slice.33
  225.9 3.3 %collective-permute-start.22 = (bf16[128,1408]{1,0:T(8,128)(2,1)S(1)}, bf16[128,1408]{1,0:T(8,128)(2,1)S(1)}, u32[]{:S(2)}, u32[]{:S(2)}) collective-permute-start(bf16[128,1408]{1,0:T(8,128)(2,1)S(1)} %slice.33), channel_id=1, source_target_pairs={{0,64},{64,0},{1,65},{65,1},{2,66},{66,2},{3,67},{67,3},{4,68},{68... | collective-permute-start | bytes 1081352 | tf_op jit(solution)/shard_map/ppermute | solution.py:751
  229.2 6.4 %output.1 = bf16[1024,2048]{1,0:T(8,128)(2,1)} custom-call(s32[1,8]{1,0:T(1,128)} %lengths_ref.2, bf16[1024,2048]{1,0:T(8,128)(2,1)} %tokens_ref.1, bf16[1024,2048]{1,0:T(8,128)(2,1)} %all-reduce.2.cloned.1.call-done.branch_ref, bf16[2048]{0:T(1024)(128)(2,1)} %b_dense_ref.1, bf16[2048]{0:T(1024)(128)(2,1)} %b_fc2_ref.1), custom_call_target="tpu_custom_call" | custom-call | flops 1 | bytes 1 | tf_op jit(solution)/shard_map/output/pallas_call | solution.py:650
  235.7 2.5 collective-permute-start.20
  238.2 0.8 collective-permute-start.19
  239.1 0.1 collective-permute-start.21
  239.2 3.9 %place.2.refs_3_ = bf16[1024,2048]{1,0:T(8,128)(2,1)} custom-call(s32[8]{0:T(128)} %stack.103.places_ref, bf16[128,2048]{1,0:T(8,128)(2,1)} %input.1.refs_0_, bf16[128,2048]{1,0:T(8,128)(2,1)} %copy-done.6, bf16[128,2048]{1,0:T(8,128)(2,1)} %copy-done.5, bf16[128,2048]{1,0:T(8,128)(2,1)} %copy-done.4, bf16[128,2048]{1,0:T(8,128)(2,1)} %copy-done.2, ...), custom_call_target="tpu_custom_call" | custom-call | flops 1 | bytes 1 | tf_op jit(solution)/shard_map/place/pallas_call | solution.py:713
  243.1 2.2 collective-permute-done.21.refs_2_
  245.3 2.3 up.1
  247.7 0.7 copy-done.13
  248.4 2.1 down.1
  250.5 1.2 slice_bitcast_fusion.2
  251.7 1.2 slice_bitcast_fusion
  252.9 1.3 slice_bitcast_fusion.1
  254.2 1.9 place.3
  256.2 0.5 copy.29
  (73 shorter events, 0.3 us)
Async XLA Ops:
  8.0 192.5 %all-reduce.2.cloned.1.call-start = ((), (), s32[]{:S(2)}) async-start(), calls=%async_computation.4 | async-start | bytes 8388608 | tf_op jit(solution)/shard_map/psum | solution.py:894
  53.6 153.5 %reduce-scatter.5.cloned.1.call-start = ((), (), s32[]{:S(2)}) async-start(), calls=%async_computation.3 | async-start | bytes 8257536 | tf_op jit(solution)/shard_map/reduce_scatter | solution.py:838
  74.1 38.8 %collective-permute-start = (bf16[48,2048]{1,0:T(8,128)(2,1)}, bf16[48,2048]{1,0:T(8,128)(2,1)S(1)}, u32[]{:S(2)}, u32[]{:S(2)}) collective-permute-start(bf16[48,2048]{1,0:T(8,128)(2,1)} %get-tuple-element.79), channel_id=1, source_target_pairs={{0,4},{4,0},{1,5},{5,1},{2,6},{6,2},{3,7},{7,3},{8,12},{12,8},{9,1... | collective-permute-start | bytes 589832 | tf_op jit(solution)/shard_map/ppermute | solution.py:751
  76.2 36.7 %collective-permute-start.1 = (bf16[48,2048]{1,0:T(8,128)(2,1)}, bf16[48,2048]{1,0:T(8,128)(2,1)S(1)}, u32[]{:S(2)}, u32[]{:S(2)}) collective-permute-start(bf16[48,2048]{1,0:T(8,128)(2,1)} %get-tuple-element.81), channel_id=1, source_target_pairs={{0,1},{1,2},{2,3},{3,0},{4,5},{5,6},{6,7},{7,4},{8,9},{9,10},{10,1... | collective-permute-start | bytes 589832 | tf_op jit(solution)/shard_map/ppermute | solution.py:751
  77.8 35.1 %collective-permute-start.2 = (bf16[32,2048]{1,0:T(8,128)(2,1)}, bf16[32,2048]{1,0:T(8,128)(2,1)S(1)}, u32[]{:S(2)}, u32[]{:S(2)}) collective-permute-start(bf16[32,2048]{1,0:T(8,128)(2,1)} %get-tuple-element.83), channel_id=1, source_target_pairs={{0,3},{1,0},{2,1},{3,2},{4,7},{5,4},{6,5},{7,6},{8,11},{9,8},{10,9... | collective-permute-start | bytes 393224 | tf_op jit(solution)/shard_map/ppermute | solution.py:751
  79.4 33.4 %collective-permute-start.3 = (f32[32,128]{1,0:T(8,128)}, f32[32,128]{1,0:T(8,128)S(1)}, u32[]{:S(2)}, u32[]{:S(2)}) collective-permute-start(f32[32,128]{1,0:T(8,128)} %get-tuple-element.87), channel_id=1, source_target_pairs={{0,4},{4,0},{1,5},{5,1},{2,6},{6,2},{3,7},{7,3},{8,12},{12,8},{9,1... | collective-permute-start | bytes 49160 | tf_op jit(solution)/shard_map/ppermute | solution.py:751
  112.9 0.7 copy-start.19
  112.9 0.7 copy-start.14
  112.9 0.8 copy-start.15
  116.5 1.0 copy-start.25
  116.5 1.5 copy-start.24
  116.5 3.1 %copy-start.23 = (bf16[128,2048]{1,0:T(8,128)(2,1)S(1)}, bf16[128,2048]{1,0:T(8,128)(2,1)}, u32[]{:S(2)}) copy-start(bf16[128,2048]{1,0:T(8,128)(2,1)} %get-tuple-element.90) | copy-start | bytes 1572868
  116.5 3.5 %copy-start.20 = (f32[32,128]{1,0:T(8,128)S(1)}, f32[32,128]{1,0:T(8,128)}, u32[]{:S(2)}) copy-start(f32[32,128]{1,0:T(8,128)} %get-tuple-element.87) | copy-start | bytes 49156
  116.6 28.3 %copy-start.22 = (bf16[128,2048]{1,0:T(8,128)(2,1)S(1)}, bf16[128,2048]{1,0:T(8,128)(2,1)}, u32[]{:S(2)}) copy-start(bf16[128,2048]{1,0:T(8,128)(2,1)} %get-tuple-element.105) | copy-start | bytes 1572868
  116.6 108.3 %reduce-scatter.3.cloned.1.call-start = ((), (), s32[]{:S(2)}) async-start(), calls=%async_computation.2 | async-start | bytes 6488064 | tf_op jit(solution)/shard_map/reduce_scatter | solution.py:838
  117.6 23.1 %collective-permute-start.6 = (bf16[128,2048]{1,0:T(8,128)(2,1)S(1)}, bf16[128,2048]{1,0:T(8,128)(2,1)S(1)}, u32[]{:S(2)}, u32[]{:S(2)}) collective-permute-start(bf16[128,2048]{1,0:T(8,128)(2,1)S(1)} %copy-done.25), channel_id=1, source_target_pairs={{0,3},{1,0},{2,1},{3,2},{4,7},{5,4},{6,5},{7,6},{8,11},{9,8},{10,9... | collective-permute-start | bytes 1572872 | tf_op jit(solution)/shard_map/ppermute | solution.py:751
  118.1 22.6 %collective-permute-start.4 = (bf16[128,2048]{1,0:T(8,128)(2,1)S(1)}, bf16[128,2048]{1,0:T(8,128)(2,1)S(1)}, u32[]{:S(2)}, u32[]{:S(2)}) collective-permute-start(bf16[128,2048]{1,0:T(8,128)(2,1)S(1)} %copy-done.24), channel_id=1, source_target_pairs={{0,1},{1,2},{2,3},{3,0},{4,5},{5,6},{6,7},{7,4},{8,9},{9,10},{10,1... | collective-permute-start | bytes 1572872 | tf_op jit(solution)/shard_map/ppermute | solution.py:751
  119.6 21.1 %collective-permute-start.5 = (bf16[128,2048]{1,0:T(8,128)(2,1)S(1)}, bf16[128,2048]{1,0:T(8,128)(2,1)S(1)}, u32[]{:S(2)}, u32[]{:S(2)}) collective-permute-start(bf16[128,2048]{1,0:T(8,128)(2,1)S(1)} %copy-done.23), channel_id=1, source_target_pairs={{0,4},{4,0},{1,5},{5,1},{2,6},{6,2},{3,7},{7,3},{8,12},{12,8},{9,1... | collective-permute-start | bytes 1572872 | tf_op jit(solution)/shard_map/ppermute | solution.py:751
  120.1 15.4 %collective-permute-start.9 = (f32[32,128]{1,0:T(8,128)S(1)}, f32[32,128]{1,0:T(8,128)S(1)}, u32[]{:S(2)}, u32[]{:S(2)}) collective-permute-start(f32[32,128]{1,0:T(8,128)S(1)} %add.196), channel_id=1, source_target_pairs={{0,2},{1,3},{2,0},{3,1},{4,6},{5,7},{6,4},{7,5},{8,10},{9,11},{10,... | collective-permute-start | bytes 49160 | tf_op jit(solution)/shard_map/ppermute | solution.py:751
  121.1 14.4 %collective-permute-start.8 = (f32[32,128]{1,0:T(8,128)S(1)}, f32[32,128]{1,0:T(8,128)S(1)}, u32[]{:S(2)}, u32[]{:S(2)}) collective-permute-start(f32[32,128]{1,0:T(8,128)S(1)} %add.196), channel_id=1, source_target_pairs={{0,3},{1,0},{2,1},{3,2},{4,7},{5,4},{6,5},{7,6},{8,11},{9,8},{10,9... | collective-permute-start | bytes 49160 | tf_op jit(solution)/shard_map/ppermute | solution.py:751
  135.4 5.3 %collective-permute-start.7 = (f32[32,128]{1,0:T(8,128)S(1)}, f32[32,128]{1,0:T(8,128)S(1)}, u32[]{:S(2)}, u32[]{:S(2)}) collective-permute-start(f32[32,128]{1,0:T(8,128)S(1)} %add.196), channel_id=1, source_target_pairs={{0,1},{1,2},{2,3},{3,0},{4,5},{5,6},{6,7},{7,4},{8,9},{9,10},{10,1... | collective-permute-start | bytes 49160 | tf_op jit(solution)/shard_map/ppermute | solution.py:751
  140.7 0.9 copy-start.7
  140.7 1.0 copy-start.8
  140.8 1.2 copy-start.9
  144.9 24.2 %collective-permute-start.12 = (bf16[128,2048]{1,0:T(8,128)(2,1)S(1)}, bf16[128,2048]{1,0:T(8,128)(2,1)S(1)}, u32[]{:S(2)}, u32[]{:S(2)}) collective-permute-start(bf16[128,2048]{1,0:T(8,128)(2,1)S(1)} %copy-done.22), channel_id=1, source_target_pairs={{0,3},{1,0},{2,1},{3,2},{4,7},{5,4},{6,5},{7,6},{8,11},{9,8},{10,9... | collective-permute-start | bytes 1572872 | tf_op jit(solution)/shard_map/ppermute | solution.py:751
  146.2 25.6 %collective-permute-start.10 = (bf16[128,2048]{1,0:T(8,128)(2,1)}, bf16[128,2048]{1,0:T(8,128)(2,1)S(1)}, u32[]{:S(2)}, u32[]{:S(2)}) collective-permute-start(bf16[128,2048]{1,0:T(8,128)(2,1)} %get-tuple-element.94), channel_id=1, source_target_pairs={{0,1},{1,2},{2,3},{3,0},{4,5},{5,6},{6,7},{7,4},{8,9},{9,10},{10,1... | collective-permute-start | bytes 1572872 | tf_op jit(solution)/shard_map/ppermute | solution.py:751
  146.9 24.9 %collective-permute-start.11 = (bf16[128,2048]{1,0:T(8,128)(2,1)}, bf16[128,2048]{1,0:T(8,128)(2,1)S(1)}, u32[]{:S(2)}, u32[]{:S(2)}) collective-permute-start(bf16[128,2048]{1,0:T(8,128)(2,1)} %get-tuple-element.95), channel_id=1, source_target_pairs={{0,4},{4,0},{1,5},{5,1},{2,6},{6,2},{3,7},{7,3},{8,12},{12,8},{9,1... | collective-permute-start | bytes 1572872 | tf_op jit(solution)/shard_map/ppermute | solution.py:751
  169.1 2.7 %copy-start.10 = (bf16[128,2048]{1,0:T(8,128)(2,1)}, bf16[128,2048]{1,0:T(8,128)(2,1)S(1)}, u32[]{:S(2)}) copy-start(bf16[128,2048]{1,0:T(8,128)(2,1)S(1)} %collective-permute-done.12.refs_3_) | copy-start | bytes 1572868
  171.8 0.8 copy-start.11
  171.8 1.0 copy-start.12
  176.9 1.0 copy-start
  177.9 18.3 %collective-permute-start.15 = (bf16[128,2048]{1,0:T(8,128)(2,1)S(1)}, bf16[128,2048]{1,0:T(8,128)(2,1)S(1)}, u32[]{:S(2)}, u32[]{:S(2)}) collective-permute-start(bf16[128,2048]{1,0:T(8,128)(2,1)S(1)} %copy-done), channel_id=1, source_target_pairs={{0,4},{4,0},{1,5},{5,1},{2,6},{6,2},{3,7},{7,3},{8,12},{12,8},{9,1... | collective-permute-start | bytes 1572872 | tf_op jit(solution)/shard_map/ppermute | solution.py:751
  179.2 17.1 %collective-permute-start.14 = (bf16[128,2048]{1,0:T(8,128)(2,1)S(1)}, bf16[128,2048]{1,0:T(8,128)(2,1)S(1)}, u32[]{:S(2)}, u32[]{:S(2)}) collective-permute-start(bf16[128,2048]{1,0:T(8,128)(2,1)S(1)} %copy-done), channel_id=1, source_target_pairs={{0,3},{1,0},{2,1},{3,2},{4,7},{5,4},{6,5},{7,6},{8,11},{9,8},{10,9... | collective-permute-start | bytes 1572872 | tf_op jit(solution)/shard_map/ppermute | solution.py:751
  189.6 10.9 %collective-permute-start.13 = (bf16[128,2048]{1,0:T(8,128)(2,1)S(1)}, bf16[128,2048]{1,0:T(8,128)(2,1)S(1)}, u32[]{:S(2)}, u32[]{:S(2)}) collective-permute-start(bf16[128,2048]{1,0:T(8,128)(2,1)S(1)} %copy-done), channel_id=1, source_target_pairs={{0,1},{1,2},{2,3},{3,0},{4,5},{5,6},{6,7},{7,4},{8,9},{9,10},{10,1... | collective-permute-start | bytes 1572872 | tf_op jit(solution)/shard_map/ppermute | solution.py:751
  196.2 39.4 %copy-start.4 = (bf16[128,2048]{1,0:T(8,128)(2,1)}, bf16[128,2048]{1,0:T(8,128)(2,1)S(1)}, u32[]{:S(2)}) copy-start(bf16[128,2048]{1,0:T(8,128)(2,1)S(1)} %collective-permute-done.15.refs_3_) | copy-start | bytes 1572868
  196.3 39.3 %copy-start.5 = (bf16[128,2048]{1,0:T(8,128)(2,1)}, bf16[128,2048]{1,0:T(8,128)(2,1)S(1)}, u32[]{:S(2)}) copy-start(bf16[128,2048]{1,0:T(8,128)(2,1)S(1)} %collective-permute-done.14.refs_2_) | copy-start | bytes 1572868
  200.5 35.1 %copy-start.6 = (bf16[128,2048]{1,0:T(8,128)(2,1)}, bf16[128,2048]{1,0:T(8,128)(2,1)S(1)}, u32[]{:S(2)}) copy-start(bf16[128,2048]{1,0:T(8,128)(2,1)S(1)} %collective-permute-done.13.refs_1_) | copy-start | bytes 1572868
  200.5 35.1 %collective-permute-start.18 = (bf16[128,2048]{1,0:T(8,128)(2,1)S(1)}, bf16[128,2048]{1,0:T(8,128)(2,1)S(1)}, u32[]{:S(2)}, u32[]{:S(2)}) collective-permute-start(bf16[128,2048]{1,0:T(8,128)(2,1)S(1)} %collective-permute-done.15.refs_3_), channel_id=1, source_target_pairs={{0,1},{1,2},{2,3},{3,0},{4,5},{5,6},{6,7},{7,4},{8,9},{9,10},{10,1... | collective-permute-start | bytes 1572872 | tf_op jit(solution)/shard_map/ppermute | solution.py:751
  200.5 35.1 %collective-permute-start.17 = (bf16[128,2048]{1,0:T(8,128)(2,1)S(1)}, bf16[128,2048]{1,0:T(8,128)(2,1)S(1)}, u32[]{:S(2)}, u32[]{:S(2)}) collective-permute-start(bf16[128,2048]{1,0:T(8,128)(2,1)S(1)} %collective-permute-done.14.refs_2_), channel_id=1, source_target_pairs={{0,4},{4,0},{1,5},{5,1},{2,6},{6,2},{3,7},{7,3},{8,12},{12,8},{9,1... | collective-permute-start | bytes 1572872 | tf_op jit(solution)/shard_map/ppermute | solution.py:751
  203.9 31.7 %collective-permute-start.16 = (bf16[128,2048]{1,0:T(8,128)(2,1)S(1)}, bf16[128,2048]{1,0:T(8,128)(2,1)S(1)}, u32[]{:S(2)}, u32[]{:S(2)}) collective-permute-start(bf16[128,2048]{1,0:T(8,128)(2,1)S(1)} %collective-permute-done.14.refs_2_), channel_id=1, source_target_pairs={{0,3},{1,0},{2,1},{3,2},{4,7},{5,4},{6,5},{7,6},{8,11},{9,8},{10,9... | collective-permute-start | bytes 1572872 | tf_op jit(solution)/shard_map/ppermute | solution.py:751
  208.9 36.4 %collective-permute-start.23 = (bf16[128,1792]{1,0:T(8,128)(2,1)}, bf16[128,1792]{1,0:T(8,128)(2,1)}, u32[]{:S(2)}, u32[]{:S(2)}) collective-permute-start(bf16[128,1792]{1,0:T(8,128)(2,1)} %slice.34), channel_id=1, source_target_pairs={{0,64},{64,0},{1,65},{65,1},{2,66},{66,2},{3,67},{67,3},{4,68},{68... | collective-permute-start | bytes 1376264 | tf_op jit(solution)/shard_map/ppermute | solution.py:751
  225.9 21.7 %collective-permute-start.22 = (bf16[128,1408]{1,0:T(8,128)(2,1)S(1)}, bf16[128,1408]{1,0:T(8,128)(2,1)S(1)}, u32[]{:S(2)}, u32[]{:S(2)}) collective-permute-start(bf16[128,1408]{1,0:T(8,128)(2,1)S(1)} %slice.33), channel_id=1, source_target_pairs={{0,64},{64,0},{1,65},{65,1},{2,66},{66,2},{3,67},{67,3},{4,68},{68... | collective-permute-start | bytes 1081352 | tf_op jit(solution)/shard_map/ppermute | solution.py:751
  235.6 3.6 %copy-start.3 = (bf16[128,2048]{1,0:T(8,128)(2,1)}, bf16[128,2048]{1,0:T(8,128)(2,1)S(1)}, u32[]{:S(2)}) copy-start(bf16[128,2048]{1,0:T(8,128)(2,1)S(1)} %collective-permute-done.18.refs_6_) | copy-start | bytes 1572868
  235.6 3.5 %copy-start.1 = (bf16[128,2048]{1,0:T(8,128)(2,1)}, bf16[128,2048]{1,0:T(8,128)(2,1)S(1)}, u32[]{:S(2)}) copy-start(bf16[128,2048]{1,0:T(8,128)(2,1)S(1)} %collective-permute-done.17.refs_5_) | copy-start | bytes 1572868
  235.6 3.5 %copy-start.2 = (bf16[128,2048]{1,0:T(8,128)(2,1)}, bf16[128,2048]{1,0:T(8,128)(2,1)S(1)}, u32[]{:S(2)}) copy-start(bf16[128,2048]{1,0:T(8,128)(2,1)S(1)} %collective-permute-done.16.refs_4_) | copy-start | bytes 1572868
  235.7 9.6 %collective-permute-start.20 = (bf16[48,2048]{1,0:T(8,128)(2,1)S(1)}, bf16[48,2048]{1,0:T(8,128)(2,1)S(1)}, u32[]{:S(2)}, u32[]{:S(2)}) collective-permute-start(bf16[48,2048]{1,0:T(8,128)(2,1)S(1)} %slice.31), channel_id=1, source_target_pairs={{0,3},{1,0},{2,1},{3,2},{4,7},{5,4},{6,5},{7,6},{8,11},{9,8},{10,9... | collective-permute-start | bytes 589832 | tf_op jit(solution)/shard_map/ppermute | solution.py:751
  238.2 7.1 %collective-permute-start.19 = (bf16[48,2048]{1,0:T(8,128)(2,1)S(1)}, bf16[48,2048]{1,0:T(8,128)(2,1)S(1)}, u32[]{:S(2)}, u32[]{:S(2)}) collective-permute-start(bf16[48,2048]{1,0:T(8,128)(2,1)S(1)} %slice.30), channel_id=1, source_target_pairs={{0,4},{4,0},{1,5},{5,1},{2,6},{6,2},{3,7},{7,3},{8,12},{12,8},{9,1... | collective-permute-start | bytes 589832 | tf_op jit(solution)/shard_map/ppermute | solution.py:751
  239.1 6.2 %collective-permute-start.21 = (bf16[32,2048]{1,0:T(8,128)(2,1)S(1)}, bf16[32,2048]{1,0:T(8,128)(2,1)S(1)}, u32[]{:S(2)}, u32[]{:S(2)}) collective-permute-start(bf16[32,2048]{1,0:T(8,128)(2,1)S(1)} %slice.32), channel_id=1, source_target_pairs={{0,1},{1,2},{2,3},{3,0},{4,5},{5,6},{6,7},{7,4},{8,9},{9,10},{10,1... | collective-permute-start | bytes 393224 | tf_op jit(solution)/shard_map/ppermute | solution.py:751
  245.3 8.9 %copy-start.18 = (bf16[32,2048]{1,0:T(8,128)(2,1)}, bf16[32,2048]{1,0:T(8,128)(2,1)S(1)}, u32[]{:S(2)}) copy-start(bf16[32,2048]{1,0:T(8,128)(2,1)S(1)} %collective-permute-done.21.refs_2_) | copy-start | bytes 393220
  245.3 8.9 %copy-start.16 = (bf16[48,2048]{1,0:T(8,128)(2,1)}, bf16[48,2048]{1,0:T(8,128)(2,1)S(1)}, u32[]{:S(2)}) copy-start(bf16[48,2048]{1,0:T(8,128)(2,1)S(1)} %collective-permute-done.20.refs_1_) | copy-start | bytes 589828
  245.3 8.9 %copy-start.17 = (bf16[48,2048]{1,0:T(8,128)(2,1)}, bf16[48,2048]{1,0:T(8,128)(2,1)S(1)}, u32[]{:S(2)}) copy-start(bf16[48,2048]{1,0:T(8,128)(2,1)S(1)} %collective-permute-done.19.refs_0_) | copy-start | bytes 589828
  247.7 0.7 copy-start.13
  254.2 2.0 copy-start.21
Sparse Core Ops, SparseCore 0:
  53.7 134.6 all-reduce.1
Sparse Core Ops, SparseCore 1:
  116.7 45.9 reduce-scatter.4
  177.0 47.9 reduce-scatter.2
where the time goes:
time: 265 us; the launch traced here: 264 us
  Pallas kernels  115 us (43%)
  waiting for transfers between devices  79.9 us (30%)
  starting transfers between devices  37.8 us (14%)
  between operations  15.9 us (6%)
  local copies, waits for them, and re-layouts  14.6 us (6%)
    ppermute x24, waiting for transfers between devices, shift(): lax.ppermute(array, axis, [(i, (i + by) % size) for i in range(size)])  63.8 us
    pallas_call x1, Pallas kernels, forward(): kernel_call(forward_kernel, 'forward', [made(slot_len, columns) for colum...  44.3 us
    ppermute x24, starting transfers between devices, shift(): lax.ppermute(array, axis, [(i, (i + by) % size) for i in range(size)])  37.7 us
    pallas_call x2, Pallas kernels, weight_blocks(): kernel_call(weight_kernel, 'weights', made(left.shape[1], width), prefetc...  24.2 us
    pallas_call x1, Pallas kernels, backward(): kernel_call(backward_kernel, 'backward', sums + [made(slot_len, units)] +...  20.4 us
    reduce_scatter x2, waiting for transfers between devices, __init__(): lax.psum_scatter(after(partial_sums, earlier), ('x', 'core'), scatter_dim...  16 us
    pallas_call x1, Pallas kernels, finish_output(): kernel_call(output_kernel, 'output', made(slot_len, width), grid=(slot_le...  6.36 us
    unnamed x53, local copies, waits for them, and re-layouts  6.19 us
  transfers between devices with their start and end apart: 27, of which 10 were waited for; matrix products, arithmetic and copies ran while one was open for 2% of the time, Pallas kernels for 25%

commit v1 on v0

--- a/solution.py
+++ b/solution.py
@@ -897,43 +897,40 @@
     )
     hidden_sum = TensorSum(blocks)
     hidden_sum.send_far()
-    norm_sum, *sums = sums
-    norm_across = across(norm_sum)
-    up_part = weight_blocks(after(order, up_grad), hidden, up_grad, qkv_grad)
-    done = hidden_sum.send_middle((up_part, norm_across))
+    down_part = weight_blocks(after(order, up_grad), grad, activated, context, *sums)
+    done = hidden_sum.send_middle(down_part)
+    down = DataSum(down_part, done)
+    up_part = weight_blocks(after(order, done), hidden, up_grad, qkv_grad)
+    done = hidden_sum.send_near(up_part)
     up = DataSum(up_part, done)
-    norm_sum = norm_sum + norm_across
-    around = [y_up(norm_sum), y_down(norm_sum), shift(norm_sum, "y", 4, 2)]
-    done = hidden_sum.send_near((done, around))
-    norm_sum = norm_sum + around[0] + around[1] + around[2]
-    down_part = weight_blocks(after(order, done), grad, activated, context, norm_sum, *sums)
     rows = input_rows(
-        after(places, down_part), hidden_sum.terms(), tokens, cotangent, stats, ln_gain
-    )
-    down = DataSum(down_part, rows)
+        after(places, done), hidden_sum.terms(), tokens, cotangent, stats, ln_gain
+    )
     input_grad = TensorGather(places, rows)
     done = input_grad.second((rows, branch_sum))
-    up.send(done)
-    down.send(up.near)
-    output = finish_output(after(seq_lengths, down.near), tokens, branch_sum, b_dense, b_fc2)
+    down.send(done)
+    up.send(down.near)
+    output = finish_output(after(seq_lengths, up.near), tokens, branch_sum, b_dense, b_fc2)
     done = input_grad.third(output)
     input_grad.three = after(input_grad.three, done)
-    grad_fc1, grad_qkv = up.finish(
-        up_kernel, "up", ((BLOCK, units), (BLOCK, w_qkv.shape[1])), input_grad.three[0]
-    )
     grad_fc2, grad_dense, small = down.finish(
         down_kernel,
         "down",
         ((units, BLOCK), (w_dense.shape[0], BLOCK), (8, BLOCK)),
-        grad_qkv,
-    )
-    input_grad = input_grad.finish(small)
+        input_grad.three[0],
+    )
+    norm_sum = small[:2] + across(small[:2])
+    grad_fc1, grad_qkv = up.finish(
+        up_kernel, "up", ((BLOCK, units), (BLOCK, w_qkv.shape[1])), small
+    )
+    norm_sum = norm_sum + y_up(norm_sum) + y_down(norm_sum) + shift(norm_sum, "y", 4, 2)
+    input_grad = input_grad.finish(grad_qkv)
     out_bias = small[2]
     return (
         output,
         input_grad,
-        small[0],
-        small[1],
+        norm_sum[0],
+        norm_sum[1],
         grad_qkv,
         small[3, :48],
         grad_dense,

time: 265 us -> 254 us (0.958)
  waiting for transfers between devices: 79.9 us -> 53.5 us
  starting transfers between devices: 37.8 us -> 52.9 us
    reduce_scatter x2, waiting for transfers between devices: 16 us -> 0.01 us  [__init__(): lax.psum_scatter(after(partial_sums, earlier), ('x', 'core'), scatter_dim...]
    ppermute x24, starting transfers between devices: 37.7 us -> 52.8 us  [shift(): lax.ppermute(array, axis, [(i, (i + by) % size) for i in range(size)])]
    ppermute x24, waiting for transfers between devices: 63.8 us -> 53.4 us  [shift(): lax.ppermute(array, axis, [(i, (i + by) % size) for i in range(size)])]
    unnamed x53 -> x57, local copies, waits for them, and re-layouts: 6.19 us -> 6.89 us
  transfers between devices with their start and end apart: 27 -> 27, of which waited for: 10 -> 13; matrix products, arithmetic and copies ran while one was open for 2% -> 3% of each run, Pallas kernels for 25% -> 26%
where the time goes in v1:
time: 254 us; the launch traced here: 253 us
  Pallas kernels  115 us (45%)
  waiting for transfers between devices  53.5 us (21%)
  starting transfers between devices  52.9 us (21%)
  between operations  15.8 us (6%)
  local copies, waits for them, and re-layouts  14.8 us (6%)
    ppermute x24, waiting for transfers between devices, shift(): lax.ppermute(array, axis, [(i, (i + by) % size) for i in range(size)])  53.4 us
    ppermute x24, starting transfers between devices, shift(): lax.ppermute(array, axis, [(i, (i + by) % size) for i in range(size)])  52.8 us
    pallas_call x1, Pallas kernels, forward(): kernel_call(forward_kernel, 'forward', [made(slot_len, columns) for colum...  44.3 us
    pallas_call x2, Pallas kernels, weight_blocks(): kernel_call(weight_kernel, 'weights', made(left.shape[1], width), prefetc...  24.2 us
    pallas_call x1, Pallas kernels, backward(): kernel_call(backward_kernel, 'backward', sums + [made(slot_len, units)] +...  20.4 us
    unnamed x57, local copies, waits for them, and re-layouts  6.89 us
    pallas_call x1, Pallas kernels, finish_output(): kernel_call(output_kernel, 'output', made(slot_len, width), grid=(slot_le...  6.37 us
    pallas_call x2, Pallas kernels, place_rows(): kernel_call(functools.partial(place_kernel, blocks), 'place', made(8 * BL...  5.82 us
  transfers between devices with their start and end apart: 27, of which 13 were waited for; matrix products, arithmetic and copies ran while one was open for 3% of the time, Pallas kernels for 26%

profile of v1, /device:TPU:0, one launch (start us, length us, event | category | flops | bytes accessed | tf_op | source)
XLA Modules:
  0.0 252.9 jit_solution(17045317926331376276)
XLA Ops:
  8.1 0.6 broadcast_in_dim_tile.3.freq_ref
  8.7 0.6 stack.103.places_ref
  9.3 44.3 %forward.1 = (bf16[1024,2048]{1,0:T(8,128)(2,1)}, bf16[1024,2048]{1,0:T(8,128)(2,1)}, bf16[1024,1024]{1,0:T(8,128)(2,1)}, bf16[1024,1024]{1,0:T(8,128)(2,1)}, bf...) custom-call(s32[1,8]{1,0:T(1,128)} %lengths_ref.2, ...), custom_call_target="tpu_custom_call" | custom-call | flops 1 | bytes 1 | tf_op jit(solution)/shard_map/forward/pallas_call | solution.py:392
  53.6 20.4 %backward.1 = (f32[32,128]{1,0:T(8,128)}, f32[16,128]{1,0:T(8,128)}, f32[16,128]{1,0:T(8,128)}, f32[16,128]{1,0:T(8,128)}, bf16[1024,1024]{1,0:T(8,128)(2,1)}, /...) custom-call(s32[8]{0:T(128)} %stack.103.places_ref, ...), custom_call_target="tpu_custom_call" | custom-call | flops 1 | bytes 1 | tf_op jit(solution)/shard_map/backward/pallas_call | solution.py:540
  74.0 2.1 collective-permute-start
  76.1 1.6 collective-permute-start.1
  77.7 1.7 collective-permute-start.2
  79.4 0.6 stack.94.order_ref
  80.0 10.6 %weights.2 = bf16[2048,1408]{1,0:T(8,128)(2,1)} custom-call(s32[16]{0:T(128)} %stack.94.order_ref, bf16[1024,2048]{1,0:T(8,128)(2,1)} %get-tuple-element.73.grad_hbm.refs_0_.refs_1_.refs_2_.refs_3_, bf16[1024,2048]{1,0:T(8,128)(2,1)} %get-tuple-element.73.grad_hbm.refs_0_.refs_1_.refs_2_.refs_3_, ...), custom_call_target="tpu_custom_call" | custom-call | flops 1 | bytes 1 | tf_op jit(solution)/shard_map/weights/pallas_call | solution.py:578
  90.7 0.6 copy-done.20
  91.3 0.1 copy-done.15
  91.4 2.8 %middle.1 = (bf16[128,2048]{1,0:T(8,128)(2,1)}, bf16[128,2048]{1,0:T(8,128)(2,1)}, bf16[128,2048]{1,0:T(8,128)(2,1)}) custom-call(bf16[128,2048]{1,0:T(8,128)(2,1)} %get-tuple-element.77.refs_0_, bf16[48,2048]{1,0:T(8,128)(2,1)} %copy-done.15, bf16[128,2048]{1,0:T(8,128)(2,1)} %get-tuple-element.79.refs_2_, bf16[48,2048]{1,0:T(8,128)(2,1)} %copy-done.16, ...), custom_call_target="tpu_custom_call" | custom-call | flops 1 | bytes 1 | tf_op jit(solution)/shard_map/middle/pallas_call | solution.py:623
  94.3 1.0 copy-done.24
  95.3 13.2 %collective-permute-start.5 = (bf16[128,2048]{1,0:T(8,128)(2,1)S(1)}, bf16[128,2048]{1,0:T(8,128)(2,1)S(1)}, u32[]{:S(2)}, u32[]{:S(2)}) collective-permute-start(bf16[128,2048]{1,0:T(8,128)(2,1)S(1)} %copy-done.24), channel_id=1, source_target_pairs={{0,3},{1,0},{2,1},{3,2},{4,7},{5,4},{6,5},{7,6},{8,11},{9,8},{10,9... | collective-permute-start | bytes 1572872 | tf_op jit(solution)/shard_map/ppermute | solution.py:751
  108.4 7.0 %collective-permute-start.4 = (bf16[128,2048]{1,0:T(8,128)(2,1)S(1)}, bf16[128,2048]{1,0:T(8,128)(2,1)S(1)}, u32[]{:S(2)}, u32[]{:S(2)}) collective-permute-start(bf16[128,2048]{1,0:T(8,128)(2,1)S(1)} %copy-done.22), channel_id=1, source_target_pairs={{0,4},{4,0},{1,5},{5,1},{2,6},{6,2},{3,7},{7,3},{8,12},{12,8},{9,1... | collective-permute-start | bytes 1572872 | tf_op jit(solution)/shard_map/ppermute | solution.py:751
  115.5 13.5 %weights.3 = bf16[2048,1792]{1,0:T(8,128)(2,1)} custom-call(s32[16]{0:T(128)} %stack.94.order_ref, bf16[1024,2048]{1,0:T(8,128)(2,1)} %get-tuple-element.96.refs_0_.refs_1_.refs_2_.refs_3_, bf16[1024,2048]{1,0:T(8,128)(2,1)} %get-tuple-element.96.refs_0_.refs_1_.refs_2_.refs_3_, bf16[1024,2048]{1,0:T(8,128)(2,1)} %get-tuple-element.96.refs_0_.refs_1_.refs_2_.refs_3_, ...), custom_call_target="tpu_custom_call" | custom-call | flops 1 | bytes 1 | tf_op jit(solution)/shard_map/weights/pallas_call | solution.py:578
  129.1 0.7 copy-done.7
  129.8 0.2 copy-done.8
  130.0 0.2 copy-done.9
  130.1 3.0 %near.1 = (bf16[128,2048]{1,0:T(8,128)(2,1)}, bf16[128,2048]{1,0:T(8,128)(2,1)}) custom-call(bf16[128,2048]{1,0:T(8,128)(2,1)} %get-tuple-element.97.refs_0_, bf16[128,2048]{1,0:T(8,128)(2,1)} %copy-done.8, bf16[128,2048]{1,0:T(8,128)(2,1)} %copy-done.9, bf16[128,2048]{1,0:T(8,128)(2,1)} %get-tuple-element.98.refs_3_, bf16[128,2048]{1,0:T(8,128)(2,1)} %copy-done.7), custom_call_target="tpu_custom_call" | custom-call | flops 1 | bytes 1 | tf_op jit(solution)/shard_map/near/pallas_call | solution.py:623
  133.1 1.0 copy-done.21
  134.2 3.3 %collective-permute-start.8 = (bf16[128,2048]{1,0:T(8,128)(2,1)S(1)}, bf16[128,2048]{1,0:T(8,128)(2,1)S(1)}, u32[]{:S(2)}, u32[]{:S(2)}) collective-permute-start(bf16[128,2048]{1,0:T(8,128)(2,1)S(1)} %copy-done.21), channel_id=1, source_target_pairs={{0,3},{1,0},{2,1},{3,2},{4,7},{5,4},{6,5},{7,6},{8,11},{9,8},{10,9... | collective-permute-start | bytes 1572872 | tf_op jit(solution)/shard_map/ppermute | solution.py:751
  137.5 0.1 collective-permute-start.7
  137.6 19.6 %collective-permute-done.8.refs_3_ = bf16[128,2048]{1,0:T(8,128)(2,1)S(1)} collective-permute-done((bf16[128,2048]{1,0:T(8,128)(2,1)S(1)}, bf16[128,2048]{1,0:T(8,128)(2,1)S(1)}, u32[]{:S(2)}, u32[]{:S(2)}) %collective-permute-start.8) | collective-permute-done | bytes 524320 | tf_op jit(solution)/shard_map/ppermute | solution.py:751
  157.2 3.7 %collective-permute-done.6.refs_1_ = bf16[128,2048]{1,0:T(8,128)(2,1)S(1)} collective-permute-done((bf16[128,2048]{1,0:T(8,128)(2,1)S(1)}, bf16[128,2048]{1,0:T(8,128)(2,1)S(1)}, u32[]{:S(2)}, u32[]{:S(2)}) %collective-permute-start.6) | collective-permute-done | bytes 524320 | tf_op jit(solution)/shard_map/ppermute | solution.py:751
  160.9 0.8 copy-done.11
  161.7 0.2 copy-done.12
  161.8 4.1 %input.1.refs_0_ = bf16[128,2048]{1,0:T(8,128)(2,1)} custom-call(s32[8]{0:T(128)} %stack.103.places_ref, bf16[128,2048]{1,0:T(8,128)(2,1)} %get-tuple-element.105.refs_0_, bf16[128,2048]{1,0:T(8,128)(2,1)} %copy-done.11, bf16[128,2048]{1,0:T(8,128)(2,1)} %copy-done.12, bf16[128,2048]{1,0:T(8,128)(2,1)} %copy-done.10, bf16[1024,2048]{1,0:T(8,128)(2,1)} %tokens_ref.1, ...), custom_call_target="tpu_custom_call" | custom-call | flops 1 | bytes 1 | tf_op jit(solution)/shard_map/input/pallas_call | solution.py:683
  166.0 9.2 %collective-permute-start.10 = (bf16[128,2048]{1,0:T(8,128)(2,1)}, bf16[128,2048]{1,0:T(8,128)(2,1)S(1)}, u32[]{:S(2)}, u32[]{:S(2)}) collective-permute-start(bf16[128,2048]{1,0:T(8,128)(2,1)} %input.1.refs_0_), channel_id=1, source_target_pairs={{0,3},{1,0},{2,1},{3,2},{4,7},{5,4},{6,5},{7,6},{8,11},{9,8},{10,9... | collective-permute-start | bytes 1572872 | tf_op jit(solution)/shard_map/ppermute | solution.py:751
  175.1 20.0 %collective-permute-done.11.refs_3_ = bf16[128,2048]{1,0:T(8,128)(2,1)S(1)} collective-permute-done((bf16[128,2048]{1,0:T(8,128)(2,1)}, bf16[128,2048]{1,0:T(8,128)(2,1)S(1)}, u32[]{:S(2)}, u32[]{:S(2)}) %collective-permute-start.11) | collective-permute-done | bytes 524320 | tf_op jit(solution)/shard_map/ppermute | solution.py:751
  195.1 0.6 collective-permute-done.9.refs_1_
  195.7 1.4 collective-permute-start.13
  197.1 3.2 %collective-permute-start.12 = (bf16[128,2048]{1,0:T(8,128)(2,1)S(1)}, bf16[128,2048]{1,0:T(8,128)(2,1)S(1)}, u32[]{:S(2)}, u32[]{:S(2)}) collective-permute-start(bf16[128,2048]{1,0:T(8,128)(2,1)S(1)} %collective-permute-done.10.refs_2_), channel_id=1, source_target_pairs={{0,3},{1,0},{2,1},{3,2},{4,7},{5,4},{6,5},{7,6},{8,11},{9,8},{10,9... | collective-permute-start | bytes 1572872 | tf_op jit(solution)/shard_map/ppermute | solution.py:751
  200.4 1.7 slice.38
  202.1 6.4 %output.1 = bf16[1024,2048]{1,0:T(8,128)(2,1)} custom-call(s32[1,8]{1,0:T(1,128)} %lengths_ref.2, bf16[1024,2048]{1,0:T(8,128)(2,1)} %tokens_ref.1, bf16[1024,2048]{1,0:T(8,128)(2,1)} %all-reduce.2.cloned.1.call-done.branch_ref, bf16[2048]{0:T(1024)(128)(2,1)} %b_dense_ref.1, bf16[2048]{0:T(1024)(128)(2,1)} %b_fc2_ref.1), custom_call_target="tpu_custom_call" | custom-call | flops 1 | bytes 1 | tf_op jit(solution)/shard_map/output/pallas_call | solution.py:650
  208.5 1.7 collective-permute-done.14.refs_6_
  210.2 0.4 collective-permute-done.13.refs_5_
  210.7 0.6 collective-permute-done.12.refs_4_
  211.3 3.8 %collective-permute-start.16 = (bf16[48,2048]{1,0:T(8,128)(2,1)S(1)}, bf16[48,2048]{1,0:T(8,128)(2,1)S(1)}, u32[]{:S(2)}, u32[]{:S(2)}) collective-permute-start(bf16[48,2048]{1,0:T(8,128)(2,1)S(1)} %slice.35), channel_id=1, source_target_pairs={{0,3},{1,0},{2,1},{3,2},{4,7},{5,4},{6,5},{7,6},{8,11},{9,8},{10,9... | collective-permute-start | bytes 589832 | tf_op jit(solution)/shard_map/ppermute | solution.py:751
  215.0 0.3 collective-permute-start.15
  215.3 0.1 collective-permute-start.17
  215.5 3.9 %place.2.refs_3_ = bf16[1024,2048]{1,0:T(8,128)(2,1)} custom-call(s32[8]{0:T(128)} %stack.103.places_ref, bf16[128,2048]{1,0:T(8,128)(2,1)} %input.1.refs_0_, bf16[128,2048]{1,0:T(8,128)(2,1)} %copy-done.6, bf16[128,2048]{1,0:T(8,128)(2,1)} %copy-done.5, bf16[128,2048]{1,0:T(8,128)(2,1)} %copy-done.4, bf16[128,2048]{1,0:T(8,128)(2,1)} %copy-done.2, ...), custom_call_target="tpu_custom_call" | custom-call | flops 1 | bytes 1 | tf_op jit(solution)/shard_map/place/pallas_call | solution.py:713
  219.4 0.5 collective-permute-start.18
  219.9 1.7 collective-permute-done.17.refs_2_
  221.6 0.7 collective-permute-done.15.refs_0_
  222.3 0.8 copy-done.14
  223.1 2.1 down.1
  225.2 0.7 slice_bitcast_fusion.1
  225.9 0.7 slice.39
  226.6 1.6 collective-permute-start.20
  228.1 1.2 slice_bitcast_fusion
  229.3 1.7 collective-permute-done.20
  231.1 0.7 slice_add_fusion
  231.8 1.5 collective-permute-start.23
  233.2 1.5 collective-permute-start.22
  234.8 0.8 collective-permute-start.21
  235.6 1.2 slice_bitcast_fusion.2
  236.8 0.3 collective-permute-done.22
  237.1 2.4 collective-permute-done.21
  239.5 0.5 slice_bitcast_fusion.3
  240.1 0.8 copy-done.13
  240.8 2.1 up.1
  243.0 1.9 place.3
  244.9 0.5 copy.29
  (79 shorter events, 0.5 us)
Async XLA Ops:
  8.0 187.7 %all-reduce.2.cloned.1.call-start = ((), (), s32[]{:S(2)}) async-start(), calls=%async_computation.4 | async-start | bytes 8388608 | tf_op jit(solution)/shard_map/psum | solution.py:894
  53.6 146.8 %reduce-scatter.5.cloned.1.call-start = ((), (), s32[]{:S(2)}) async-start(), calls=%async_computation.3 | async-start | bytes 6488064 | tf_op jit(solution)/shard_map/reduce_scatter | solution.py:838
  74.0 16.6 %collective-permute-start = (bf16[48,2048]{1,0:T(8,128)(2,1)}, bf16[48,2048]{1,0:T(8,128)(2,1)S(1)}, u32[]{:S(2)}, u32[]{:S(2)}) collective-permute-start(bf16[48,2048]{1,0:T(8,128)(2,1)} %get-tuple-element.78), channel_id=1, source_target_pairs={{0,4},{4,0},{1,5},{5,1},{2,6},{6,2},{3,7},{7,3},{8,12},{12,8},{9,1... | collective-permute-start | bytes 589832 | tf_op jit(solution)/shard_map/ppermute | solution.py:751
  76.1 14.6 %collective-permute-start.1 = (bf16[48,2048]{1,0:T(8,128)(2,1)}, bf16[48,2048]{1,0:T(8,128)(2,1)S(1)}, u32[]{:S(2)}, u32[]{:S(2)}) collective-permute-start(bf16[48,2048]{1,0:T(8,128)(2,1)} %get-tuple-element.80), channel_id=1, source_target_pairs={{0,1},{1,2},{2,3},{3,0},{4,5},{5,6},{6,7},{7,4},{8,9},{9,10},{10,1... | collective-permute-start | bytes 589832 | tf_op jit(solution)/shard_map/ppermute | solution.py:751
  77.7 12.9 %collective-permute-start.2 = (bf16[32,2048]{1,0:T(8,128)(2,1)}, bf16[32,2048]{1,0:T(8,128)(2,1)S(1)}, u32[]{:S(2)}, u32[]{:S(2)}) collective-permute-start(bf16[32,2048]{1,0:T(8,128)(2,1)} %get-tuple-element.82), channel_id=1, source_target_pairs={{0,3},{1,0},{2,1},{3,2},{4,7},{5,4},{6,5},{7,6},{8,11},{9,8},{10,9... | collective-permute-start | bytes 393224 | tf_op jit(solution)/shard_map/ppermute | solution.py:751
  90.6 0.7 copy-start.20
  90.7 0.7 copy-start.15
  90.7 0.7 copy-start.16
  94.2 1.0 copy-start.24
  94.2 14.2 %copy-start.23 = (bf16[128,2048]{1,0:T(8,128)(2,1)S(1)}, bf16[128,2048]{1,0:T(8,128)(2,1)}, u32[]{:S(2)}) copy-start(bf16[128,2048]{1,0:T(8,128)(2,1)} %get-tuple-element.92) | copy-start | bytes 1572868
  94.2 14.2 %copy-start.22 = (bf16[128,2048]{1,0:T(8,128)(2,1)S(1)}, bf16[128,2048]{1,0:T(8,128)(2,1)}, u32[]{:S(2)}) copy-start(bf16[128,2048]{1,0:T(8,128)(2,1)} %get-tuple-element.93) | copy-start | bytes 1572868
  94.2 107.9 %reduce-scatter.3.cloned.1.call-start = ((), (), s32[]{:S(2)}) async-start(), calls=%async_computation.2 | async-start | bytes 8257536 | tf_op jit(solution)/shard_map/reduce_scatter | solution.py:838
  95.3 33.7 %collective-permute-start.5 = (bf16[128,2048]{1,0:T(8,128)(2,1)S(1)}, bf16[128,2048]{1,0:T(8,128)(2,1)S(1)}, u32[]{:S(2)}, u32[]{:S(2)}) collective-permute-start(bf16[128,2048]{1,0:T(8,128)(2,1)S(1)} %copy-done.24), channel_id=1, source_target_pairs={{0,3},{1,0},{2,1},{3,2},{4,7},{5,4},{6,5},{7,6},{8,11},{9,8},{10,9... | collective-permute-start | bytes 1572872 | tf_op jit(solution)/shard_map/ppermute | solution.py:751
  108.4 20.6 %collective-permute-start.3 = (bf16[128,2048]{1,0:T(8,128)(2,1)S(1)}, bf16[128,2048]{1,0:T(8,128)(2,1)S(1)}, u32[]{:S(2)}, u32[]{:S(2)}) collective-permute-start(bf16[128,2048]{1,0:T(8,128)(2,1)S(1)} %copy-done.23), channel_id=1, source_target_pairs={{0,1},{1,2},{2,3},{3,0},{4,5},{5,6},{6,7},{7,4},{8,9},{9,10},{10,1... | collective-permute-start | bytes 1572872 | tf_op jit(solution)/shard_map/ppermute | solution.py:751
  108.4 20.6 %collective-permute-start.4 = (bf16[128,2048]{1,0:T(8,128)(2,1)S(1)}, bf16[128,2048]{1,0:T(8,128)(2,1)S(1)}, u32[]{:S(2)}, u32[]{:S(2)}) collective-permute-start(bf16[128,2048]{1,0:T(8,128)(2,1)S(1)} %copy-done.22), channel_id=1, source_target_pairs={{0,4},{4,0},{1,5},{5,1},{2,6},{6,2},{3,7},{7,3},{8,12},{12,8},{9,1... | collective-permute-start | bytes 1572872 | tf_op jit(solution)/shard_map/ppermute | solution.py:751
  129.0 0.8 copy-start.7
  129.0 0.9 copy-start.8
  129.0 1.1 copy-start.9
  133.1 1.1 copy-start.21
  133.1 4.4 %copy-start.26 = (bf16[128,2048]{1,0:T(8,128)(2,1)S(1)}, bf16[128,2048]{1,0:T(8,128)(2,1)}, u32[]{:S(2)}) copy-start(bf16[128,2048]{1,0:T(8,128)(2,1)} %get-tuple-element.100) | copy-start | bytes 1572868
  133.1 4.4 %copy-start.25 = (bf16[128,2048]{1,0:T(8,128)(2,1)S(1)}, bf16[128,2048]{1,0:T(8,128)(2,1)}, u32[]{:S(2)}) copy-start(bf16[128,2048]{1,0:T(8,128)(2,1)} %get-tuple-element.101) | copy-start | bytes 1572868
  134.2 23.0 %collective-permute-start.8 = (bf16[128,2048]{1,0:T(8,128)(2,1)S(1)}, bf16[128,2048]{1,0:T(8,128)(2,1)S(1)}, u32[]{:S(2)}, u32[]{:S(2)}) collective-permute-start(bf16[128,2048]{1,0:T(8,128)(2,1)S(1)} %copy-done.21), channel_id=1, source_target_pairs={{0,3},{1,0},{2,1},{3,2},{4,7},{5,4},{6,5},{7,6},{8,11},{9,8},{10,9... | collective-permute-start | bytes 1572872 | tf_op jit(solution)/shard_map/ppermute | solution.py:751
  137.5 23.3 %collective-permute-start.6 = (bf16[128,2048]{1,0:T(8,128)(2,1)S(1)}, bf16[128,2048]{1,0:T(8,128)(2,1)S(1)}, u32[]{:S(2)}, u32[]{:S(2)}) collective-permute-start(bf16[128,2048]{1,0:T(8,128)(2,1)S(1)} %copy-done.26), channel_id=1, source_target_pairs={{0,1},{1,2},{2,3},{3,0},{4,5},{5,6},{6,7},{7,4},{8,9},{9,10},{10,1... | collective-permute-start | bytes 1572872 | tf_op jit(solution)/shard_map/ppermute | solution.py:751
  137.5 23.3 %collective-permute-start.7 = (bf16[128,2048]{1,0:T(8,128)(2,1)S(1)}, bf16[128,2048]{1,0:T(8,128)(2,1)S(1)}, u32[]{:S(2)}, u32[]{:S(2)}) collective-permute-start(bf16[128,2048]{1,0:T(8,128)(2,1)S(1)} %copy-done.25), channel_id=1, source_target_pairs={{0,4},{4,0},{1,5},{5,1},{2,6},{6,2},{3,7},{7,3},{8,12},{12,8},{9,1... | collective-permute-start | bytes 1572872 | tf_op jit(solution)/shard_map/ppermute | solution.py:751
  157.2 3.7 %copy-start.10 = (bf16[128,2048]{1,0:T(8,128)(2,1)}, bf16[128,2048]{1,0:T(8,128)(2,1)S(1)}, u32[]{:S(2)}) copy-start(bf16[128,2048]{1,0:T(8,128)(2,1)S(1)} %collective-permute-done.8.refs_3_) | copy-start | bytes 1572868
  160.9 0.8 copy-start.11
  160.9 1.0 copy-start.12
  165.9 29.2 %collective-permute-start.11 = (bf16[128,2048]{1,0:T(8,128)(2,1)}, bf16[128,2048]{1,0:T(8,128)(2,1)S(1)}, u32[]{:S(2)}, u32[]{:S(2)}) collective-permute-start(bf16[128,2048]{1,0:T(8,128)(2,1)} %input.1.refs_0_), channel_id=1, source_target_pairs={{0,4},{4,0},{1,5},{5,1},{2,6},{6,2},{3,7},{7,3},{8,12},{12,8},{9,1... | collective-permute-start | bytes 1572872 | tf_op jit(solution)/shard_map/ppermute | solution.py:751
  166.0 29.2 %collective-permute-start.10 = (bf16[128,2048]{1,0:T(8,128)(2,1)}, bf16[128,2048]{1,0:T(8,128)(2,1)S(1)}, u32[]{:S(2)}, u32[]{:S(2)}) collective-permute-start(bf16[128,2048]{1,0:T(8,128)(2,1)} %input.1.refs_0_), channel_id=1, source_target_pairs={{0,3},{1,0},{2,1},{3,2},{4,7},{5,4},{6,5},{7,6},{8,11},{9,8},{10,9... | collective-permute-start | bytes 1572872 | tf_op jit(solution)/shard_map/ppermute | solution.py:751
  175.1 20.6 %collective-permute-start.9 = (bf16[128,2048]{1,0:T(8,128)(2,1)}, bf16[128,2048]{1,0:T(8,128)(2,1)S(1)}, u32[]{:S(2)}, u32[]{:S(2)}) collective-permute-start(bf16[128,2048]{1,0:T(8,128)(2,1)} %input.1.refs_0_), channel_id=1, source_target_pairs={{0,1},{1,2},{2,3},{3,0},{4,5},{5,6},{6,7},{7,4},{8,9},{9,10},{10,1... | collective-permute-start | bytes 1572872 | tf_op jit(solution)/shard_map/ppermute | solution.py:751
  195.1 13.4 %copy-start.4 = (bf16[128,2048]{1,0:T(8,128)(2,1)}, bf16[128,2048]{1,0:T(8,128)(2,1)S(1)}, u32[]{:S(2)}) copy-start(bf16[128,2048]{1,0:T(8,128)(2,1)S(1)} %collective-permute-done.11.refs_3_) | copy-start | bytes 1572868
  195.1 13.4 %copy-start.5 = (bf16[128,2048]{1,0:T(8,128)(2,1)}, bf16[128,2048]{1,0:T(8,128)(2,1)S(1)}, u32[]{:S(2)}) copy-start(bf16[128,2048]{1,0:T(8,128)(2,1)S(1)} %collective-permute-done.10.refs_2_) | copy-start | bytes 1572868
  195.7 12.8 %copy-start.6 = (bf16[128,2048]{1,0:T(8,128)(2,1)}, bf16[128,2048]{1,0:T(8,128)(2,1)S(1)}, u32[]{:S(2)}) copy-start(bf16[128,2048]{1,0:T(8,128)(2,1)S(1)} %collective-permute-done.9.refs_1_) | copy-start | bytes 1572868
  195.7 14.5 %collective-permute-start.14 = (bf16[128,2048]{1,0:T(8,128)(2,1)S(1)}, bf16[128,2048]{1,0:T(8,128)(2,1)S(1)}, u32[]{:S(2)}, u32[]{:S(2)}) collective-permute-start(bf16[128,2048]{1,0:T(8,128)(2,1)S(1)} %collective-permute-done.11.refs_3_), channel_id=1, source_target_pairs={{0,1},{1,2},{2,3},{3,0},{4,5},{5,6},{6,7},{7,4},{8,9},{9,10},{10,1... | collective-permute-start | bytes 1572872 | tf_op jit(solution)/shard_map/ppermute | solution.py:751
  195.7 14.9 %collective-permute-start.13 = (bf16[128,2048]{1,0:T(8,128)(2,1)S(1)}, bf16[128,2048]{1,0:T(8,128)(2,1)S(1)}, u32[]{:S(2)}, u32[]{:S(2)}) collective-permute-start(bf16[128,2048]{1,0:T(8,128)(2,1)S(1)} %collective-permute-done.10.refs_2_), channel_id=1, source_target_pairs={{0,4},{4,0},{1,5},{5,1},{2,6},{6,2},{3,7},{7,3},{8,12},{12,8},{9,1... | collective-permute-start | bytes 1572872 | tf_op jit(solution)/shard_map/ppermute | solution.py:751
  197.1 14.1 %collective-permute-start.12 = (bf16[128,2048]{1,0:T(8,128)(2,1)S(1)}, bf16[128,2048]{1,0:T(8,128)(2,1)S(1)}, u32[]{:S(2)}, u32[]{:S(2)}) collective-permute-start(bf16[128,2048]{1,0:T(8,128)(2,1)S(1)} %collective-permute-done.10.refs_2_), channel_id=1, source_target_pairs={{0,3},{1,0},{2,1},{3,2},{4,7},{5,4},{6,5},{7,6},{8,11},{9,8},{10,9... | collective-permute-start | bytes 1572872 | tf_op jit(solution)/shard_map/ppermute | solution.py:751
  202.1 20.2 %collective-permute-start.19 = (bf16[128,1408]{1,0:T(8,128)(2,1)}, bf16[128,1408]{1,0:T(8,128)(2,1)S(1)}, u32[]{:S(2)}, u32[]{:S(2)}) collective-permute-start(bf16[128,1408]{1,0:T(8,128)(2,1)} %slice.38), channel_id=1, source_target_pairs={{0,64},{64,0},{1,65},{65,1},{2,66},{66,2},{3,67},{67,3},{4,68},{68... | collective-permute-start | bytes 1081352 | tf_op jit(solution)/shard_map/ppermute | solution.py:751
  210.2 5.2 %copy-start.3 = (bf16[128,2048]{1,0:T(8,128)(2,1)}, bf16[128,2048]{1,0:T(8,128)(2,1)S(1)}, u32[]{:S(2)}) copy-start(bf16[128,2048]{1,0:T(8,128)(2,1)S(1)} %collective-permute-done.14.refs_6_) | copy-start | bytes 1572868
  210.6 4.8 %copy-start.1 = (bf16[128,2048]{1,0:T(8,128)(2,1)}, bf16[128,2048]{1,0:T(8,128)(2,1)S(1)}, u32[]{:S(2)}) copy-start(bf16[128,2048]{1,0:T(8,128)(2,1)S(1)} %collective-permute-done.13.refs_5_) | copy-start | bytes 1572868
  211.2 4.2 %copy-start.2 = (bf16[128,2048]{1,0:T(8,128)(2,1)}, bf16[128,2048]{1,0:T(8,128)(2,1)S(1)}, u32[]{:S(2)}) copy-start(bf16[128,2048]{1,0:T(8,128)(2,1)S(1)} %collective-permute-done.12.refs_4_) | copy-start | bytes 1572868
  211.2 8.1 %copy-start = (bf16[256,1792]{1,0:T(8,128)(2,1)S(1)}, bf16[256,1792]{1,0:T(8,128)(2,1)}, u32[]{:S(2)}) copy-start(bf16[256,1792]{1,0:T(8,128)(2,1)} %reduce-scatter.3.cloned.1.call-done.near_ref) | copy-start | bytes 2752516
  211.3 10.3 %collective-permute-start.16 = (bf16[48,2048]{1,0:T(8,128)(2,1)S(1)}, bf16[48,2048]{1,0:T(8,128)(2,1)S(1)}, u32[]{:S(2)}, u32[]{:S(2)}) collective-permute-start(bf16[48,2048]{1,0:T(8,128)(2,1)S(1)} %slice.35), channel_id=1, source_target_pairs={{0,3},{1,0},{2,1},{3,2},{4,7},{5,4},{6,5},{7,6},{8,11},{9,8},{10,9... | collective-permute-start | bytes 589832 | tf_op jit(solution)/shard_map/ppermute | solution.py:751
  215.0 7.3 %collective-permute-start.15 = (bf16[48,2048]{1,0:T(8,128)(2,1)S(1)}, bf16[48,2048]{1,0:T(8,128)(2,1)S(1)}, u32[]{:S(2)}, u32[]{:S(2)}) collective-permute-start(bf16[48,2048]{1,0:T(8,128)(2,1)S(1)} %slice.34), channel_id=1, source_target_pairs={{0,4},{4,0},{1,5},{5,1},{2,6},{6,2},{3,7},{7,3},{8,12},{12,8},{9,1... | collective-permute-start | bytes 589832 | tf_op jit(solution)/shard_map/ppermute | solution.py:751
  215.3 6.2 %collective-permute-start.17 = (bf16[32,2048]{1,0:T(8,128)(2,1)S(1)}, bf16[32,2048]{1,0:T(8,128)(2,1)S(1)}, u32[]{:S(2)}, u32[]{:S(2)}) collective-permute-start(bf16[32,2048]{1,0:T(8,128)(2,1)S(1)} %slice.36), channel_id=1, source_target_pairs={{0,1},{1,2},{2,3},{3,0},{4,5},{5,6},{6,7},{7,4},{8,9},{9,10},{10,1... | collective-permute-start | bytes 393224 | tf_op jit(solution)/shard_map/ppermute | solution.py:751
  219.4 20.7 %collective-permute-start.18 = (bf16[128,1792]{1,0:T(8,128)(2,1)S(1)}, bf16[128,1792]{1,0:T(8,128)(2,1)S(1)}, u32[]{:S(2)}, u32[]{:S(2)}) collective-permute-start(bf16[128,1792]{1,0:T(8,128)(2,1)S(1)} %slice.37), channel_id=1, source_target_pairs={{0,64},{64,0},{1,65},{65,1},{2,66},{66,2},{3,67},{67,3},{4,68},{68... | collective-permute-start | bytes 1376264 | tf_op jit(solution)/shard_map/ppermute | solution.py:751
  221.6 21.4 %copy-start.19 = (bf16[32,2048]{1,0:T(8,128)(2,1)}, bf16[32,2048]{1,0:T(8,128)(2,1)S(1)}, u32[]{:S(2)}) copy-start(bf16[32,2048]{1,0:T(8,128)(2,1)S(1)} %collective-permute-done.17.refs_2_) | copy-start | bytes 393220
  221.6 21.4 %copy-start.17 = (bf16[48,2048]{1,0:T(8,128)(2,1)}, bf16[48,2048]{1,0:T(8,128)(2,1)S(1)}, u32[]{:S(2)}) copy-start(bf16[48,2048]{1,0:T(8,128)(2,1)S(1)} %collective-permute-done.16.refs_1_) | copy-start | bytes 589828
  222.3 20.7 %copy-start.18 = (bf16[48,2048]{1,0:T(8,128)(2,1)}, bf16[48,2048]{1,0:T(8,128)(2,1)S(1)}, u32[]{:S(2)}) copy-start(bf16[48,2048]{1,0:T(8,128)(2,1)S(1)} %collective-permute-done.15.refs_0_) | copy-start | bytes 589828
  222.3 0.8 copy-start.14
  225.9 19.0 %copy-start.27 = (f32[128]{0:T(128)}, f32[128]{0:T(128)S(1)}, u32[]{:S(2)}) copy-start(f32[128]{0:T(128)S(1)} %slice_bitcast_fusion.1) | copy-start | bytes 1540
  226.6 4.5 %collective-permute-start.20 = (f32[2,128]{1,0:T(2,128)S(1)}, f32[2,128]{1,0:T(2,128)S(1)}, u32[]{:S(2)}, u32[]{:S(2)}) collective-permute-start(f32[2,128]{1,0:T(2,128)S(1)} %slice.39), channel_id=1, source_target_pairs={{0,4},{4,0},{1,5},{5,1},{2,6},{6,2},{3,7},{7,3},{8,12},{12,8},{9,1... | collective-permute-start | bytes 3080 | tf_op jit(solution)/shard_map/ppermute | solution.py:751
  231.8 5.1 %collective-permute-start.23 = (f32[2,128]{1,0:T(2,128)S(1)}, f32[2,128]{1,0:T(2,128)S(1)}, u32[]{:S(2)}, u32[]{:S(2)}) collective-permute-start(f32[2,128]{1,0:T(2,128)S(1)} %slice_add_fusion), channel_id=1, source_target_pairs={{0,2},{1,3},{2,0},{3,1},{4,6},{5,7},{6,4},{7,5},{8,10},{9,11},{10,... | collective-permute-start | bytes 3080 | tf_op jit(solution)/shard_map/ppermute | solution.py:751
  233.2 3.9 %collective-permute-start.22 = (f32[2,128]{1,0:T(2,128)S(1)}, f32[2,128]{1,0:T(2,128)S(1)}, u32[]{:S(2)}, u32[]{:S(2)}) collective-permute-start(f32[2,128]{1,0:T(2,128)S(1)} %slice_add_fusion), channel_id=1, source_target_pairs={{0,3},{1,0},{2,1},{3,2},{4,7},{5,4},{6,5},{7,6},{8,11},{9,8},{10,9... | collective-permute-start | bytes 3080 | tf_op jit(solution)/shard_map/ppermute | solution.py:751
  234.8 4.8 %collective-permute-start.21 = (f32[2,128]{1,0:T(2,128)S(1)}, f32[2,128]{1,0:T(2,128)S(1)}, u32[]{:S(2)}, u32[]{:S(2)}) collective-permute-start(f32[2,128]{1,0:T(2,128)S(1)} %slice_add_fusion), channel_id=1, source_target_pairs={{0,1},{1,2},{2,3},{3,0},{4,5},{5,6},{6,7},{7,4},{8,9},{9,10},{10,1... | collective-permute-start | bytes 3080 | tf_op jit(solution)/shard_map/ppermute | solution.py:751
  240.1 0.8 copy-start.13
Sparse Core Ops, SparseCore 0:
  53.7 141.3 all-reduce.1
Sparse Core Ops, SparseCore 1:
  94.3 56.5 reduce-scatter.4
  153.1 47.0 reduce-scatter.2

commit v2 on v1

--- a/solution.py
+++ b/solution.py
@@ -907,21 +907,24 @@
         after(places, done), hidden_sum.terms(), tokens, cotangent, stats, ln_gain
     )
     input_grad = TensorGather(places, rows)
-    done = input_grad.second((rows, branch_sum))
-    down.send(done)
-    up.send(down.near)
-    output = finish_output(after(seq_lengths, up.near), tokens, branch_sum, b_dense, b_fc2)
-    done = input_grad.third(output)
-    input_grad.three = after(input_grad.three, done)
+    down.send((rows, branch_sum))
+    done = input_grad.second(down.near)
     grad_fc2, grad_dense, small = down.finish(
         down_kernel,
         "down",
         ((units, BLOCK), (w_dense.shape[0], BLOCK), (8, BLOCK)),
-        input_grad.three[0],
-    )
-    norm_sum = small[:2] + across(small[:2])
+        done,
+    )
+    norm_sum = small[:2]
+    norm_across = across(norm_sum)
+    output = finish_output(after(seq_lengths, small), tokens, branch_sum, b_dense, b_fc2)
+    up.send(output)
+    input_grad.third((output, up.near))
+    *three, up.far = after([*input_grad.three, up.far], input_grad.whole)
+    input_grad.three = three
+    norm_sum = norm_sum + after(norm_across, three[0])
     grad_fc1, grad_qkv = up.finish(
-        up_kernel, "up", ((BLOCK, units), (BLOCK, w_qkv.shape[1])), small
+        up_kernel, "up", ((BLOCK, units), (BLOCK, w_qkv.shape[1])), input_grad.three[0]
     )
     norm_sum = norm_sum + y_up(norm_sum) + y_down(norm_sum) + shift(norm_sum, "y", 4, 2)
     input_grad = input_grad.finish(grad_qkv)

time: 254 us -> 251 us (0.988)
  local copies, waits for them, and re-layouts: 14.8 us -> 11.6 us
    psum x1, waiting for transfers between devices: 0.01 us -> 20 us  [per_device(): branch_sum = lax.psum(branch_part, TENSOR)]
    ppermute x24, waiting for transfers between devices: 53.4 us -> 35.3 us  [shift(): lax.ppermute(array, axis, [(i, (i + by) % size) for i in range(size)])]
  transfers between devices with their start and end apart: 27 -> 27, of which waited for: 13 -> 5; matrix products, arithmetic and copies ran while one was open for 3% -> 2% of each run, Pallas kernels for 26% -> 28%
where the time goes in v2:
time: 251 us; the launch traced here: 250 us
  Pallas kernels  115 us (46%)
  waiting for transfers between devices  55.3 us (22%)
  starting transfers between devices  52.3 us (21%)
  between operations  16 us (6%)
  local copies, waits for them, and re-layouts  11.6 us (5%)
    ppermute x24, starting transfers between devices, shift(): lax.ppermute(array, axis, [(i, (i + by) % size) for i in range(size)])  52.2 us
    pallas_call x1, Pallas kernels, forward(): kernel_call(forward_kernel, 'forward', [made(slot_len, columns) for colum...  44.3 us
    ppermute x24, waiting for transfers between devices, shift(): lax.ppermute(array, axis, [(i, (i + by) % size) for i in range(size)])  35.3 us
    pallas_call x2, Pallas kernels, weight_blocks(): kernel_call(weight_kernel, 'weights', made(left.shape[1], width), prefetc...  24.2 us
    pallas_call x1, Pallas kernels, backward(): kernel_call(backward_kernel, 'backward', sums + [made(slot_len, units)] +...  20.4 us
    psum x1, waiting for transfers between devices, per_device(): branch_sum = lax.psum(branch_part, TENSOR)  20 us
    pallas_call x1, Pallas kernels, finish_output(): kernel_call(output_kernel, 'output', made(slot_len, width), grid=(slot_le...  6.37 us
    unnamed x57, local copies, waits for them, and re-layouts  6.1 us
  transfers between devices with their start and end apart: 27, of which 5 were waited for; matrix products, arithmetic and copies ran while one was open for 2% of the time, Pallas kernels for 28%

profile of v2, /device:TPU:0, one launch (start us, length us, event | category | flops | bytes accessed | tf_op | source)
XLA Modules:
  0.0 250.3 jit_solution(8466653083978663855)
XLA Ops:
  8.0 0.0 all-reduce.2.cloned.1.call-start
  8.1 0.6 broadcast_in_dim_tile.3.freq_ref
  8.7 0.6 stack.103.places_ref
  9.3 44.3 %forward.1 = (bf16[1024,2048]{1,0:T(8,128)(2,1)}, bf16[1024,2048]{1,0:T(8,128)(2,1)}, bf16[1024,1024]{1,0:T(8,128)(2,1)}, bf16[1024,1024]{1,0:T(8,128)(2,1)}, bf...) custom-call(s32[1,8]{1,0:T(1,128)} %lengths_ref.2, ...), custom_call_target="tpu_custom_call" | custom-call | flops 1 | bytes 1 | tf_op jit(solution)/shard_map/forward/pallas_call | solution.py:392
  53.6 0.0 all-reduce.2.cloned.1.call-update
  53.6 0.0 reduce-scatter.3.cloned.1.call-start
  53.6 20.4 %backward.1 = (f32[32,128]{1,0:T(8,128)}, f32[16,128]{1,0:T(8,128)}, f32[16,128]{1,0:T(8,128)}, f32[16,128]{1,0:T(8,128)}, bf16[1024,1024]{1,0:T(8,128)(2,1)}, /...) custom-call(s32[8]{0:T(128)} %stack.103.places_ref, ...), custom_call_target="tpu_custom_call" | custom-call | flops 1 | bytes 1 | tf_op jit(solution)/shard_map/backward/pallas_call | solution.py:540
  74.0 2.1 collective-permute-start
  76.1 1.6 collective-permute-start.1
  77.7 1.7 collective-permute-start.2
  79.4 0.6 stack.94.order_ref
  80.0 10.6 %weights.2 = bf16[2048,1408]{1,0:T(8,128)(2,1)} custom-call(s32[16]{0:T(128)} %stack.94.order_ref, bf16[1024,2048]{1,0:T(8,128)(2,1)} %get-tuple-element.75.grad_hbm.refs_0_.refs_1_.refs_2_.refs_3_, bf16[1024,2048]{1,0:T(8,128)(2,1)} %get-tuple-element.75.grad_hbm.refs_0_.refs_1_.refs_2_.refs_3_, ...), custom_call_target="tpu_custom_call" | custom-call | flops 1 | bytes 1 | tf_op jit(solution)/shard_map/weights/pallas_call | solution.py:578
  90.7 0.6 copy-done.19
  91.3 0.1 copy-done.14
  91.4 0.1 copy-done.15
  91.4 2.8 %middle.1 = (bf16[128,2048]{1,0:T(8,128)(2,1)}, bf16[128,2048]{1,0:T(8,128)(2,1)}, bf16[128,2048]{1,0:T(8,128)(2,1)}) custom-call(bf16[128,2048]{1,0:T(8,128)(2,1)} %get-tuple-element.87.refs_0_, bf16[48,2048]{1,0:T(8,128)(2,1)} %copy-done.14, bf16[128,2048]{1,0:T(8,128)(2,1)} %get-tuple-element.89.refs_2_, bf16[48,2048]{1,0:T(8,128)(2,1)} %copy-done.15, ...), custom_call_target="tpu_custom_call" | custom-call | flops 1 | bytes 1 | tf_op jit(solution)/shard_map/middle/pallas_call | solution.py:623
  94.2 0.0 reduce-scatter.3.cloned.1.call-update
  94.2 0.0 reduce-scatter.5.cloned.1.call-start
  94.3 1.0 copy-done.24
  95.3 13.2 %collective-permute-start.5 = (bf16[128,2048]{1,0:T(8,128)(2,1)S(1)}, bf16[128,2048]{1,0:T(8,128)(2,1)S(1)}, u32[]{:S(2)}, u32[]{:S(2)}) collective-permute-start(bf16[128,2048]{1,0:T(8,128)(2,1)S(1)} %copy-done.24), channel_id=1, source_target_pairs={{0,3},{1,0},{2,1},{3,2},{4,7},{5,4},{6,5},{7,6},{8,11},{9,8},{10,9... | collective-permute-start | bytes 1572872 | tf_op jit(solution)/shard_map/ppermute | solution.py:751
  108.4 7.0 %collective-permute-start.4 = (bf16[128,2048]{1,0:T(8,128)(2,1)S(1)}, bf16[128,2048]{1,0:T(8,128)(2,1)S(1)}, u32[]{:S(2)}, u32[]{:S(2)}) collective-permute-start(bf16[128,2048]{1,0:T(8,128)(2,1)S(1)} %copy-done.22), channel_id=1, source_target_pairs={{0,4},{4,0},{1,5},{5,1},{2,6},{6,2},{3,7},{7,3},{8,12},{12,8},{9,1... | collective-permute-start | bytes 1572872 | tf_op jit(solution)/shard_map/ppermute | solution.py:751
  115.5 13.5 %weights.3 = bf16[2048,1792]{1,0:T(8,128)(2,1)} custom-call(s32[16]{0:T(128)} %stack.94.order_ref, bf16[1024,2048]{1,0:T(8,128)(2,1)} %get-tuple-element.101.refs_0_.refs_1_.refs_2_.refs_3_, bf16[1024,2048]{1,0:T(8,128)(2,1)} %get-tuple-element.101.refs_0_.refs_1_.refs_2_.refs_3_, bf16[1024,2048]{1,0:T(8,128)(2,1)} %get-tuple-element.101.refs_0_.refs_1_.refs_2_.refs_3_, ...), custom_call_target="tpu_custom_call" | custom-call | flops 1 | bytes 1 | tf_op jit(solution)/shard_map/weights/pallas_call | solution.py:578
  129.1 0.7 copy-done.6
  129.8 0.2 copy-done.7
  130.0 0.2 copy-done.8
  130.1 3.0 %near.1 = (bf16[128,2048]{1,0:T(8,128)(2,1)}, bf16[128,2048]{1,0:T(8,128)(2,1)}) custom-call(bf16[128,2048]{1,0:T(8,128)(2,1)} %get-tuple-element.98.refs_0_, bf16[128,2048]{1,0:T(8,128)(2,1)} %copy-done.7, bf16[128,2048]{1,0:T(8,128)(2,1)} %copy-done.8, bf16[128,2048]{1,0:T(8,128)(2,1)} %get-tuple-element.99.refs_3_, bf16[128,2048]{1,0:T(8,128)(2,1)} %copy-done.6), custom_call_target="tpu_custom_call" | custom-call | flops 1 | bytes 1 | tf_op jit(solution)/shard_map/near/pallas_call | solution.py:623
  133.1 0.0 reduce-scatter.5.cloned.1.call-update
  133.1 1.0 copy-done.21
  134.2 3.3 %collective-permute-start.8 = (bf16[128,2048]{1,0:T(8,128)(2,1)S(1)}, bf16[128,2048]{1,0:T(8,128)(2,1)S(1)}, u32[]{:S(2)}, u32[]{:S(2)}) collective-permute-start(bf16[128,2048]{1,0:T(8,128)(2,1)S(1)} %copy-done.21), channel_id=1, source_target_pairs={{0,3},{1,0},{2,1},{3,2},{4,7},{5,4},{6,5},{7,6},{8,11},{9,8},{10,9... | collective-permute-start | bytes 1572872 | tf_op jit(solution)/shard_map/ppermute | solution.py:751
  137.5 0.1 collective-permute-start.7
  137.6 19.6 %collective-permute-done.8.refs_3_ = bf16[128,2048]{1,0:T(8,128)(2,1)S(1)} collective-permute-done((bf16[128,2048]{1,0:T(8,128)(2,1)S(1)}, bf16[128,2048]{1,0:T(8,128)(2,1)S(1)}, u32[]{:S(2)}, u32[]{:S(2)}) %collective-permute-start.8) | collective-permute-done | bytes 524320 | tf_op jit(solution)/shard_map/ppermute | solution.py:751
  157.2 3.7 %collective-permute-done.6.refs_1_ = bf16[128,2048]{1,0:T(8,128)(2,1)S(1)} collective-permute-done((bf16[128,2048]{1,0:T(8,128)(2,1)S(1)}, bf16[128,2048]{1,0:T(8,128)(2,1)S(1)}, u32[]{:S(2)}, u32[]{:S(2)}) %collective-permute-start.6) | collective-permute-done | bytes 524320 | tf_op jit(solution)/shard_map/ppermute | solution.py:751
  160.9 0.8 copy-done.10
  161.7 0.2 copy-done.11
  161.8 4.1 %input.1.refs_0_ = bf16[128,2048]{1,0:T(8,128)(2,1)} custom-call(s32[8]{0:T(128)} %stack.103.places_ref, bf16[128,2048]{1,0:T(8,128)(2,1)} %get-tuple-element.106.refs_0_, bf16[128,2048]{1,0:T(8,128)(2,1)} %copy-done.10, bf16[128,2048]{1,0:T(8,128)(2,1)} %copy-done.11, bf16[128,2048]{1,0:T(8,128)(2,1)} %copy-done.9, bf16[1024,2048]{1,0:T(8,128)(2,1)} %tokens_ref.1, ...), custom_call_target="tpu_custom_call" | custom-call | flops 1 | bytes 1 | tf_op jit(solution)/shard_map/input/pallas_call | solution.py:683
  166.0 9.2 %collective-permute-start.11 = (bf16[128,2048]{1,0:T(8,128)(2,1)}, bf16[128,2048]{1,0:T(8,128)(2,1)S(1)}, u32[]{:S(2)}, u32[]{:S(2)}) collective-permute-start(bf16[128,2048]{1,0:T(8,128)(2,1)} %input.1.refs_0_), channel_id=1, source_target_pairs={{0,3},{1,0},{2,1},{3,2},{4,7},{5,4},{6,5},{7,6},{8,11},{9,8},{10,9... | collective-permute-start | bytes 1572872 | tf_op jit(solution)/shard_map/ppermute | solution.py:751
  175.1 20.0 %all-reduce.2.cloned.1.call-done.branch_ref = bf16[1024,2048]{1,0:T(8,128)(2,1)} async-done(((bf16[1024,2048]{1,0:T(8,128)(2,1)}), bf16[1024,2048]{1,0:T(8,128)(2,1)}) %all-reduce.2.cloned.1.call-update) | async-done | bytes 4194320 | tf_op jit(solution)/shard_map/psum | solution.py:894
  195.1 1.0 slice.33
  196.1 1.0 collective-permute-start.9
  197.2 0.1 collective-permute-start.15
  197.3 1.2 collective-permute-start.14
  198.5 3.1 %collective-permute-start.13 = (bf16[128,2048]{1,0:T(8,128)(2,1)S(1)}, bf16[128,2048]{1,0:T(8,128)(2,1)S(1)}, u32[]{:S(2)}, u32[]{:S(2)}) collective-permute-start(bf16[128,2048]{1,0:T(8,128)(2,1)S(1)} %collective-permute-done.11.refs_2_), channel_id=1, source_target_pairs={{0,3},{1,0},{2,1},{3,2},{4,7},{5,4},{6,5},{7,6},{8,11},{9,8},{10,9... | collective-permute-start | bytes 1572872 | tf_op jit(solution)/shard_map/ppermute | solution.py:751
  201.6 7.4 %collective-permute-done.9.far_ref = bf16[128,1408]{1,0:T(8,128)(2,1)S(1)} collective-permute-done((bf16[128,1408]{1,0:T(8,128)(2,1)S(1)}, bf16[128,1408]{1,0:T(8,128)(2,1)S(1)}, u32[]{:S(2)}, u32[]{:S(2)}) %collective-permute-start.9) | collective-permute-done | bytes 360480 | tf_op jit(solution)/shard_map/ppermute | solution.py:751
  209.0 0.7 copy-done.13
  209.7 2.1 down.1
  211.9 6.4 %output.1 = bf16[1024,2048]{1,0:T(8,128)(2,1)} custom-call(s32[1,8]{1,0:T(1,128)} %lengths_ref.2, bf16[1024,2048]{1,0:T(8,128)(2,1)} %tokens_ref.1, bf16[1024,2048]{1,0:T(8,128)(2,1)} %all-reduce.2.cloned.1.call-done.branch_ref, bf16[2048]{0:T(1024)(128)(2,1)} %b_dense_ref.1, bf16[2048]{0:T(1024)(128)(2,1)} %b_fc2_ref.1), custom_call_target="tpu_custom_call" | custom-call | flops 1 | bytes 1 | tf_op jit(solution)/shard_map/output/pallas_call | solution.py:650
  218.2 0.0 reduce-scatter.5.cloned.1.call-done.near_ref
  218.3 1.1 slice.37
  219.3 1.1 collective-permute-start.19
  220.4 1.1 collective-permute-start.20
  221.6 0.1 collective-permute-start.18
  221.8 3.3 %collective-permute-start.17 = (bf16[48,2048]{1,0:T(8,128)(2,1)S(1)}, bf16[48,2048]{1,0:T(8,128)(2,1)S(1)}, u32[]{:S(2)}, u32[]{:S(2)}) collective-permute-start(bf16[48,2048]{1,0:T(8,128)(2,1)S(1)} %slice.35), channel_id=1, source_target_pairs={{0,3},{1,0},{2,1},{3,2},{4,7},{5,4},{6,5},{7,6},{8,11},{9,8},{10,9... | collective-permute-start | bytes 589832 | tf_op jit(solution)/shard_map/ppermute | solution.py:751
  225.0 0.9 collective-permute-start.16
  225.9 0.5 slice_bitcast_fusion
  226.4 3.9 %place.2.refs_3_ = bf16[1024,2048]{1,0:T(8,128)(2,1)} custom-call(s32[8]{0:T(128)} %stack.103.places_ref, bf16[128,2048]{1,0:T(8,128)(2,1)} %input.1.refs_0_, bf16[128,2048]{1,0:T(8,128)(2,1)} %copy-done.5, bf16[128,2048]{1,0:T(8,128)(2,1)} %copy-done.4, bf16[128,2048]{1,0:T(8,128)(2,1)} %copy-done.3, bf16[128,2048]{1,0:T(8,128)(2,1)} %copy-done.1, ...), custom_call_target="tpu_custom_call" | custom-call | flops 1 | bytes 1 | tf_op jit(solution)/shard_map/place/pallas_call | solution.py:713
  230.4 4.6 %collective-permute-done.16.refs_0_ = bf16[48,2048]{1,0:T(8,128)(2,1)S(1)} collective-permute-done((bf16[48,2048]{1,0:T(8,128)(2,1)S(1)}, bf16[48,2048]{1,0:T(8,128)(2,1)S(1)}, u32[]{:S(2)}, u32[]{:S(2)}) %collective-permute-start.16) | collective-permute-done | bytes 196640 | tf_op jit(solution)/shard_map/ppermute | solution.py:751
  235.0 0.1 collective-permute-start.23
  235.1 1.4 collective-permute-start.22
  236.6 0.7 collective-permute-start.21
  237.2 0.5 slice_bitcast_fusion.2
  237.7 2.1 up.1
  239.9 1.9 place.3
  241.8 0.5 slice_bitcast_fusion.3
  242.4 0.5 copy.29
  (79 shorter events, 0.2 us)
Async XLA Ops:
  8.0 187.1 %all-reduce.2.cloned.1.call-start = ((), (), s32[]{:S(2)}) async-start(), calls=%async_computation.3 | async-start | bytes 8388608 | tf_op jit(solution)/shard_map/psum | solution.py:894
  53.6 141.5 %reduce-scatter.3.cloned.1.call-start = ((), (), s32[]{:S(2)}) async-start(), calls=%async_computation.2 | async-start | bytes 6488064 | tf_op jit(solution)/shard_map/reduce_scatter | solution.py:838
  74.0 16.6 %collective-permute-start = (bf16[48,2048]{1,0:T(8,128)(2,1)}, bf16[48,2048]{1,0:T(8,128)(2,1)S(1)}, u32[]{:S(2)}, u32[]{:S(2)}) collective-permute-start(bf16[48,2048]{1,0:T(8,128)(2,1)} %get-tuple-element.88), channel_id=1, source_target_pairs={{0,4},{4,0},{1,5},{5,1},{2,6},{6,2},{3,7},{7,3},{8,12},{12,8},{9,1... | collective-permute-start | bytes 589832 | tf_op jit(solution)/shard_map/ppermute | solution.py:751
  76.1 14.6 %collective-permute-start.1 = (bf16[48,2048]{1,0:T(8,128)(2,1)}, bf16[48,2048]{1,0:T(8,128)(2,1)S(1)}, u32[]{:S(2)}, u32[]{:S(2)}) collective-permute-start(bf16[48,2048]{1,0:T(8,128)(2,1)} %get-tuple-element.90), channel_id=1, source_target_pairs={{0,1},{1,2},{2,3},{3,0},{4,5},{5,6},{6,7},{7,4},{8,9},{9,10},{10,1... | collective-permute-start | bytes 589832 | tf_op jit(solution)/shard_map/ppermute | solution.py:751
  77.7 12.9 %collective-permute-start.2 = (bf16[32,2048]{1,0:T(8,128)(2,1)}, bf16[32,2048]{1,0:T(8,128)(2,1)S(1)}, u32[]{:S(2)}, u32[]{:S(2)}) collective-permute-start(bf16[32,2048]{1,0:T(8,128)(2,1)} %get-tuple-element.92), channel_id=1, source_target_pairs={{0,3},{1,0},{2,1},{3,2},{4,7},{5,4},{6,5},{7,6},{8,11},{9,8},{10,9... | collective-permute-start | bytes 393224 | tf_op jit(solution)/shard_map/ppermute | solution.py:751
  90.6 0.7 copy-start.19
  90.7 0.7 copy-start.14
  90.7 0.7 copy-start.15
  94.2 1.0 copy-start.24
  94.2 14.2 %copy-start.23 = (bf16[128,2048]{1,0:T(8,128)(2,1)S(1)}, bf16[128,2048]{1,0:T(8,128)(2,1)}, u32[]{:S(2)}) copy-start(bf16[128,2048]{1,0:T(8,128)(2,1)} %get-tuple-element.94) | copy-start | bytes 1572868
  94.2 14.2 %copy-start.22 = (bf16[128,2048]{1,0:T(8,128)(2,1)S(1)}, bf16[128,2048]{1,0:T(8,128)(2,1)}, u32[]{:S(2)}) copy-start(bf16[128,2048]{1,0:T(8,128)(2,1)} %get-tuple-element.95) | copy-start | bytes 1572868
  94.2 124.0 %reduce-scatter.5.cloned.1.call-start = ((), (), s32[]{:S(2)}) async-start(), calls=%async_computation.4 | async-start | bytes 8257536 | tf_op jit(solution)/shard_map/reduce_scatter | solution.py:838
  95.3 33.7 %collective-permute-start.5 = (bf16[128,2048]{1,0:T(8,128)(2,1)S(1)}, bf16[128,2048]{1,0:T(8,128)(2,1)S(1)}, u32[]{:S(2)}, u32[]{:S(2)}) collective-permute-start(bf16[128,2048]{1,0:T(8,128)(2,1)S(1)} %copy-done.24), channel_id=1, source_target_pairs={{0,3},{1,0},{2,1},{3,2},{4,7},{5,4},{6,5},{7,6},{8,11},{9,8},{10,9... | collective-permute-start | bytes 1572872 | tf_op jit(solution)/shard_map/ppermute | solution.py:751
  108.4 20.6 %collective-permute-start.3 = (bf16[128,2048]{1,0:T(8,128)(2,1)S(1)}, bf16[128,2048]{1,0:T(8,128)(2,1)S(1)}, u32[]{:S(2)}, u32[]{:S(2)}) collective-permute-start(bf16[128,2048]{1,0:T(8,128)(2,1)S(1)} %copy-done.23), channel_id=1, source_target_pairs={{0,1},{1,2},{2,3},{3,0},{4,5},{5,6},{6,7},{7,4},{8,9},{9,10},{10,1... | collective-permute-start | bytes 1572872 | tf_op jit(solution)/shard_map/ppermute | solution.py:751
  108.4 20.6 %collective-permute-start.4 = (bf16[128,2048]{1,0:T(8,128)(2,1)S(1)}, bf16[128,2048]{1,0:T(8,128)(2,1)S(1)}, u32[]{:S(2)}, u32[]{:S(2)}) collective-permute-start(bf16[128,2048]{1,0:T(8,128)(2,1)S(1)} %copy-done.22), channel_id=1, source_target_pairs={{0,4},{4,0},{1,5},{5,1},{2,6},{6,2},{3,7},{7,3},{8,12},{12,8},{9,1... | collective-permute-start | bytes 1572872 | tf_op jit(solution)/shard_map/ppermute | solution.py:751
  129.0 0.8 copy-start.6
  129.0 0.9 copy-start.7
  129.0 1.1 copy-start.8
  133.1 1.1 copy-start.21
  133.1 4.4 %copy-start.26 = (bf16[128,2048]{1,0:T(8,128)(2,1)S(1)}, bf16[128,2048]{1,0:T(8,128)(2,1)}, u32[]{:S(2)}) copy-start(bf16[128,2048]{1,0:T(8,128)(2,1)} %get-tuple-element.103) | copy-start | bytes 1572868
  133.1 4.4 %copy-start.25 = (bf16[128,2048]{1,0:T(8,128)(2,1)S(1)}, bf16[128,2048]{1,0:T(8,128)(2,1)}, u32[]{:S(2)}) copy-start(bf16[128,2048]{1,0:T(8,128)(2,1)} %get-tuple-element.104) | copy-start | bytes 1572868
  134.2 23.0 %collective-permute-start.8 = (bf16[128,2048]{1,0:T(8,128)(2,1)S(1)}, bf16[128,2048]{1,0:T(8,128)(2,1)S(1)}, u32[]{:S(2)}, u32[]{:S(2)}) collective-permute-start(bf16[128,2048]{1,0:T(8,128)(2,1)S(1)} %copy-done.21), channel_id=1, source_target_pairs={{0,3},{1,0},{2,1},{3,2},{4,7},{5,4},{6,5},{7,6},{8,11},{9,8},{10,9... | collective-permute-start | bytes 1572872 | tf_op jit(solution)/shard_map/ppermute | solution.py:751
  137.5 23.3 %collective-permute-start.6 = (bf16[128,2048]{1,0:T(8,128)(2,1)S(1)}, bf16[128,2048]{1,0:T(8,128)(2,1)S(1)}, u32[]{:S(2)}, u32[]{:S(2)}) collective-permute-start(bf16[128,2048]{1,0:T(8,128)(2,1)S(1)} %copy-done.26), channel_id=1, source_target_pairs={{0,1},{1,2},{2,3},{3,0},{4,5},{5,6},{6,7},{7,4},{8,9},{9,10},{10,1... | collective-permute-start | bytes 1572872 | tf_op jit(solution)/shard_map/ppermute | solution.py:751
  137.5 23.3 %collective-permute-start.7 = (bf16[128,2048]{1,0:T(8,128)(2,1)S(1)}, bf16[128,2048]{1,0:T(8,128)(2,1)S(1)}, u32[]{:S(2)}, u32[]{:S(2)}) collective-permute-start(bf16[128,2048]{1,0:T(8,128)(2,1)S(1)} %copy-done.25), channel_id=1, source_target_pairs={{0,4},{4,0},{1,5},{5,1},{2,6},{6,2},{3,7},{7,3},{8,12},{12,8},{9,1... | collective-permute-start | bytes 1572872 | tf_op jit(solution)/shard_map/ppermute | solution.py:751
  157.2 3.7 %copy-start.9 = (bf16[128,2048]{1,0:T(8,128)(2,1)}, bf16[128,2048]{1,0:T(8,128)(2,1)S(1)}, u32[]{:S(2)}) copy-start(bf16[128,2048]{1,0:T(8,128)(2,1)S(1)} %collective-permute-done.8.refs_3_) | copy-start | bytes 1572868
  160.9 0.8 copy-start.10
  160.9 1.0 copy-start.11
  165.9 31.2 %collective-permute-start.12 = (bf16[128,2048]{1,0:T(8,128)(2,1)}, bf16[128,2048]{1,0:T(8,128)(2,1)S(1)}, u32[]{:S(2)}, u32[]{:S(2)}) collective-permute-start(bf16[128,2048]{1,0:T(8,128)(2,1)} %input.1.refs_0_), channel_id=1, source_target_pairs={{0,4},{4,0},{1,5},{5,1},{2,6},{6,2},{3,7},{7,3},{8,12},{12,8},{9,1... | collective-permute-start | bytes 1572872 | tf_op jit(solution)/shard_map/ppermute | solution.py:751
  166.0 31.2 %collective-permute-start.11 = (bf16[128,2048]{1,0:T(8,128)(2,1)}, bf16[128,2048]{1,0:T(8,128)(2,1)S(1)}, u32[]{:S(2)}, u32[]{:S(2)}) collective-permute-start(bf16[128,2048]{1,0:T(8,128)(2,1)} %input.1.refs_0_), channel_id=1, source_target_pairs={{0,3},{1,0},{2,1},{3,2},{4,7},{5,4},{6,5},{7,6},{8,11},{9,8},{10,9... | collective-permute-start | bytes 1572872 | tf_op jit(solution)/shard_map/ppermute | solution.py:751
  175.1 22.1 %collective-permute-start.10 = (bf16[128,2048]{1,0:T(8,128)(2,1)}, bf16[128,2048]{1,0:T(8,128)(2,1)S(1)}, u32[]{:S(2)}, u32[]{:S(2)}) collective-permute-start(bf16[128,2048]{1,0:T(8,128)(2,1)} %input.1.refs_0_), channel_id=1, source_target_pairs={{0,1},{1,2},{2,3},{3,0},{4,5},{5,6},{6,7},{7,4},{8,9},{9,10},{10,1... | collective-permute-start | bytes 1572872 | tf_op jit(solution)/shard_map/ppermute | solution.py:751
  196.1 12.9 %collective-permute-start.9 = (bf16[128,1408]{1,0:T(8,128)(2,1)S(1)}, bf16[128,1408]{1,0:T(8,128)(2,1)S(1)}, u32[]{:S(2)}, u32[]{:S(2)}) collective-permute-start(bf16[128,1408]{1,0:T(8,128)(2,1)S(1)} %slice.33), channel_id=1, source_target_pairs={{0,64},{64,0},{1,65},{65,1},{2,66},{66,2},{3,67},{67,3},{4,68},{68... | collective-permute-start | bytes 1081352 | tf_op jit(solution)/shard_map/ppermute | solution.py:751
  197.2 21.1 %copy-start.3 = (bf16[128,2048]{1,0:T(8,128)(2,1)}, bf16[128,2048]{1,0:T(8,128)(2,1)S(1)}, u32[]{:S(2)}) copy-start(bf16[128,2048]{1,0:T(8,128)(2,1)S(1)} %collective-permute-done.12.refs_3_) | copy-start | bytes 1572868
  197.2 21.1 %copy-start.4 = (bf16[128,2048]{1,0:T(8,128)(2,1)}, bf16[128,2048]{1,0:T(8,128)(2,1)S(1)}, u32[]{:S(2)}) copy-start(bf16[128,2048]{1,0:T(8,128)(2,1)S(1)} %collective-permute-done.11.refs_2_) | copy-start | bytes 1572868
  197.2 21.0 %copy-start.5 = (bf16[128,2048]{1,0:T(8,128)(2,1)}, bf16[128,2048]{1,0:T(8,128)(2,1)S(1)}, u32[]{:S(2)}) copy-start(bf16[128,2048]{1,0:T(8,128)(2,1)S(1)} %collective-permute-done.10.refs_1_) | copy-start | bytes 1572868
  197.2 24.3 %collective-permute-start.15 = (bf16[128,2048]{1,0:T(8,128)(2,1)S(1)}, bf16[128,2048]{1,0:T(8,128)(2,1)S(1)}, u32[]{:S(2)}, u32[]{:S(2)}) collective-permute-start(bf16[128,2048]{1,0:T(8,128)(2,1)S(1)} %collective-permute-done.12.refs_3_), channel_id=1, source_target_pairs={{0,1},{1,2},{2,3},{3,0},{4,5},{5,6},{6,7},{7,4},{8,9},{9,10},{10,1... | collective-permute-start | bytes 1572872 | tf_op jit(solution)/shard_map/ppermute | solution.py:751
  197.3 24.3 %collective-permute-start.14 = (bf16[128,2048]{1,0:T(8,128)(2,1)S(1)}, bf16[128,2048]{1,0:T(8,128)(2,1)S(1)}, u32[]{:S(2)}, u32[]{:S(2)}) collective-permute-start(bf16[128,2048]{1,0:T(8,128)(2,1)S(1)} %collective-permute-done.11.refs_2_), channel_id=1, source_target_pairs={{0,4},{4,0},{1,5},{5,1},{2,6},{6,2},{3,7},{7,3},{8,12},{12,8},{9,1... | collective-permute-start | bytes 1572872 | tf_op jit(solution)/shard_map/ppermute | solution.py:751
  198.5 23.1 %collective-permute-start.13 = (bf16[128,2048]{1,0:T(8,128)(2,1)S(1)}, bf16[128,2048]{1,0:T(8,128)(2,1)S(1)}, u32[]{:S(2)}, u32[]{:S(2)}) collective-permute-start(bf16[128,2048]{1,0:T(8,128)(2,1)S(1)} %collective-permute-done.11.refs_2_), channel_id=1, source_target_pairs={{0,3},{1,0},{2,1},{3,2},{4,7},{5,4},{6,5},{7,6},{8,11},{9,8},{10,9... | collective-permute-start | bytes 1572872 | tf_op jit(solution)/shard_map/ppermute | solution.py:751
  209.0 0.7 copy-start.13
  211.9 8.5 %copy-start.20 = (f32[8,128]{1,0:T(8,128)S(1)}, f32[8,128]{1,0:T(8,128)}, u32[]{:S(2)}) copy-start(f32[8,128]{1,0:T(8,128)} %get-tuple-element.114) | copy-start | bytes 12292
  219.3 15.7 %collective-permute-start.19 = (bf16[128,1792]{1,0:T(8,128)(2,1)S(1)}, bf16[128,1792]{1,0:T(8,128)(2,1)S(1)}, u32[]{:S(2)}, u32[]{:S(2)}) collective-permute-start(bf16[128,1792]{1,0:T(8,128)(2,1)S(1)} %slice.37), channel_id=1, source_target_pairs={{0,64},{64,0},{1,65},{65,1},{2,66},{66,2},{3,67},{67,3},{4,68},{68... | collective-permute-start | bytes 1376264 | tf_op jit(solution)/shard_map/ppermute | solution.py:751
  220.4 14.6 %collective-permute-start.20 = (f32[2,128]{1,0:T(2,128)S(1)}, f32[2,128]{1,0:T(2,128)S(1)}, u32[]{:S(2)}, u32[]{:S(2)}) collective-permute-start(f32[2,128]{1,0:T(2,128)S(1)} %slice.38), channel_id=1, source_target_pairs={{0,4},{4,0},{1,5},{5,1},{2,6},{6,2},{3,7},{7,3},{8,12},{12,8},{9,1... | collective-permute-start | bytes 3080 | tf_op jit(solution)/shard_map/ppermute | solution.py:751
  221.5 20.8 %copy-start.27 = (f32[128]{0:T(128)}, f32[128]{0:T(128)S(1)}, u32[]{:S(2)}) copy-start(f32[128]{0:T(128)S(1)} %slice_bitcast_fusion.1) | copy-start | bytes 1540
  221.6 4.9 %copy-start.2 = (bf16[128,2048]{1,0:T(8,128)(2,1)}, bf16[128,2048]{1,0:T(8,128)(2,1)S(1)}, u32[]{:S(2)}) copy-start(bf16[128,2048]{1,0:T(8,128)(2,1)S(1)} %collective-permute-done.15.refs_6_) | copy-start | bytes 1572868
  221.6 4.9 %copy-start = (bf16[128,2048]{1,0:T(8,128)(2,1)}, bf16[128,2048]{1,0:T(8,128)(2,1)S(1)}, u32[]{:S(2)}) copy-start(bf16[128,2048]{1,0:T(8,128)(2,1)S(1)} %collective-permute-done.14.refs_5_) | copy-start | bytes 1572868
  221.6 4.8 %copy-start.1 = (bf16[128,2048]{1,0:T(8,128)(2,1)}, bf16[128,2048]{1,0:T(8,128)(2,1)S(1)}, u32[]{:S(2)}) copy-start(bf16[128,2048]{1,0:T(8,128)(2,1)S(1)} %collective-permute-done.13.refs_4_) | copy-start | bytes 1572868
  221.6 8.7 %collective-permute-start.18 = (bf16[32,2048]{1,0:T(8,128)(2,1)S(1)}, bf16[32,2048]{1,0:T(8,128)(2,1)S(1)}, u32[]{:S(2)}, u32[]{:S(2)}) collective-permute-start(bf16[32,2048]{1,0:T(8,128)(2,1)S(1)} %slice.36), channel_id=1, source_target_pairs={{0,1},{1,2},{2,3},{3,0},{4,5},{5,6},{6,7},{7,4},{8,9},{9,10},{10,1... | collective-permute-start | bytes 393224 | tf_op jit(solution)/shard_map/ppermute | solution.py:751
  221.8 8.6 %collective-permute-start.17 = (bf16[48,2048]{1,0:T(8,128)(2,1)S(1)}, bf16[48,2048]{1,0:T(8,128)(2,1)S(1)}, u32[]{:S(2)}, u32[]{:S(2)}) collective-permute-start(bf16[48,2048]{1,0:T(8,128)(2,1)S(1)} %slice.35), channel_id=1, source_target_pairs={{0,3},{1,0},{2,1},{3,2},{4,7},{5,4},{6,5},{7,6},{8,11},{9,8},{10,9... | collective-permute-start | bytes 589832 | tf_op jit(solution)/shard_map/ppermute | solution.py:751
  225.0 9.9 %collective-permute-start.16 = (bf16[48,2048]{1,0:T(8,128)(2,1)S(1)}, bf16[48,2048]{1,0:T(8,128)(2,1)S(1)}, u32[]{:S(2)}, u32[]{:S(2)}) collective-permute-start(bf16[48,2048]{1,0:T(8,128)(2,1)S(1)} %slice.34), channel_id=1, source_target_pairs={{0,4},{4,0},{1,5},{5,1},{2,6},{6,2},{3,7},{7,3},{8,12},{12,8},{9,1... | collective-permute-start | bytes 589832 | tf_op jit(solution)/shard_map/ppermute | solution.py:751
  230.4 9.5 %copy-start.18 = (bf16[32,2048]{1,0:T(8,128)(2,1)}, bf16[32,2048]{1,0:T(8,128)(2,1)S(1)}, u32[]{:S(2)}) copy-start(bf16[32,2048]{1,0:T(8,128)(2,1)S(1)} %collective-permute-done.18.refs_2_) | copy-start | bytes 393220
  230.4 9.5 %copy-start.16 = (bf16[48,2048]{1,0:T(8,128)(2,1)}, bf16[48,2048]{1,0:T(8,128)(2,1)S(1)}, u32[]{:S(2)}) copy-start(bf16[48,2048]{1,0:T(8,128)(2,1)S(1)} %collective-permute-done.17.refs_1_) | copy-start | bytes 589828
  235.0 4.9 %copy-start.17 = (bf16[48,2048]{1,0:T(8,128)(2,1)}, bf16[48,2048]{1,0:T(8,128)(2,1)S(1)}, u32[]{:S(2)}) copy-start(bf16[48,2048]{1,0:T(8,128)(2,1)S(1)} %collective-permute-done.16.refs_0_) | copy-start | bytes 589828
  235.0 2.7 %copy-start.12 = (bf16[128,1792]{1,0:T(8,128)(2,1)}, bf16[128,1792]{1,0:T(8,128)(2,1)S(1)}, u32[]{:S(2)}) copy-start(bf16[128,1792]{1,0:T(8,128)(2,1)S(1)} %collective-permute-done.19.far_ref) | copy-start | bytes 1376260
  235.0 6.8 %collective-permute-start.23 = (f32[2,128]{1,0:T(2,128)S(1)}, f32[2,128]{1,0:T(2,128)S(1)}, u32[]{:S(2)}, u32[]{:S(2)}) collective-permute-start(f32[2,128]{1,0:T(2,128)S(1)} %slice_add_fusion), channel_id=1, source_target_pairs={{0,2},{1,3},{2,0},{3,1},{4,6},{5,7},{6,4},{7,5},{8,10},{9,11},{10,... | collective-permute-start | bytes 3080 | tf_op jit(solution)/shard_map/ppermute | solution.py:751
  235.1 6.7 %collective-permute-start.22 = (f32[2,128]{1,0:T(2,128)S(1)}, f32[2,128]{1,0:T(2,128)S(1)}, u32[]{:S(2)}, u32[]{:S(2)}) collective-permute-start(f32[2,128]{1,0:T(2,128)S(1)} %slice_add_fusion), channel_id=1, source_target_pairs={{0,3},{1,0},{2,1},{3,2},{4,7},{5,4},{6,5},{7,6},{8,11},{9,8},{10,9... | collective-permute-start | bytes 3080 | tf_op jit(solution)/shard_map/ppermute | solution.py:751
  236.6 5.3 %collective-permute-start.21 = (f32[2,128]{1,0:T(2,128)S(1)}, f32[2,128]{1,0:T(2,128)S(1)}, u32[]{:S(2)}, u32[]{:S(2)}) collective-permute-start(f32[2,128]{1,0:T(2,128)S(1)} %slice_add_fusion), channel_id=1, source_target_pairs={{0,1},{1,2},{2,3},{3,0},{4,5},{5,6},{6,7},{7,4},{8,9},{9,10},{10,1... | collective-permute-start | bytes 3080 | tf_op jit(solution)/shard_map/ppermute | solution.py:751
Sparse Core Ops, SparseCore 0:
  53.7 141.3 all-reduce.1
Sparse Core Ops, SparseCore 1:
  94.3 56.5 reduce-scatter.2
  153.1 47.0 reduce-scatter.4

commit v3 on v2

--- a/solution.py
+++ b/solution.py
@@ -909,17 +909,17 @@
     input_grad = TensorGather(places, rows)
     down.send((rows, branch_sum))
     done = input_grad.second(down.near)
+    up.send(done)
+    output = finish_output(after(seq_lengths, up.near), tokens, branch_sum, b_dense, b_fc2)
     grad_fc2, grad_dense, small = down.finish(
         down_kernel,
         "down",
         ((units, BLOCK), (w_dense.shape[0], BLOCK), (8, BLOCK)),
-        done,
+        output,
     )
     norm_sum = small[:2]
     norm_across = across(norm_sum)
-    output = finish_output(after(seq_lengths, small), tokens, branch_sum, b_dense, b_fc2)
-    up.send(output)
-    input_grad.third((output, up.near))
+    input_grad.third(small)
     *three, up.far = after([*input_grad.three, up.far], input_grad.whole)
     input_grad.three = three
     norm_sum = norm_sum + after(norm_across, three[0])

time: 251 us -> 251 us (level)
  waiting for transfers between devices: 55.3 us -> 48.1 us
  starting transfers between devices: 52.3 us -> 55.9 us
  local copies, waits for them, and re-layouts: 11.6 us -> 15 us
    ppermute x24, waiting for transfers between devices: 35.3 us -> 28.8 us  [shift(): lax.ppermute(array, axis, [(i, (i + by) % size) for i in range(size)])]
    ppermute x24, starting transfers between devices: 52.2 us -> 55.7 us  [shift(): lax.ppermute(array, axis, [(i, (i + by) % size) for i in range(size)])]
    unnamed x57 -> x55, local copies, waits for them, and re-layouts: 6.1 us -> 6.1 us
  transfers between devices with their start and end apart: 27 -> 27, of which waited for: 5 -> 6; matrix products, arithmetic and copies ran while one was open for 2% -> 3% of each run, Pallas kernels for 28% -> 28%
where the time goes in v3:
time: 251 us
  Pallas kernels  115 us (46%)
  starting transfers between devices  55.9 us (22%)
  waiting for transfers between devices  48.1 us (19%)
  between operations  15.9 us (6%)
  local copies, waits for them, and re-layouts  15 us (6%)
    ppermute x24, starting transfers between devices, shift(): lax.ppermute(array, axis, [(i, (i + by) % size) for i in range(size)])  55.7 us
    pallas_call x1, Pallas kernels, forward(): kernel_call(forward_kernel, 'forward', [made(slot_len, columns) for colum...  44.2 us
    ppermute x24, waiting for transfers between devices, shift(): lax.ppermute(array, axis, [(i, (i + by) % size) for i in range(size)])  28.8 us
    pallas_call x2, Pallas kernels, weight_blocks(): kernel_call(weight_kernel, 'weights', made(left.shape[1], width), prefetc...  24.2 us
    pallas_call x1, Pallas kernels, backward(): kernel_call(backward_kernel, 'backward', sums + [made(slot_len, units)] +...  20.4 us
    psum x1, waiting for transfers between devices, per_device(): branch_sum = lax.psum(branch_part, TENSOR)  19.3 us
    pallas_call x1, Pallas kernels, finish_output(): kernel_call(output_kernel, 'output', made(slot_len, width), grid=(slot_le...  6.36 us
    unnamed x55, local copies, waits for them, and re-layouts  6.1 us
  transfers between devices with their start and end apart: 27, of which 6 were waited for; matrix products, arithmetic and copies ran while one was open for 3% of the time, Pallas kernels for 28%

profile of v3, /device:TPU:0, one launch (start us, length us, event | category | flops | bytes accessed | tf_op | source)
XLA Modules:
  0.0 250.7 jit_solution(2490363704886910996)
XLA Ops:
  8.0 0.0 all-reduce.2.cloned.1.call-start
  8.1 0.6 broadcast_in_dim_tile.3.freq_ref
  8.7 0.6 stack.103.places_ref
  9.4 44.2 %forward.1 = (bf16[1024,2048]{1,0:T(8,128)(2,1)}, bf16[1024,2048]{1,0:T(8,128)(2,1)}, bf16[1024,1024]{1,0:T(8,128)(2,1)}, bf16[1024,1024]{1,0:T(8,128)(2,1)}, bf...) custom-call(s32[1,8]{1,0:T(1,128)} %lengths_ref.2, ...), custom_call_target="tpu_custom_call" | custom-call | flops 1 | bytes 1 | tf_op jit(solution)/shard_map/forward/pallas_call | solution.py:392
  53.6 0.0 reduce-scatter.5.cloned.1.call-start
  53.7 20.4 %backward.1 = (f32[32,128]{1,0:T(8,128)}, f32[16,128]{1,0:T(8,128)}, f32[16,128]{1,0:T(8,128)}, f32[16,128]{1,0:T(8,128)}, bf16[1024,1024]{1,0:T(8,128)(2,1)}, /...) custom-call(s32[8]{0:T(128)} %stack.103.places_ref, ...), custom_call_target="tpu_custom_call" | custom-call | flops 1 | bytes 1 | tf_op jit(solution)/shard_map/backward/pallas_call | solution.py:540
  74.1 2.1 collective-permute-start
  76.2 1.6 collective-permute-start.1
  77.8 1.7 collective-permute-start.2
  79.4 0.6 stack.94.order_ref
  80.0 10.6 %weights.2 = bf16[2048,1408]{1,0:T(8,128)(2,1)} custom-call(s32[16]{0:T(128)} %stack.94.order_ref, bf16[1024,2048]{1,0:T(8,128)(2,1)} %get-tuple-element.75.grad_hbm.refs_0_.refs_1_.refs_2_.refs_3_, bf16[1024,2048]{1,0:T(8,128)(2,1)} %get-tuple-element.75.grad_hbm.refs_0_.refs_1_.refs_2_.refs_3_, ...), custom_call_target="tpu_custom_call" | custom-call | flops 1 | bytes 1 | tf_op jit(solution)/shard_map/weights/pallas_call | solution.py:578
  90.7 0.6 copy-done.19
  91.3 0.1 copy-done.14
  91.4 0.1 copy-done.15
  91.4 2.8 %middle.1 = (bf16[128,2048]{1,0:T(8,128)(2,1)}, bf16[128,2048]{1,0:T(8,128)(2,1)}, bf16[128,2048]{1,0:T(8,128)(2,1)}) custom-call(bf16[128,2048]{1,0:T(8,128)(2,1)} %get-tuple-element.79.refs_0_, bf16[48,2048]{1,0:T(8,128)(2,1)} %copy-done.14, bf16[128,2048]{1,0:T(8,128)(2,1)} %get-tuple-element.81.refs_2_, bf16[48,2048]{1,0:T(8,128)(2,1)} %copy-done.15, ...), custom_call_target="tpu_custom_call" | custom-call | flops 1 | bytes 1 | tf_op jit(solution)/shard_map/middle/pallas_call | solution.py:623
  94.2 0.0 reduce-scatter.5.cloned.1.call-update
  94.3 0.0 reduce-scatter.3.cloned.1.call-start
  94.3 1.0 copy-done.23
  95.3 13.2 %collective-permute-start.5 = (bf16[128,2048]{1,0:T(8,128)(2,1)S(1)}, bf16[128,2048]{1,0:T(8,128)(2,1)S(1)}, u32[]{:S(2)}, u32[]{:S(2)}) collective-permute-start(bf16[128,2048]{1,0:T(8,128)(2,1)S(1)} %copy-done.23), channel_id=1, source_target_pairs={{0,3},{1,0},{2,1},{3,2},{4,7},{5,4},{6,5},{7,6},{8,11},{9,8},{10,9... | collective-permute-start | bytes 1572872 | tf_op jit(solution)/shard_map/ppermute | solution.py:751
  108.5 7.0 %collective-permute-start.4 = (bf16[128,2048]{1,0:T(8,128)(2,1)S(1)}, bf16[128,2048]{1,0:T(8,128)(2,1)S(1)}, u32[]{:S(2)}, u32[]{:S(2)}) collective-permute-start(bf16[128,2048]{1,0:T(8,128)(2,1)S(1)} %copy-done.21), channel_id=1, source_target_pairs={{0,4},{4,0},{1,5},{5,1},{2,6},{6,2},{3,7},{7,3},{8,12},{12,8},{9,1... | collective-permute-start | bytes 1572872 | tf_op jit(solution)/shard_map/ppermute | solution.py:751
  115.5 13.5 %weights.3 = bf16[2048,1792]{1,0:T(8,128)(2,1)} custom-call(s32[16]{0:T(128)} %stack.94.order_ref, bf16[1024,2048]{1,0:T(8,128)(2,1)} %get-tuple-element.98.refs_0_.refs_1_.refs_2_.refs_3_, bf16[1024,2048]{1,0:T(8,128)(2,1)} %get-tuple-element.98.refs_0_.refs_1_.refs_2_.refs_3_, bf16[1024,2048]{1,0:T(8,128)(2,1)} %get-tuple-element.98.refs_0_.refs_1_.refs_2_.refs_3_, ...), custom_call_target="tpu_custom_call" | custom-call | flops 1 | bytes 1 | tf_op jit(solution)/shard_map/weights/pallas_call | solution.py:578
  129.1 0.7 copy-done.6
  129.8 0.2 copy-done.7
  130.0 0.2 copy-done.8
  130.2 3.0 %near.1 = (bf16[128,2048]{1,0:T(8,128)(2,1)}, bf16[128,2048]{1,0:T(8,128)(2,1)}) custom-call(bf16[128,2048]{1,0:T(8,128)(2,1)} %get-tuple-element.99.refs_0_, bf16[128,2048]{1,0:T(8,128)(2,1)} %copy-done.7, bf16[128,2048]{1,0:T(8,128)(2,1)} %copy-done.8, bf16[128,2048]{1,0:T(8,128)(2,1)} %get-tuple-element.100.refs_3_, bf16[128,2048]{1,0:T(8,128)(2,1)} %copy-done.6), custom_call_target="tpu_custom_call" | custom-call | flops 1 | bytes 1 | tf_op jit(solution)/shard_map/near/pallas_call | solution.py:623
  133.2 0.0 reduce-scatter.3.cloned.1.call-update
  133.2 1.0 copy-done.20
  134.2 3.3 %collective-permute-start.8 = (bf16[128,2048]{1,0:T(8,128)(2,1)S(1)}, bf16[128,2048]{1,0:T(8,128)(2,1)S(1)}, u32[]{:S(2)}, u32[]{:S(2)}) collective-permute-start(bf16[128,2048]{1,0:T(8,128)(2,1)S(1)} %copy-done.20), channel_id=1, source_target_pairs={{0,3},{1,0},{2,1},{3,2},{4,7},{5,4},{6,5},{7,6},{8,11},{9,8},{10,9... | collective-permute-start | bytes 1572872 | tf_op jit(solution)/shard_map/ppermute | solution.py:751
  137.6 0.1 collective-permute-start.7
  137.7 19.7 %collective-permute-done.8.refs_3_ = bf16[128,2048]{1,0:T(8,128)(2,1)S(1)} collective-permute-done((bf16[128,2048]{1,0:T(8,128)(2,1)S(1)}, bf16[128,2048]{1,0:T(8,128)(2,1)S(1)}, u32[]{:S(2)}, u32[]{:S(2)}) %collective-permute-start.8) | collective-permute-done | bytes 524320 | tf_op jit(solution)/shard_map/ppermute | solution.py:751
  157.3 3.7 %collective-permute-done.6.refs_1_ = bf16[128,2048]{1,0:T(8,128)(2,1)S(1)} collective-permute-done((bf16[128,2048]{1,0:T(8,128)(2,1)S(1)}, bf16[128,2048]{1,0:T(8,128)(2,1)S(1)}, u32[]{:S(2)}, u32[]{:S(2)}) %collective-permute-start.6) | collective-permute-done | bytes 524320 | tf_op jit(solution)/shard_map/ppermute | solution.py:751
  161.0 0.8 copy-done.10
  161.8 0.2 copy-done.11
  162.0 4.1 %input.1.refs_0_ = bf16[128,2048]{1,0:T(8,128)(2,1)} custom-call(s32[8]{0:T(128)} %stack.103.places_ref, bf16[128,2048]{1,0:T(8,128)(2,1)} %get-tuple-element.106.refs_0_, bf16[128,2048]{1,0:T(8,128)(2,1)} %copy-done.10, bf16[128,2048]{1,0:T(8,128)(2,1)} %copy-done.11, bf16[128,2048]{1,0:T(8,128)(2,1)} %copy-done.9, bf16[1024,2048]{1,0:T(8,128)(2,1)} %tokens_ref.1, ...), custom_call_target="tpu_custom_call" | custom-call | flops 1 | bytes 1 | tf_op jit(solution)/shard_map/input/pallas_call | solution.py:683
  166.1 9.5 %collective-permute-start.10 = (bf16[128,2048]{1,0:T(8,128)(2,1)}, bf16[128,2048]{1,0:T(8,128)(2,1)S(1)}, u32[]{:S(2)}, u32[]{:S(2)}) collective-permute-start(bf16[128,2048]{1,0:T(8,128)(2,1)} %input.1.refs_0_), channel_id=1, source_target_pairs={{0,3},{1,0},{2,1},{3,2},{4,7},{5,4},{6,5},{7,6},{8,11},{9,8},{10,9... | collective-permute-start | bytes 1572872 | tf_op jit(solution)/shard_map/ppermute | solution.py:751
  175.7 19.3 %all-reduce.2.cloned.1.call-done.branch_ref = bf16[1024,2048]{1,0:T(8,128)(2,1)} async-done(((bf16[1024,2048]{1,0:T(8,128)(2,1)}), bf16[1024,2048]{1,0:T(8,128)(2,1)}) %all-reduce.2.cloned.1.call-update) | async-done | bytes 4194320 | tf_op jit(solution)/shard_map/psum | solution.py:894
  194.9 0.4 collective-permute-done.11.refs_3_
  195.4 0.5 collective-permute-done.9.refs_1_
  195.9 1.4 collective-permute-start.13
  197.3 3.1 %collective-permute-start.12 = (bf16[128,2048]{1,0:T(8,128)(2,1)S(1)}, bf16[128,2048]{1,0:T(8,128)(2,1)S(1)}, u32[]{:S(2)}, u32[]{:S(2)}) collective-permute-start(bf16[128,2048]{1,0:T(8,128)(2,1)S(1)} %collective-permute-done.10.refs_2_), channel_id=1, source_target_pairs={{0,3},{1,0},{2,1},{3,2},{4,7},{5,4},{6,5},{7,6},{8,11},{9,8},{10,9... | collective-permute-start | bytes 1572872 | tf_op jit(solution)/shard_map/ppermute | solution.py:751
  200.5 1.7 slice.33
  202.2 1.0 slice.37
  203.3 3.6 %collective-permute-start.19 = (bf16[128,1792]{1,0:T(8,128)(2,1)S(1)}, bf16[128,1792]{1,0:T(8,128)(2,1)S(1)}, u32[]{:S(2)}, u32[]{:S(2)}) collective-permute-start(bf16[128,1792]{1,0:T(8,128)(2,1)S(1)} %slice.37), channel_id=1, source_target_pairs={{0,64},{64,0},{1,65},{65,1},{2,66},{66,2},{3,67},{67,3},{4,68},{68... | collective-permute-start | bytes 1376264 | tf_op jit(solution)/shard_map/ppermute | solution.py:751
  206.9 6.4 %output.1 = bf16[1024,2048]{1,0:T(8,128)(2,1)} custom-call(s32[1,8]{1,0:T(1,128)} %lengths_ref.2, bf16[1024,2048]{1,0:T(8,128)(2,1)} %tokens_ref.1, bf16[1024,2048]{1,0:T(8,128)(2,1)} %all-reduce.2.cloned.1.call-done.branch_ref, bf16[2048]{0:T(1024)(128)(2,1)} %b_dense_ref.1, bf16[2048]{0:T(1024)(128)(2,1)} %b_fc2_ref.1), custom_call_target="tpu_custom_call" | custom-call | flops 1 | bytes 1 | tf_op jit(solution)/shard_map/output/pallas_call | solution.py:650
  213.2 4.5 %collective-permute-done.15.far_ref = bf16[128,1408]{1,0:T(8,128)(2,1)S(1)} collective-permute-done((bf16[128,1408]{1,0:T(8,128)(2,1)}, bf16[128,1408]{1,0:T(8,128)(2,1)S(1)}, u32[]{:S(2)}, u32[]{:S(2)}) %collective-permute-start.15) | collective-permute-done | bytes 360480 | tf_op jit(solution)/shard_map/ppermute | solution.py:751
  217.7 0.7 copy-done.13
  218.4 2.1 down.1
  220.6 0.7 slice.38
  221.2 1.0 collective-permute-start.20
  222.3 0.1 collective-permute-start.18
  222.4 3.3 %collective-permute-start.17 = (bf16[48,2048]{1,0:T(8,128)(2,1)S(1)}, bf16[48,2048]{1,0:T(8,128)(2,1)S(1)}, u32[]{:S(2)}, u32[]{:S(2)}) collective-permute-start(bf16[48,2048]{1,0:T(8,128)(2,1)S(1)} %slice.35), channel_id=1, source_target_pairs={{0,3},{1,0},{2,1},{3,2},{4,7},{5,4},{6,5},{7,6},{8,11},{9,8},{10,9... | collective-permute-start | bytes 589832 | tf_op jit(solution)/shard_map/ppermute | solution.py:751
  225.7 1.0 collective-permute-start.16
  226.7 0.7 slice_bitcast_fusion.1
  227.4 1.2 slice_bitcast_fusion
  228.6 3.9 %place.2.refs_3_ = bf16[1024,2048]{1,0:T(8,128)(2,1)} custom-call(s32[8]{0:T(128)} %stack.103.places_ref, bf16[128,2048]{1,0:T(8,128)(2,1)} %input.1.refs_0_, bf16[128,2048]{1,0:T(8,128)(2,1)} %copy-done.5, bf16[128,2048]{1,0:T(8,128)(2,1)} %copy-done.4, bf16[128,2048]{1,0:T(8,128)(2,1)} %copy-done.3, bf16[128,2048]{1,0:T(8,128)(2,1)} %copy-done.1, ...), custom_call_target="tpu_custom_call" | custom-call | flops 1 | bytes 1 | tf_op jit(solution)/shard_map/place/pallas_call | solution.py:713
  232.6 0.7 slice_add_fusion
  233.3 1.6 collective-permute-start.23
  234.9 0.7 collective-permute-start.22
  235.6 1.3 collective-permute-start.21
  236.9 1.2 slice_bitcast_fusion.2
  238.1 2.1 up.1
  240.3 1.9 place.3
  242.2 0.5 slice_bitcast_fusion.3
  242.8 0.5 copy.29
  (77 shorter events, 0.2 us)
Async XLA Ops:
  8.0 186.9 %all-reduce.2.cloned.1.call-start = ((), (), s32[]{:S(2)}) async-start(), calls=%async_computation.4 | async-start | bytes 8388608 | tf_op jit(solution)/shard_map/psum | solution.py:894
  53.6 141.3 %reduce-scatter.5.cloned.1.call-start = ((), (), s32[]{:S(2)}) async-start(), calls=%async_computation.3 | async-start | bytes 6488064 | tf_op jit(solution)/shard_map/reduce_scatter | solution.py:838
  74.1 16.6 %collective-permute-start = (bf16[48,2048]{1,0:T(8,128)(2,1)}, bf16[48,2048]{1,0:T(8,128)(2,1)S(1)}, u32[]{:S(2)}, u32[]{:S(2)}) collective-permute-start(bf16[48,2048]{1,0:T(8,128)(2,1)} %get-tuple-element.80), channel_id=1, source_target_pairs={{0,4},{4,0},{1,5},{5,1},{2,6},{6,2},{3,7},{7,3},{8,12},{12,8},{9,1... | collective-permute-start | bytes 589832 | tf_op jit(solution)/shard_map/ppermute | solution.py:751
  76.2 14.5 %collective-permute-start.1 = (bf16[48,2048]{1,0:T(8,128)(2,1)}, bf16[48,2048]{1,0:T(8,128)(2,1)S(1)}, u32[]{:S(2)}, u32[]{:S(2)}) collective-permute-start(bf16[48,2048]{1,0:T(8,128)(2,1)} %get-tuple-element.82), channel_id=1, source_target_pairs={{0,1},{1,2},{2,3},{3,0},{4,5},{5,6},{6,7},{7,4},{8,9},{9,10},{10,1... | collective-permute-start | bytes 589832 | tf_op jit(solution)/shard_map/ppermute | solution.py:751
  77.8 12.9 %collective-permute-start.2 = (bf16[32,2048]{1,0:T(8,128)(2,1)}, bf16[32,2048]{1,0:T(8,128)(2,1)S(1)}, u32[]{:S(2)}, u32[]{:S(2)}) collective-permute-start(bf16[32,2048]{1,0:T(8,128)(2,1)} %get-tuple-element.84), channel_id=1, source_target_pairs={{0,3},{1,0},{2,1},{3,2},{4,7},{5,4},{6,5},{7,6},{8,11},{9,8},{10,9... | collective-permute-start | bytes 393224 | tf_op jit(solution)/shard_map/ppermute | solution.py:751
  90.6 0.7 copy-start.19
  90.7 0.7 copy-start.14
  90.7 0.7 copy-start.15
  94.2 1.0 copy-start.23
  94.2 14.3 %copy-start.22 = (bf16[128,2048]{1,0:T(8,128)(2,1)S(1)}, bf16[128,2048]{1,0:T(8,128)(2,1)}, u32[]{:S(2)}) copy-start(bf16[128,2048]{1,0:T(8,128)(2,1)} %get-tuple-element.94) | copy-start | bytes 1572868
  94.2 14.3 %copy-start.21 = (bf16[128,2048]{1,0:T(8,128)(2,1)S(1)}, bf16[128,2048]{1,0:T(8,128)(2,1)}, u32[]{:S(2)}) copy-start(bf16[128,2048]{1,0:T(8,128)(2,1)} %get-tuple-element.95) | copy-start | bytes 1572868
  94.3 107.9 %reduce-scatter.3.cloned.1.call-start = ((), (), s32[]{:S(2)}) async-start(), calls=%async_computation.2 | async-start | bytes 8257536 | tf_op jit(solution)/shard_map/reduce_scatter | solution.py:838
  95.3 33.8 %collective-permute-start.5 = (bf16[128,2048]{1,0:T(8,128)(2,1)S(1)}, bf16[128,2048]{1,0:T(8,128)(2,1)S(1)}, u32[]{:S(2)}, u32[]{:S(2)}) collective-permute-start(bf16[128,2048]{1,0:T(8,128)(2,1)S(1)} %copy-done.23), channel_id=1, source_target_pairs={{0,3},{1,0},{2,1},{3,2},{4,7},{5,4},{6,5},{7,6},{8,11},{9,8},{10,9... | collective-permute-start | bytes 1572872 | tf_op jit(solution)/shard_map/ppermute | solution.py:751
  108.5 20.5 %collective-permute-start.3 = (bf16[128,2048]{1,0:T(8,128)(2,1)S(1)}, bf16[128,2048]{1,0:T(8,128)(2,1)S(1)}, u32[]{:S(2)}, u32[]{:S(2)}) collective-permute-start(bf16[128,2048]{1,0:T(8,128)(2,1)S(1)} %copy-done.22), channel_id=1, source_target_pairs={{0,1},{1,2},{2,3},{3,0},{4,5},{5,6},{6,7},{7,4},{8,9},{9,10},{10,1... | collective-permute-start | bytes 1572872 | tf_op jit(solution)/shard_map/ppermute | solution.py:751
  108.5 20.6 %collective-permute-start.4 = (bf16[128,2048]{1,0:T(8,128)(2,1)S(1)}, bf16[128,2048]{1,0:T(8,128)(2,1)S(1)}, u32[]{:S(2)}, u32[]{:S(2)}) collective-permute-start(bf16[128,2048]{1,0:T(8,128)(2,1)S(1)} %copy-done.21), channel_id=1, source_target_pairs={{0,4},{4,0},{1,5},{5,1},{2,6},{6,2},{3,7},{7,3},{8,12},{12,8},{9,1... | collective-permute-start | bytes 1572872 | tf_op jit(solution)/shard_map/ppermute | solution.py:751
  129.0 0.8 copy-start.6
  129.1 0.9 copy-start.7
  129.1 1.1 copy-start.8
  133.1 1.1 copy-start.20
  133.1 4.4 %copy-start.25 = (bf16[128,2048]{1,0:T(8,128)(2,1)S(1)}, bf16[128,2048]{1,0:T(8,128)(2,1)}, u32[]{:S(2)}) copy-start(bf16[128,2048]{1,0:T(8,128)(2,1)} %get-tuple-element.102) | copy-start | bytes 1572868
  133.1 4.4 %copy-start.24 = (bf16[128,2048]{1,0:T(8,128)(2,1)S(1)}, bf16[128,2048]{1,0:T(8,128)(2,1)}, u32[]{:S(2)}) copy-start(bf16[128,2048]{1,0:T(8,128)(2,1)} %get-tuple-element.103) | copy-start | bytes 1572868
  134.2 23.1 %collective-permute-start.8 = (bf16[128,2048]{1,0:T(8,128)(2,1)S(1)}, bf16[128,2048]{1,0:T(8,128)(2,1)S(1)}, u32[]{:S(2)}, u32[]{:S(2)}) collective-permute-start(bf16[128,2048]{1,0:T(8,128)(2,1)S(1)} %copy-done.20), channel_id=1, source_target_pairs={{0,3},{1,0},{2,1},{3,2},{4,7},{5,4},{6,5},{7,6},{8,11},{9,8},{10,9... | collective-permute-start | bytes 1572872 | tf_op jit(solution)/shard_map/ppermute | solution.py:751
  137.5 23.5 %collective-permute-start.6 = (bf16[128,2048]{1,0:T(8,128)(2,1)S(1)}, bf16[128,2048]{1,0:T(8,128)(2,1)S(1)}, u32[]{:S(2)}, u32[]{:S(2)}) collective-permute-start(bf16[128,2048]{1,0:T(8,128)(2,1)S(1)} %copy-done.25), channel_id=1, source_target_pairs={{0,1},{1,2},{2,3},{3,0},{4,5},{5,6},{6,7},{7,4},{8,9},{9,10},{10,1... | collective-permute-start | bytes 1572872 | tf_op jit(solution)/shard_map/ppermute | solution.py:751
  137.6 23.5 %collective-permute-start.7 = (bf16[128,2048]{1,0:T(8,128)(2,1)S(1)}, bf16[128,2048]{1,0:T(8,128)(2,1)S(1)}, u32[]{:S(2)}, u32[]{:S(2)}) collective-permute-start(bf16[128,2048]{1,0:T(8,128)(2,1)S(1)} %copy-done.24), channel_id=1, source_target_pairs={{0,4},{4,0},{1,5},{5,1},{2,6},{6,2},{3,7},{7,3},{8,12},{12,8},{9,1... | collective-permute-start | bytes 1572872 | tf_op jit(solution)/shard_map/ppermute | solution.py:751
  157.3 3.7 %copy-start.9 = (bf16[128,2048]{1,0:T(8,128)(2,1)}, bf16[128,2048]{1,0:T(8,128)(2,1)S(1)}, u32[]{:S(2)}) copy-start(bf16[128,2048]{1,0:T(8,128)(2,1)S(1)} %collective-permute-done.8.refs_3_) | copy-start | bytes 1572868
  161.0 0.8 copy-start.10
  161.0 1.0 copy-start.11
  166.1 29.2 %collective-permute-start.11 = (bf16[128,2048]{1,0:T(8,128)(2,1)}, bf16[128,2048]{1,0:T(8,128)(2,1)S(1)}, u32[]{:S(2)}, u32[]{:S(2)}) collective-permute-start(bf16[128,2048]{1,0:T(8,128)(2,1)} %input.1.refs_0_), channel_id=1, source_target_pairs={{0,4},{4,0},{1,5},{5,1},{2,6},{6,2},{3,7},{7,3},{8,12},{12,8},{9,1... | collective-permute-start | bytes 1572872 | tf_op jit(solution)/shard_map/ppermute | solution.py:751
  166.1 29.2 %collective-permute-start.10 = (bf16[128,2048]{1,0:T(8,128)(2,1)}, bf16[128,2048]{1,0:T(8,128)(2,1)S(1)}, u32[]{:S(2)}, u32[]{:S(2)}) collective-permute-start(bf16[128,2048]{1,0:T(8,128)(2,1)} %input.1.refs_0_), channel_id=1, source_target_pairs={{0,3},{1,0},{2,1},{3,2},{4,7},{5,4},{6,5},{7,6},{8,11},{9,8},{10,9... | collective-permute-start | bytes 1572872 | tf_op jit(solution)/shard_map/ppermute | solution.py:751
  175.7 20.2 %collective-permute-start.9 = (bf16[128,2048]{1,0:T(8,128)(2,1)}, bf16[128,2048]{1,0:T(8,128)(2,1)S(1)}, u32[]{:S(2)}, u32[]{:S(2)}) collective-permute-start(bf16[128,2048]{1,0:T(8,128)(2,1)} %input.1.refs_0_), channel_id=1, source_target_pairs={{0,1},{1,2},{2,3},{3,0},{4,5},{5,6},{6,7},{7,4},{8,9},{9,10},{10,1... | collective-permute-start | bytes 1572872 | tf_op jit(solution)/shard_map/ppermute | solution.py:751
  195.3 17.9 %copy-start.3 = (bf16[128,2048]{1,0:T(8,128)(2,1)}, bf16[128,2048]{1,0:T(8,128)(2,1)S(1)}, u32[]{:S(2)}) copy-start(bf16[128,2048]{1,0:T(8,128)(2,1)S(1)} %collective-permute-done.11.refs_3_) | copy-start | bytes 1572868
  195.3 17.9 %copy-start.4 = (bf16[128,2048]{1,0:T(8,128)(2,1)}, bf16[128,2048]{1,0:T(8,128)(2,1)S(1)}, u32[]{:S(2)}) copy-start(bf16[128,2048]{1,0:T(8,128)(2,1)S(1)} %collective-permute-done.10.refs_2_) | copy-start | bytes 1572868
  195.9 17.4 %copy-start.5 = (bf16[128,2048]{1,0:T(8,128)(2,1)}, bf16[128,2048]{1,0:T(8,128)(2,1)S(1)}, u32[]{:S(2)}) copy-start(bf16[128,2048]{1,0:T(8,128)(2,1)S(1)} %collective-permute-done.9.refs_1_) | copy-start | bytes 1572868
  195.9 26.3 %collective-permute-start.14 = (bf16[128,2048]{1,0:T(8,128)(2,1)S(1)}, bf16[128,2048]{1,0:T(8,128)(2,1)S(1)}, u32[]{:S(2)}, u32[]{:S(2)}) collective-permute-start(bf16[128,2048]{1,0:T(8,128)(2,1)S(1)} %collective-permute-done.11.refs_3_), channel_id=1, source_target_pairs={{0,1},{1,2},{2,3},{3,0},{4,5},{5,6},{6,7},{7,4},{8,9},{9,10},{10,1... | collective-permute-start | bytes 1572872 | tf_op jit(solution)/shard_map/ppermute | solution.py:751
  195.9 26.3 %collective-permute-start.13 = (bf16[128,2048]{1,0:T(8,128)(2,1)S(1)}, bf16[128,2048]{1,0:T(8,128)(2,1)S(1)}, u32[]{:S(2)}, u32[]{:S(2)}) collective-permute-start(bf16[128,2048]{1,0:T(8,128)(2,1)S(1)} %collective-permute-done.10.refs_2_), channel_id=1, source_target_pairs={{0,4},{4,0},{1,5},{5,1},{2,6},{6,2},{3,7},{7,3},{8,12},{12,8},{9,1... | collective-permute-start | bytes 1572872 | tf_op jit(solution)/shard_map/ppermute | solution.py:751
  197.3 24.9 %collective-permute-start.12 = (bf16[128,2048]{1,0:T(8,128)(2,1)S(1)}, bf16[128,2048]{1,0:T(8,128)(2,1)S(1)}, u32[]{:S(2)}, u32[]{:S(2)}) collective-permute-start(bf16[128,2048]{1,0:T(8,128)(2,1)S(1)} %collective-permute-done.10.refs_2_), channel_id=1, source_target_pairs={{0,3},{1,0},{2,1},{3,2},{4,7},{5,4},{6,5},{7,6},{8,11},{9,8},{10,9... | collective-permute-start | bytes 1572872 | tf_op jit(solution)/shard_map/ppermute | solution.py:751
  202.2 15.5 %collective-permute-start.15 = (bf16[128,1408]{1,0:T(8,128)(2,1)}, bf16[128,1408]{1,0:T(8,128)(2,1)S(1)}, u32[]{:S(2)}, u32[]{:S(2)}) collective-permute-start(bf16[128,1408]{1,0:T(8,128)(2,1)} %slice.33), channel_id=1, source_target_pairs={{0,64},{64,0},{1,65},{65,1},{2,66},{66,2},{3,67},{67,3},{4,68},{68... | collective-permute-start | bytes 1081352 | tf_op jit(solution)/shard_map/ppermute | solution.py:751
  203.3 29.3 %collective-permute-start.19 = (bf16[128,1792]{1,0:T(8,128)(2,1)S(1)}, bf16[128,1792]{1,0:T(8,128)(2,1)S(1)}, u32[]{:S(2)}, u32[]{:S(2)}) collective-permute-start(bf16[128,1792]{1,0:T(8,128)(2,1)S(1)} %slice.37), channel_id=1, source_target_pairs={{0,64},{64,0},{1,65},{65,1},{2,66},{66,2},{3,67},{67,3},{4,68},{68... | collective-permute-start | bytes 1376264 | tf_op jit(solution)/shard_map/ppermute | solution.py:751
  217.7 0.7 copy-start.13
  221.2 11.4 %collective-permute-start.20 = (f32[2,128]{1,0:T(2,128)S(1)}, f32[2,128]{1,0:T(2,128)S(1)}, u32[]{:S(2)}, u32[]{:S(2)}) collective-permute-start(f32[2,128]{1,0:T(2,128)S(1)} %slice.38), channel_id=1, source_target_pairs={{0,4},{4,0},{1,5},{5,1},{2,6},{6,2},{3,7},{7,3},{8,12},{12,8},{9,1... | collective-permute-start | bytes 3080 | tf_op jit(solution)/shard_map/ppermute | solution.py:751
  222.2 6.4 %copy-start.2 = (bf16[128,2048]{1,0:T(8,128)(2,1)}, bf16[128,2048]{1,0:T(8,128)(2,1)S(1)}, u32[]{:S(2)}) copy-start(bf16[128,2048]{1,0:T(8,128)(2,1)S(1)} %collective-permute-done.14.refs_6_) | copy-start | bytes 1572868
  222.2 6.4 %copy-start = (bf16[128,2048]{1,0:T(8,128)(2,1)}, bf16[128,2048]{1,0:T(8,128)(2,1)S(1)}, u32[]{:S(2)}) copy-start(bf16[128,2048]{1,0:T(8,128)(2,1)S(1)} %collective-permute-done.13.refs_5_) | copy-start | bytes 1572868
  222.2 6.4 %copy-start.1 = (bf16[128,2048]{1,0:T(8,128)(2,1)}, bf16[128,2048]{1,0:T(8,128)(2,1)S(1)}, u32[]{:S(2)}) copy-start(bf16[128,2048]{1,0:T(8,128)(2,1)S(1)} %collective-permute-done.12.refs_4_) | copy-start | bytes 1572868
  222.3 10.2 %collective-permute-start.18 = (bf16[32,2048]{1,0:T(8,128)(2,1)S(1)}, bf16[32,2048]{1,0:T(8,128)(2,1)S(1)}, u32[]{:S(2)}, u32[]{:S(2)}) collective-permute-start(bf16[32,2048]{1,0:T(8,128)(2,1)S(1)} %slice.36), channel_id=1, source_target_pairs={{0,1},{1,2},{2,3},{3,0},{4,5},{5,6},{6,7},{7,4},{8,9},{9,10},{10,1... | collective-permute-start | bytes 393224 | tf_op jit(solution)/shard_map/ppermute | solution.py:751
  222.4 10.1 %collective-permute-start.17 = (bf16[48,2048]{1,0:T(8,128)(2,1)S(1)}, bf16[48,2048]{1,0:T(8,128)(2,1)S(1)}, u32[]{:S(2)}, u32[]{:S(2)}) collective-permute-start(bf16[48,2048]{1,0:T(8,128)(2,1)S(1)} %slice.35), channel_id=1, source_target_pairs={{0,3},{1,0},{2,1},{3,2},{4,7},{5,4},{6,5},{7,6},{8,11},{9,8},{10,9... | collective-permute-start | bytes 589832 | tf_op jit(solution)/shard_map/ppermute | solution.py:751
  225.7 6.9 %collective-permute-start.16 = (bf16[48,2048]{1,0:T(8,128)(2,1)S(1)}, bf16[48,2048]{1,0:T(8,128)(2,1)S(1)}, u32[]{:S(2)}, u32[]{:S(2)}) collective-permute-start(bf16[48,2048]{1,0:T(8,128)(2,1)S(1)} %slice.34), channel_id=1, source_target_pairs={{0,4},{4,0},{1,5},{5,1},{2,6},{6,2},{3,7},{7,3},{8,12},{12,8},{9,1... | collective-permute-start | bytes 589832 | tf_op jit(solution)/shard_map/ppermute | solution.py:751
  227.4 15.4 %copy-start.26 = (f32[128]{0:T(128)}, f32[128]{0:T(128)S(1)}, u32[]{:S(2)}) copy-start(f32[128]{0:T(128)S(1)} %slice_bitcast_fusion.1) | copy-start | bytes 1540
  232.5 7.7 %copy-start.18 = (bf16[32,2048]{1,0:T(8,128)(2,1)}, bf16[32,2048]{1,0:T(8,128)(2,1)S(1)}, u32[]{:S(2)}) copy-start(bf16[32,2048]{1,0:T(8,128)(2,1)S(1)} %collective-permute-done.18.refs_2_) | copy-start | bytes 393220
  232.5 7.7 %copy-start.16 = (bf16[48,2048]{1,0:T(8,128)(2,1)}, bf16[48,2048]{1,0:T(8,128)(2,1)S(1)}, u32[]{:S(2)}) copy-start(bf16[48,2048]{1,0:T(8,128)(2,1)S(1)} %collective-permute-done.17.refs_1_) | copy-start | bytes 589828
  232.6 7.7 %copy-start.17 = (bf16[48,2048]{1,0:T(8,128)(2,1)}, bf16[48,2048]{1,0:T(8,128)(2,1)S(1)}, u32[]{:S(2)}) copy-start(bf16[48,2048]{1,0:T(8,128)(2,1)S(1)} %collective-permute-done.16.refs_0_) | copy-start | bytes 589828
  232.6 5.5 %copy-start.12 = (bf16[128,1792]{1,0:T(8,128)(2,1)}, bf16[128,1792]{1,0:T(8,128)(2,1)S(1)}, u32[]{:S(2)}) copy-start(bf16[128,1792]{1,0:T(8,128)(2,1)S(1)} %collective-permute-done.19.far_ref) | copy-start | bytes 1376260
  233.3 8.9 %collective-permute-start.23 = (f32[2,128]{1,0:T(2,128)S(1)}, f32[2,128]{1,0:T(2,128)S(1)}, u32[]{:S(2)}, u32[]{:S(2)}) collective-permute-start(f32[2,128]{1,0:T(2,128)S(1)} %slice_add_fusion), channel_id=1, source_target_pairs={{0,2},{1,3},{2,0},{3,1},{4,6},{5,7},{6,4},{7,5},{8,10},{9,11},{10,... | collective-permute-start | bytes 3080 | tf_op jit(solution)/shard_map/ppermute | solution.py:751
  234.9 7.3 %collective-permute-start.22 = (f32[2,128]{1,0:T(2,128)S(1)}, f32[2,128]{1,0:T(2,128)S(1)}, u32[]{:S(2)}, u32[]{:S(2)}) collective-permute-start(f32[2,128]{1,0:T(2,128)S(1)} %slice_add_fusion), channel_id=1, source_target_pairs={{0,3},{1,0},{2,1},{3,2},{4,7},{5,4},{6,5},{7,6},{8,11},{9,8},{10,9... | collective-permute-start | bytes 3080 | tf_op jit(solution)/shard_map/ppermute | solution.py:751
  235.6 6.6 %collective-permute-start.21 = (f32[2,128]{1,0:T(2,128)S(1)}, f32[2,128]{1,0:T(2,128)S(1)}, u32[]{:S(2)}, u32[]{:S(2)}) collective-permute-start(f32[2,128]{1,0:T(2,128)S(1)} %slice_add_fusion), channel_id=1, source_target_pairs={{0,1},{1,2},{2,3},{3,0},{4,5},{5,6},{6,7},{7,4},{8,9},{9,10},{10,1... | collective-permute-start | bytes 3080 | tf_op jit(solution)/shard_map/ppermute | solution.py:751
Sparse Core Ops, SparseCore 0:
  53.7 141.1 all-reduce.1
Sparse Core Ops, SparseCore 1:
  94.3 56.4 reduce-scatter.4
  153.1 47.0 reduce-scatter.2

commit v4 on v2

--- a/solution.py
+++ b/solution.py
@@ -909,15 +909,15 @@
     input_grad = TensorGather(places, rows)
     down.send((rows, branch_sum))
     done = input_grad.second(down.near)
+    output = finish_output(after(seq_lengths, done), tokens, branch_sum, b_dense, b_fc2)
     grad_fc2, grad_dense, small = down.finish(
         down_kernel,
         "down",
         ((units, BLOCK), (w_dense.shape[0], BLOCK), (8, BLOCK)),
-        done,
+        output,
     )
     norm_sum = small[:2]
     norm_across = across(norm_sum)
-    output = finish_output(after(seq_lengths, small), tokens, branch_sum, b_dense, b_fc2)
     up.send(output)
     input_grad.third((output, up.near))
     *three, up.far = after([*input_grad.three, up.far], input_grad.whole)

time: 251 us -> 251 us (level)
  waiting for transfers between devices: 55.3 us -> 47.6 us
  local copies, waits for them, and re-layouts: 11.6 us -> 15 us
  starting transfers between devices: 52.3 us -> 55.2 us
    ppermute x24, waiting for transfers between devices: 35.3 us -> 28.2 us  [shift(): lax.ppermute(array, axis, [(i, (i + by) % size) for i in range(size)])]
    ppermute x24, starting transfers between devices: 52.2 us -> 55.1 us  [shift(): lax.ppermute(array, axis, [(i, (i + by) % size) for i in range(size)])]
    unnamed x57 -> x55, local copies, waits for them, and re-layouts: 6.1 us -> 6.1 us
  transfers between devices with their start and end apart: 27 -> 27, of which waited for: 5 -> 5; matrix products, arithmetic and copies ran while one was open for 2% -> 3% of each run, Pallas kernels for 28% -> 28%
where the time goes in v4:
time: 251 us; the launch traced here: 249 us
  Pallas kernels  115 us (46%)
  starting transfers between devices  55.2 us (22%)
  waiting for transfers between devices  47.6 us (19%)
  between operations  15.9 us (6%)
  local copies, waits for them, and re-layouts  15 us (6%)
    ppermute x24, starting transfers between devices, shift(): lax.ppermute(array, axis, [(i, (i + by) % size) for i in range(size)])  55.1 us
    pallas_call x1, Pallas kernels, forward(): kernel_call(forward_kernel, 'forward', [made(slot_len, columns) for colum...  44.2 us
    ppermute x24, waiting for transfers between devices, shift(): lax.ppermute(array, axis, [(i, (i + by) % size) for i in range(size)])  28.2 us
    pallas_call x2, Pallas kernels, weight_blocks(): kernel_call(weight_kernel, 'weights', made(left.shape[1], width), prefetc...  24.2 us
    pallas_call x1, Pallas kernels, backward(): kernel_call(backward_kernel, 'backward', sums + [made(slot_len, units)] +...  20.4 us
    psum x1, waiting for transfers between devices, per_device(): branch_sum = lax.psum(branch_part, TENSOR)  19.3 us
    pallas_call x1, Pallas kernels, finish_output(): kernel_call(output_kernel, 'output', made(slot_len, width), grid=(slot_le...  6.36 us
    unnamed x55, local copies, waits for them, and re-layouts  6.1 us
  transfers between devices with their start and end apart: 27, of which 5 were waited for; matrix products, arithmetic and copies ran while one was open for 3% of the time, Pallas kernels for 28%

profile of v4, /device:TPU:0, one launch (start us, length us, event | category | flops | bytes accessed | tf_op | source)
XLA Modules:
  0.0 249.5 jit_solution(18345653203799834663)
XLA Ops:
  8.0 0.0 all-reduce.2.cloned.1.call-start
  8.1 0.6 broadcast_in_dim_tile.3.freq_ref
  8.7 0.6 stack.86.places_ref
  9.4 44.2 %forward.1 = (bf16[1024,2048]{1,0:T(8,128)(2,1)}, bf16[1024,2048]{1,0:T(8,128)(2,1)}, bf16[1024,1024]{1,0:T(8,128)(2,1)}, bf16[1024,1024]{1,0:T(8,128)(2,1)}, bf...) custom-call(s32[1,8]{1,0:T(1,128)} %lengths_ref.2, ...), custom_call_target="tpu_custom_call" | custom-call | flops 1 | bytes 1 | tf_op jit(solution)/shard_map/forward/pallas_call | solution.py:392
  53.6 0.0 reduce-scatter.3.cloned.1.call-start
  53.7 20.4 %backward.1 = (f32[32,128]{1,0:T(8,128)}, f32[16,128]{1,0:T(8,128)}, f32[16,128]{1,0:T(8,128)}, f32[16,128]{1,0:T(8,128)}, bf16[1024,1024]{1,0:T(8,128)(2,1)}, /...) custom-call(s32[8]{0:T(128)} %stack.86.places_ref, ...), custom_call_target="tpu_custom_call" | custom-call | flops 1 | bytes 1 | tf_op jit(solution)/shard_map/backward/pallas_call | solution.py:540
  74.1 2.1 collective-permute-start
  76.2 1.6 collective-permute-start.1
  77.8 1.7 collective-permute-start.2
  79.4 0.6 stack.103.order_ref
  80.0 10.6 %weights.2 = bf16[2048,1408]{1,0:T(8,128)(2,1)} custom-call(s32[16]{0:T(128)} %stack.103.order_ref, bf16[1024,2048]{1,0:T(8,128)(2,1)} %get-tuple-element.75.grad_hbm.refs_0_.refs_1_.refs_2_.refs_3_, bf16[1024,2048]{1,0:T(8,128)(2,1)} %get-tuple-element.75.grad_hbm.refs_0_.refs_1_.refs_2_.refs_3_, ...), custom_call_target="tpu_custom_call" | custom-call | flops 1 | bytes 1 | tf_op jit(solution)/shard_map/weights/pallas_call | solution.py:578
  90.7 0.6 copy-done.19
  91.3 0.1 copy-done.14
  91.4 0.1 copy-done.15
  91.4 2.8 %middle.1 = (bf16[128,2048]{1,0:T(8,128)(2,1)}, bf16[128,2048]{1,0:T(8,128)(2,1)}, bf16[128,2048]{1,0:T(8,128)(2,1)}) custom-call(bf16[128,2048]{1,0:T(8,128)(2,1)} %get-tuple-element.80.refs_0_, bf16[48,2048]{1,0:T(8,128)(2,1)} %copy-done.14, bf16[128,2048]{1,0:T(8,128)(2,1)} %get-tuple-element.82.refs_2_, bf16[48,2048]{1,0:T(8,128)(2,1)} %copy-done.15, ...), custom_call_target="tpu_custom_call" | custom-call | flops 1 | bytes 1 | tf_op jit(solution)/shard_map/middle/pallas_call | solution.py:623
  94.2 0.0 reduce-scatter.3.cloned.1.call-update
  94.3 0.0 reduce-scatter.5.cloned.1.call-start
  94.3 1.0 copy-done.23
  95.3 13.2 %collective-permute-start.5 = (bf16[128,2048]{1,0:T(8,128)(2,1)S(1)}, bf16[128,2048]{1,0:T(8,128)(2,1)S(1)}, u32[]{:S(2)}, u32[]{:S(2)}) collective-permute-start(bf16[128,2048]{1,0:T(8,128)(2,1)S(1)} %copy-done.23), channel_id=1, source_target_pairs={{0,3},{1,0},{2,1},{3,2},{4,7},{5,4},{6,5},{7,6},{8,11},{9,8},{10,9... | collective-permute-start | bytes 1572872 | tf_op jit(solution)/shard_map/ppermute | solution.py:751
  108.5 7.0 %collective-permute-start.4 = (bf16[128,2048]{1,0:T(8,128)(2,1)S(1)}, bf16[128,2048]{1,0:T(8,128)(2,1)S(1)}, u32[]{:S(2)}, u32[]{:S(2)}) collective-permute-start(bf16[128,2048]{1,0:T(8,128)(2,1)S(1)} %copy-done.21), channel_id=1, source_target_pairs={{0,4},{4,0},{1,5},{5,1},{2,6},{6,2},{3,7},{7,3},{8,12},{12,8},{9,1... | collective-permute-start | bytes 1572872 | tf_op jit(solution)/shard_map/ppermute | solution.py:751
  115.5 13.5 %weights.3 = bf16[2048,1792]{1,0:T(8,128)(2,1)} custom-call(s32[16]{0:T(128)} %stack.103.order_ref, bf16[1024,2048]{1,0:T(8,128)(2,1)} %get-tuple-element.100.refs_0_.refs_1_.refs_2_.refs_3_, bf16[1024,2048]{1,0:T(8,128)(2,1)} %get-tuple-element.100.refs_0_.refs_1_.refs_2_.refs_3_, bf16[1024,2048]{1,0:T(8,128)(2,1)} %get-tuple-element.100.refs_0_.refs_1_.refs_2_.refs_3_, ...), custom_call_target="tpu_custom_call" | custom-call | flops 1 | bytes 1 | tf_op jit(solution)/shard_map/weights/pallas_call | solution.py:578
  129.1 0.7 copy-done.6
  129.8 0.2 copy-done.7
  130.0 0.2 copy-done.8
  130.2 3.0 %near.1 = (bf16[128,2048]{1,0:T(8,128)(2,1)}, bf16[128,2048]{1,0:T(8,128)(2,1)}) custom-call(bf16[128,2048]{1,0:T(8,128)(2,1)} %get-tuple-element.79.refs_0_, bf16[128,2048]{1,0:T(8,128)(2,1)} %copy-done.7, bf16[128,2048]{1,0:T(8,128)(2,1)} %copy-done.8, bf16[128,2048]{1,0:T(8,128)(2,1)} %get-tuple-element.97.refs_3_, bf16[128,2048]{1,0:T(8,128)(2,1)} %copy-done.6), custom_call_target="tpu_custom_call" | custom-call | flops 1 | bytes 1 | tf_op jit(solution)/shard_map/near/pallas_call | solution.py:623
  133.2 0.0 reduce-scatter.5.cloned.1.call-update
  133.2 1.0 copy-done.20
  134.2 3.3 %collective-permute-start.8 = (bf16[128,2048]{1,0:T(8,128)(2,1)S(1)}, bf16[128,2048]{1,0:T(8,128)(2,1)S(1)}, u32[]{:S(2)}, u32[]{:S(2)}) collective-permute-start(bf16[128,2048]{1,0:T(8,128)(2,1)S(1)} %copy-done.20), channel_id=1, source_target_pairs={{0,3},{1,0},{2,1},{3,2},{4,7},{5,4},{6,5},{7,6},{8,11},{9,8},{10,9... | collective-permute-start | bytes 1572872 | tf_op jit(solution)/shard_map/ppermute | solution.py:751
  137.6 0.1 collective-permute-start.7
  137.7 19.7 %collective-permute-done.8.refs_3_ = bf16[128,2048]{1,0:T(8,128)(2,1)S(1)} collective-permute-done((bf16[128,2048]{1,0:T(8,128)(2,1)S(1)}, bf16[128,2048]{1,0:T(8,128)(2,1)S(1)}, u32[]{:S(2)}, u32[]{:S(2)}) %collective-permute-start.8) | collective-permute-done | bytes 524320 | tf_op jit(solution)/shard_map/ppermute | solution.py:751
  157.3 3.7 %collective-permute-done.6.refs_1_ = bf16[128,2048]{1,0:T(8,128)(2,1)S(1)} collective-permute-done((bf16[128,2048]{1,0:T(8,128)(2,1)S(1)}, bf16[128,2048]{1,0:T(8,128)(2,1)S(1)}, u32[]{:S(2)}, u32[]{:S(2)}) %collective-permute-start.6) | collective-permute-done | bytes 524320 | tf_op jit(solution)/shard_map/ppermute | solution.py:751
  161.0 0.8 copy-done.10
  161.8 0.2 copy-done.11
  162.0 4.1 %input.1.refs_0_ = bf16[128,2048]{1,0:T(8,128)(2,1)} custom-call(s32[8]{0:T(128)} %stack.86.places_ref, bf16[128,2048]{1,0:T(8,128)(2,1)} %get-tuple-element.105.refs_0_, bf16[128,2048]{1,0:T(8,128)(2,1)} %copy-done.10, bf16[128,2048]{1,0:T(8,128)(2,1)} %copy-done.11, bf16[128,2048]{1,0:T(8,128)(2,1)} %copy-done.9, bf16[1024,2048]{1,0:T(8,128)(2,1)} %tokens_ref.1, ...), custom_call_target="tpu_custom_call" | custom-call | flops 1 | bytes 1 | tf_op jit(solution)/shard_map/input/pallas_call | solution.py:683
  166.1 9.5 %collective-permute-start.10 = (bf16[128,2048]{1,0:T(8,128)(2,1)}, bf16[128,2048]{1,0:T(8,128)(2,1)S(1)}, u32[]{:S(2)}, u32[]{:S(2)}) collective-permute-start(bf16[128,2048]{1,0:T(8,128)(2,1)} %input.1.refs_0_), channel_id=1, source_target_pairs={{0,3},{1,0},{2,1},{3,2},{4,7},{5,4},{6,5},{7,6},{8,11},{9,8},{10,9... | collective-permute-start | bytes 1572872 | tf_op jit(solution)/shard_map/ppermute | solution.py:751
  175.7 19.3 %all-reduce.2.cloned.1.call-done.branch_ref = bf16[1024,2048]{1,0:T(8,128)(2,1)} async-done(((bf16[1024,2048]{1,0:T(8,128)(2,1)}), bf16[1024,2048]{1,0:T(8,128)(2,1)}) %all-reduce.2.cloned.1.call-update) | async-done | bytes 4194320 | tf_op jit(solution)/shard_map/psum | solution.py:894
  194.9 1.7 slice.37
  196.7 1.6 collective-permute-start.19
  198.4 0.1 collective-permute-start.14
  198.5 0.6 collective-permute-start.13
  199.1 3.1 %collective-permute-start.12 = (bf16[128,2048]{1,0:T(8,128)(2,1)S(1)}, bf16[128,2048]{1,0:T(8,128)(2,1)S(1)}, u32[]{:S(2)}, u32[]{:S(2)}) collective-permute-start(bf16[128,2048]{1,0:T(8,128)(2,1)S(1)} %collective-permute-done.10.refs_2_), channel_id=1, source_target_pairs={{0,3},{1,0},{2,1},{3,2},{4,7},{5,4},{6,5},{7,6},{8,11},{9,8},{10,9... | collective-permute-start | bytes 1572872 | tf_op jit(solution)/shard_map/ppermute | solution.py:751
  202.2 6.4 %output.1 = bf16[1024,2048]{1,0:T(8,128)(2,1)} custom-call(s32[1,8]{1,0:T(1,128)} %lengths_ref.2, bf16[1024,2048]{1,0:T(8,128)(2,1)} %tokens_ref.1, bf16[1024,2048]{1,0:T(8,128)(2,1)} %all-reduce.2.cloned.1.call-done.branch_ref, bf16[2048]{0:T(1024)(128)(2,1)} %b_dense_ref.1, bf16[2048]{0:T(1024)(128)(2,1)} %b_fc2_ref.1), custom_call_target="tpu_custom_call" | custom-call | flops 1 | bytes 1 | tf_op jit(solution)/shard_map/output/pallas_call | solution.py:650
  208.6 0.0 reduce-scatter.5.cloned.1.call-done.near_ref
  208.6 1.1 slice.36
  209.7 4.2 %collective-permute-start.18 = (bf16[128,1792]{1,0:T(8,128)(2,1)S(1)}, bf16[128,1792]{1,0:T(8,128)(2,1)S(1)}, u32[]{:S(2)}, u32[]{:S(2)}) collective-permute-start(bf16[128,1792]{1,0:T(8,128)(2,1)S(1)} %slice.36), channel_id=1, source_target_pairs={{0,64},{64,0},{1,65},{65,1},{2,66},{66,2},{3,67},{67,3},{4,68},{68... | collective-permute-start | bytes 1376264 | tf_op jit(solution)/shard_map/ppermute | solution.py:751
  213.9 0.7 copy-done.13
  214.6 2.1 down.1
  216.8 0.7 slice.38
  217.4 0.7 slice_bitcast_fusion.1
  218.1 1.4 collective-permute-done.13.refs_5_
  219.5 0.1 collective-permute-start.17
  219.7 3.3 %collective-permute-start.16 = (bf16[48,2048]{1,0:T(8,128)(2,1)S(1)}, bf16[48,2048]{1,0:T(8,128)(2,1)S(1)}, u32[]{:S(2)}, u32[]{:S(2)}) collective-permute-start(bf16[48,2048]{1,0:T(8,128)(2,1)S(1)} %slice.34), channel_id=1, source_target_pairs={{0,3},{1,0},{2,1},{3,2},{4,7},{5,4},{6,5},{7,6},{8,11},{9,8},{10,9... | collective-permute-start | bytes 589832 | tf_op jit(solution)/shard_map/ppermute | solution.py:751
  223.0 1.5 collective-permute-start.15
  224.5 1.2 slice_bitcast_fusion
  225.7 3.9 %place.2.refs_3_ = bf16[1024,2048]{1,0:T(8,128)(2,1)} custom-call(s32[8]{0:T(128)} %stack.86.places_ref, bf16[128,2048]{1,0:T(8,128)(2,1)} %input.1.refs_0_, bf16[128,2048]{1,0:T(8,128)(2,1)} %copy-done.5, bf16[128,2048]{1,0:T(8,128)(2,1)} %copy-done.4, bf16[128,2048]{1,0:T(8,128)(2,1)} %copy-done.3, bf16[128,2048]{1,0:T(8,128)(2,1)} %copy-done.1, ...), custom_call_target="tpu_custom_call" | custom-call | flops 1 | bytes 1 | tf_op jit(solution)/shard_map/place/pallas_call | solution.py:713
  229.6 3.4 %collective-permute-done.15.refs_0_ = bf16[48,2048]{1,0:T(8,128)(2,1)S(1)} collective-permute-done((bf16[48,2048]{1,0:T(8,128)(2,1)S(1)}, bf16[48,2048]{1,0:T(8,128)(2,1)S(1)}, u32[]{:S(2)}, u32[]{:S(2)}) %collective-permute-start.15) | collective-permute-done | bytes 196640 | tf_op jit(solution)/shard_map/ppermute | solution.py:751
  233.0 0.7 slice_add_fusion
  233.7 1.7 collective-permute-start.22
  235.4 0.3 collective-permute-start.21
  235.7 1.2 slice_bitcast_fusion.2
  236.9 2.1 up.1
  239.1 1.9 place.3
  241.0 0.5 slice_bitcast_fusion.3
  241.6 0.5 copy.29
  (77 shorter events, 0.2 us)
Async XLA Ops:
  8.0 186.9 %all-reduce.2.cloned.1.call-start = ((), (), s32[]{:S(2)}) async-start(), calls=%async_computation.3 | async-start | bytes 8388608 | tf_op jit(solution)/shard_map/psum | solution.py:894
  53.6 141.3 %reduce-scatter.3.cloned.1.call-start = ((), (), s32[]{:S(2)}) async-start(), calls=%async_computation.2 | async-start | bytes 6488064 | tf_op jit(solution)/shard_map/reduce_scatter | solution.py:838
  74.1 16.6 %collective-permute-start = (bf16[48,2048]{1,0:T(8,128)(2,1)}, bf16[48,2048]{1,0:T(8,128)(2,1)S(1)}, u32[]{:S(2)}, u32[]{:S(2)}) collective-permute-start(bf16[48,2048]{1,0:T(8,128)(2,1)} %get-tuple-element.81), channel_id=1, source_target_pairs={{0,4},{4,0},{1,5},{5,1},{2,6},{6,2},{3,7},{7,3},{8,12},{12,8},{9,1... | collective-permute-start | bytes 589832 | tf_op jit(solution)/shard_map/ppermute | solution.py:751
  76.2 14.5 %collective-permute-start.1 = (bf16[48,2048]{1,0:T(8,128)(2,1)}, bf16[48,2048]{1,0:T(8,128)(2,1)S(1)}, u32[]{:S(2)}, u32[]{:S(2)}) collective-permute-start(bf16[48,2048]{1,0:T(8,128)(2,1)} %get-tuple-element.83), channel_id=1, source_target_pairs={{0,1},{1,2},{2,3},{3,0},{4,5},{5,6},{6,7},{7,4},{8,9},{9,10},{10,1... | collective-permute-start | bytes 589832 | tf_op jit(solution)/shard_map/ppermute | solution.py:751
  77.8 12.9 %collective-permute-start.2 = (bf16[32,2048]{1,0:T(8,128)(2,1)}, bf16[32,2048]{1,0:T(8,128)(2,1)S(1)}, u32[]{:S(2)}, u32[]{:S(2)}) collective-permute-start(bf16[32,2048]{1,0:T(8,128)(2,1)} %get-tuple-element.85), channel_id=1, source_target_pairs={{0,3},{1,0},{2,1},{3,2},{4,7},{5,4},{6,5},{7,6},{8,11},{9,8},{10,9... | collective-permute-start | bytes 393224 | tf_op jit(solution)/shard_map/ppermute | solution.py:751
  90.6 0.7 copy-start.19
  90.7 0.7 copy-start.14
  90.7 0.7 copy-start.15
  94.2 1.0 copy-start.23
  94.2 14.3 %copy-start.22 = (bf16[128,2048]{1,0:T(8,128)(2,1)S(1)}, bf16[128,2048]{1,0:T(8,128)(2,1)}, u32[]{:S(2)}) copy-start(bf16[128,2048]{1,0:T(8,128)(2,1)} %get-tuple-element.95) | copy-start | bytes 1572868
  94.2 14.3 %copy-start.21 = (bf16[128,2048]{1,0:T(8,128)(2,1)S(1)}, bf16[128,2048]{1,0:T(8,128)(2,1)}, u32[]{:S(2)}) copy-start(bf16[128,2048]{1,0:T(8,128)(2,1)} %get-tuple-element.96) | copy-start | bytes 1572868
  94.3 114.4 %reduce-scatter.5.cloned.1.call-start = ((), (), s32[]{:S(2)}) async-start(), calls=%async_computation.4 | async-start | bytes 8257536 | tf_op jit(solution)/shard_map/reduce_scatter | solution.py:838
  95.3 33.8 %collective-permute-start.5 = (bf16[128,2048]{1,0:T(8,128)(2,1)S(1)}, bf16[128,2048]{1,0:T(8,128)(2,1)S(1)}, u32[]{:S(2)}, u32[]{:S(2)}) collective-permute-start(bf16[128,2048]{1,0:T(8,128)(2,1)S(1)} %copy-done.23), channel_id=1, source_target_pairs={{0,3},{1,0},{2,1},{3,2},{4,7},{5,4},{6,5},{7,6},{8,11},{9,8},{10,9... | collective-permute-start | bytes 1572872 | tf_op jit(solution)/shard_map/ppermute | solution.py:751
  108.5 20.5 %collective-permute-start.3 = (bf16[128,2048]{1,0:T(8,128)(2,1)S(1)}, bf16[128,2048]{1,0:T(8,128)(2,1)S(1)}, u32[]{:S(2)}, u32[]{:S(2)}) collective-permute-start(bf16[128,2048]{1,0:T(8,128)(2,1)S(1)} %copy-done.22), channel_id=1, source_target_pairs={{0,1},{1,2},{2,3},{3,0},{4,5},{5,6},{6,7},{7,4},{8,9},{9,10},{10,1... | collective-permute-start | bytes 1572872 | tf_op jit(solution)/shard_map/ppermute | solution.py:751
  108.5 20.6 %collective-permute-start.4 = (bf16[128,2048]{1,0:T(8,128)(2,1)S(1)}, bf16[128,2048]{1,0:T(8,128)(2,1)S(1)}, u32[]{:S(2)}, u32[]{:S(2)}) collective-permute-start(bf16[128,2048]{1,0:T(8,128)(2,1)S(1)} %copy-done.21), channel_id=1, source_target_pairs={{0,4},{4,0},{1,5},{5,1},{2,6},{6,2},{3,7},{7,3},{8,12},{12,8},{9,1... | collective-permute-start | bytes 1572872 | tf_op jit(solution)/shard_map/ppermute | solution.py:751
  129.0 0.8 copy-start.6
  129.1 0.9 copy-start.7
  129.1 1.1 copy-start.8
  133.1 1.1 copy-start.20
  133.1 4.4 %copy-start.25 = (bf16[128,2048]{1,0:T(8,128)(2,1)S(1)}, bf16[128,2048]{1,0:T(8,128)(2,1)}, u32[]{:S(2)}) copy-start(bf16[128,2048]{1,0:T(8,128)(2,1)} %get-tuple-element.102) | copy-start | bytes 1572868
  133.1 4.4 %copy-start.24 = (bf16[128,2048]{1,0:T(8,128)(2,1)S(1)}, bf16[128,2048]{1,0:T(8,128)(2,1)}, u32[]{:S(2)}) copy-start(bf16[128,2048]{1,0:T(8,128)(2,1)} %get-tuple-element.103) | copy-start | bytes 1572868
  134.2 23.1 %collective-permute-start.8 = (bf16[128,2048]{1,0:T(8,128)(2,1)S(1)}, bf16[128,2048]{1,0:T(8,128)(2,1)S(1)}, u32[]{:S(2)}, u32[]{:S(2)}) collective-permute-start(bf16[128,2048]{1,0:T(8,128)(2,1)S(1)} %copy-done.20), channel_id=1, source_target_pairs={{0,3},{1,0},{2,1},{3,2},{4,7},{5,4},{6,5},{7,6},{8,11},{9,8},{10,9... | collective-permute-start | bytes 1572872 | tf_op jit(solution)/shard_map/ppermute | solution.py:751
  137.5 23.5 %collective-permute-start.6 = (bf16[128,2048]{1,0:T(8,128)(2,1)S(1)}, bf16[128,2048]{1,0:T(8,128)(2,1)S(1)}, u32[]{:S(2)}, u32[]{:S(2)}) collective-permute-start(bf16[128,2048]{1,0:T(8,128)(2,1)S(1)} %copy-done.25), channel_id=1, source_target_pairs={{0,1},{1,2},{2,3},{3,0},{4,5},{5,6},{6,7},{7,4},{8,9},{9,10},{10,1... | collective-permute-start | bytes 1572872 | tf_op jit(solution)/shard_map/ppermute | solution.py:751
  137.6 23.5 %collective-permute-start.7 = (bf16[128,2048]{1,0:T(8,128)(2,1)S(1)}, bf16[128,2048]{1,0:T(8,128)(2,1)S(1)}, u32[]{:S(2)}, u32[]{:S(2)}) collective-permute-start(bf16[128,2048]{1,0:T(8,128)(2,1)S(1)} %copy-done.24), channel_id=1, source_target_pairs={{0,4},{4,0},{1,5},{5,1},{2,6},{6,2},{3,7},{7,3},{8,12},{12,8},{9,1... | collective-permute-start | bytes 1572872 | tf_op jit(solution)/shard_map/ppermute | solution.py:751
  157.3 3.7 %copy-start.9 = (bf16[128,2048]{1,0:T(8,128)(2,1)}, bf16[128,2048]{1,0:T(8,128)(2,1)S(1)}, u32[]{:S(2)}) copy-start(bf16[128,2048]{1,0:T(8,128)(2,1)S(1)} %collective-permute-done.8.refs_3_) | copy-start | bytes 1572868
  161.0 0.8 copy-start.10
  161.0 1.0 copy-start.11
  166.1 32.2 %collective-permute-start.11 = (bf16[128,2048]{1,0:T(8,128)(2,1)}, bf16[128,2048]{1,0:T(8,128)(2,1)S(1)}, u32[]{:S(2)}, u32[]{:S(2)}) collective-permute-start(bf16[128,2048]{1,0:T(8,128)(2,1)} %input.1.refs_0_), channel_id=1, source_target_pairs={{0,4},{4,0},{1,5},{5,1},{2,6},{6,2},{3,7},{7,3},{8,12},{12,8},{9,1... | collective-permute-start | bytes 1572872 | tf_op jit(solution)/shard_map/ppermute | solution.py:751
  166.1 32.2 %collective-permute-start.10 = (bf16[128,2048]{1,0:T(8,128)(2,1)}, bf16[128,2048]{1,0:T(8,128)(2,1)S(1)}, u32[]{:S(2)}, u32[]{:S(2)}) collective-permute-start(bf16[128,2048]{1,0:T(8,128)(2,1)} %input.1.refs_0_), channel_id=1, source_target_pairs={{0,3},{1,0},{2,1},{3,2},{4,7},{5,4},{6,5},{7,6},{8,11},{9,8},{10,9... | collective-permute-start | bytes 1572872 | tf_op jit(solution)/shard_map/ppermute | solution.py:751
  175.7 22.7 %collective-permute-start.9 = (bf16[128,2048]{1,0:T(8,128)(2,1)}, bf16[128,2048]{1,0:T(8,128)(2,1)S(1)}, u32[]{:S(2)}, u32[]{:S(2)}) collective-permute-start(bf16[128,2048]{1,0:T(8,128)(2,1)} %input.1.refs_0_), channel_id=1, source_target_pairs={{0,1},{1,2},{2,3},{3,0},{4,5},{5,6},{6,7},{7,4},{8,9},{9,10},{10,1... | collective-permute-start | bytes 1572872 | tf_op jit(solution)/shard_map/ppermute | solution.py:751
  196.7 17.2 %collective-permute-start.19 = (bf16[128,1408]{1,0:T(8,128)(2,1)}, bf16[128,1408]{1,0:T(8,128)(2,1)S(1)}, u32[]{:S(2)}, u32[]{:S(2)}) collective-permute-start(bf16[128,1408]{1,0:T(8,128)(2,1)} %slice.37), channel_id=1, source_target_pairs={{0,64},{64,0},{1,65},{65,1},{2,66},{66,2},{3,67},{67,3},{4,68},{68... | collective-permute-start | bytes 1081352 | tf_op jit(solution)/shard_map/ppermute | solution.py:751
  198.3 10.2 %copy-start.3 = (bf16[128,2048]{1,0:T(8,128)(2,1)}, bf16[128,2048]{1,0:T(8,128)(2,1)S(1)}, u32[]{:S(2)}) copy-start(bf16[128,2048]{1,0:T(8,128)(2,1)S(1)} %collective-permute-done.11.refs_3_) | copy-start | bytes 1572868
  198.3 10.2 %copy-start.4 = (bf16[128,2048]{1,0:T(8,128)(2,1)}, bf16[128,2048]{1,0:T(8,128)(2,1)S(1)}, u32[]{:S(2)}) copy-start(bf16[128,2048]{1,0:T(8,128)(2,1)S(1)} %collective-permute-done.10.refs_2_) | copy-start | bytes 1572868
  198.4 10.2 %copy-start.5 = (bf16[128,2048]{1,0:T(8,128)(2,1)}, bf16[128,2048]{1,0:T(8,128)(2,1)S(1)}, u32[]{:S(2)}) copy-start(bf16[128,2048]{1,0:T(8,128)(2,1)S(1)} %collective-permute-done.9.refs_1_) | copy-start | bytes 1572868
  198.4 19.7 %collective-permute-start.14 = (bf16[128,2048]{1,0:T(8,128)(2,1)S(1)}, bf16[128,2048]{1,0:T(8,128)(2,1)S(1)}, u32[]{:S(2)}, u32[]{:S(2)}) collective-permute-start(bf16[128,2048]{1,0:T(8,128)(2,1)S(1)} %collective-permute-done.11.refs_3_), channel_id=1, source_target_pairs={{0,1},{1,2},{2,3},{3,0},{4,5},{5,6},{6,7},{7,4},{8,9},{9,10},{10,1... | collective-permute-start | bytes 1572872 | tf_op jit(solution)/shard_map/ppermute | solution.py:751
  198.5 21.1 %collective-permute-start.13 = (bf16[128,2048]{1,0:T(8,128)(2,1)S(1)}, bf16[128,2048]{1,0:T(8,128)(2,1)S(1)}, u32[]{:S(2)}, u32[]{:S(2)}) collective-permute-start(bf16[128,2048]{1,0:T(8,128)(2,1)S(1)} %collective-permute-done.10.refs_2_), channel_id=1, source_target_pairs={{0,4},{4,0},{1,5},{5,1},{2,6},{6,2},{3,7},{7,3},{8,12},{12,8},{9,1... | collective-permute-start | bytes 1572872 | tf_op jit(solution)/shard_map/ppermute | solution.py:751
  199.1 20.4 %collective-permute-start.12 = (bf16[128,2048]{1,0:T(8,128)(2,1)S(1)}, bf16[128,2048]{1,0:T(8,128)(2,1)S(1)}, u32[]{:S(2)}, u32[]{:S(2)}) collective-permute-start(bf16[128,2048]{1,0:T(8,128)(2,1)S(1)} %collective-permute-done.10.refs_2_), channel_id=1, source_target_pairs={{0,3},{1,0},{2,1},{3,2},{4,7},{5,4},{6,5},{7,6},{8,11},{9,8},{10,9... | collective-permute-start | bytes 1572872 | tf_op jit(solution)/shard_map/ppermute | solution.py:751
  209.7 23.3 %collective-permute-start.18 = (bf16[128,1792]{1,0:T(8,128)(2,1)S(1)}, bf16[128,1792]{1,0:T(8,128)(2,1)S(1)}, u32[]{:S(2)}, u32[]{:S(2)}) collective-permute-start(bf16[128,1792]{1,0:T(8,128)(2,1)S(1)} %slice.36), channel_id=1, source_target_pairs={{0,64},{64,0},{1,65},{65,1},{2,66},{66,2},{3,67},{67,3},{4,68},{68... | collective-permute-start | bytes 1376264 | tf_op jit(solution)/shard_map/ppermute | solution.py:751
  213.9 0.7 copy-start.13
  217.4 15.6 %collective-permute-start.20 = (f32[2,128]{1,0:T(2,128)S(1)}, f32[2,128]{1,0:T(2,128)S(1)}, u32[]{:S(2)}, u32[]{:S(2)}) collective-permute-start(f32[2,128]{1,0:T(2,128)S(1)} %slice.38), channel_id=1, source_target_pairs={{0,4},{4,0},{1,5},{5,1},{2,6},{6,2},{3,7},{7,3},{8,12},{12,8},{9,1... | collective-permute-start | bytes 3080 | tf_op jit(solution)/shard_map/ppermute | solution.py:751
  218.1 23.4 %copy-start.26 = (f32[128]{0:T(128)}, f32[128]{0:T(128)S(1)}, u32[]{:S(2)}) copy-start(f32[128]{0:T(128)S(1)} %slice_bitcast_fusion.1) | copy-start | bytes 1540
  218.1 7.6 %copy-start.2 = (bf16[128,2048]{1,0:T(8,128)(2,1)}, bf16[128,2048]{1,0:T(8,128)(2,1)S(1)}, u32[]{:S(2)}) copy-start(bf16[128,2048]{1,0:T(8,128)(2,1)S(1)} %collective-permute-done.14.refs_6_) | copy-start | bytes 1572868
  219.5 6.2 %copy-start = (bf16[128,2048]{1,0:T(8,128)(2,1)}, bf16[128,2048]{1,0:T(8,128)(2,1)S(1)}, u32[]{:S(2)}) copy-start(bf16[128,2048]{1,0:T(8,128)(2,1)S(1)} %collective-permute-done.13.refs_5_) | copy-start | bytes 1572868
  219.5 6.2 %copy-start.1 = (bf16[128,2048]{1,0:T(8,128)(2,1)}, bf16[128,2048]{1,0:T(8,128)(2,1)S(1)}, u32[]{:S(2)}) copy-start(bf16[128,2048]{1,0:T(8,128)(2,1)S(1)} %collective-permute-done.12.refs_4_) | copy-start | bytes 1572868
  219.5 10.0 %collective-permute-start.17 = (bf16[32,2048]{1,0:T(8,128)(2,1)S(1)}, bf16[32,2048]{1,0:T(8,128)(2,1)S(1)}, u32[]{:S(2)}, u32[]{:S(2)}) collective-permute-start(bf16[32,2048]{1,0:T(8,128)(2,1)S(1)} %slice.35), channel_id=1, source_target_pairs={{0,1},{1,2},{2,3},{3,0},{4,5},{5,6},{6,7},{7,4},{8,9},{9,10},{10,1... | collective-permute-start | bytes 393224 | tf_op jit(solution)/shard_map/ppermute | solution.py:751
  219.7 9.9 %collective-permute-start.16 = (bf16[48,2048]{1,0:T(8,128)(2,1)S(1)}, bf16[48,2048]{1,0:T(8,128)(2,1)S(1)}, u32[]{:S(2)}, u32[]{:S(2)}) collective-permute-start(bf16[48,2048]{1,0:T(8,128)(2,1)S(1)} %slice.34), channel_id=1, source_target_pairs={{0,3},{1,0},{2,1},{3,2},{4,7},{5,4},{6,5},{7,6},{8,11},{9,8},{10,9... | collective-permute-start | bytes 589832 | tf_op jit(solution)/shard_map/ppermute | solution.py:751
  223.0 10.1 %collective-permute-start.15 = (bf16[48,2048]{1,0:T(8,128)(2,1)S(1)}, bf16[48,2048]{1,0:T(8,128)(2,1)S(1)}, u32[]{:S(2)}, u32[]{:S(2)}) collective-permute-start(bf16[48,2048]{1,0:T(8,128)(2,1)S(1)} %slice.33), channel_id=1, source_target_pairs={{0,4},{4,0},{1,5},{5,1},{2,6},{6,2},{3,7},{7,3},{8,12},{12,8},{9,1... | collective-permute-start | bytes 589832 | tf_op jit(solution)/shard_map/ppermute | solution.py:751
  229.6 9.5 %copy-start.18 = (bf16[32,2048]{1,0:T(8,128)(2,1)}, bf16[32,2048]{1,0:T(8,128)(2,1)S(1)}, u32[]{:S(2)}) copy-start(bf16[32,2048]{1,0:T(8,128)(2,1)S(1)} %collective-permute-done.17.refs_2_) | copy-start | bytes 393220
  229.6 9.4 %copy-start.16 = (bf16[48,2048]{1,0:T(8,128)(2,1)}, bf16[48,2048]{1,0:T(8,128)(2,1)S(1)}, u32[]{:S(2)}) copy-start(bf16[48,2048]{1,0:T(8,128)(2,1)S(1)} %collective-permute-done.16.refs_1_) | copy-start | bytes 589828
  233.0 6.0 %copy-start.17 = (bf16[48,2048]{1,0:T(8,128)(2,1)}, bf16[48,2048]{1,0:T(8,128)(2,1)S(1)}, u32[]{:S(2)}) copy-start(bf16[48,2048]{1,0:T(8,128)(2,1)S(1)} %collective-permute-done.15.refs_0_) | copy-start | bytes 589828
  233.0 3.9 %copy-start.12 = (bf16[128,1792]{1,0:T(8,128)(2,1)}, bf16[128,1792]{1,0:T(8,128)(2,1)S(1)}, u32[]{:S(2)}) copy-start(bf16[128,1792]{1,0:T(8,128)(2,1)S(1)} %collective-permute-done.18.far_ref) | copy-start | bytes 1376260
  233.7 7.3 %collective-permute-start.23 = (f32[2,128]{1,0:T(2,128)S(1)}, f32[2,128]{1,0:T(2,128)S(1)}, u32[]{:S(2)}, u32[]{:S(2)}) collective-permute-start(f32[2,128]{1,0:T(2,128)S(1)} %slice_add_fusion), channel_id=1, source_target_pairs={{0,2},{1,3},{2,0},{3,1},{4,6},{5,7},{6,4},{7,5},{8,10},{9,11},{10,... | collective-permute-start | bytes 3080 | tf_op jit(solution)/shard_map/ppermute | solution.py:751
  233.7 7.3 %collective-permute-start.22 = (f32[2,128]{1,0:T(2,128)S(1)}, f32[2,128]{1,0:T(2,128)S(1)}, u32[]{:S(2)}, u32[]{:S(2)}) collective-permute-start(f32[2,128]{1,0:T(2,128)S(1)} %slice_add_fusion), channel_id=1, source_target_pairs={{0,3},{1,0},{2,1},{3,2},{4,7},{5,4},{6,5},{7,6},{8,11},{9,8},{10,9... | collective-permute-start | bytes 3080 | tf_op jit(solution)/shard_map/ppermute | solution.py:751
  235.4 5.6 %collective-permute-start.21 = (f32[2,128]{1,0:T(2,128)S(1)}, f32[2,128]{1,0:T(2,128)S(1)}, u32[]{:S(2)}, u32[]{:S(2)}) collective-permute-start(f32[2,128]{1,0:T(2,128)S(1)} %slice_add_fusion), channel_id=1, source_target_pairs={{0,1},{1,2},{2,3},{3,0},{4,5},{5,6},{6,7},{7,4},{8,9},{9,10},{10,1... | collective-permute-start | bytes 3080 | tf_op jit(solution)/shard_map/ppermute | solution.py:751
Sparse Core Ops, SparseCore 0:
  53.7 141.1 all-reduce.1
Sparse Core Ops, SparseCore 1:
  94.3 56.4 reduce-scatter.2
  153.1 47.0 reduce-scatter.4
